TPU v7x, 256 devices: a whole 4x4x8 slice. The times are simulated.
256 devices in a mesh: pipe: 8 (over z), expert: 32 (over x, y, core).
Axes of the slice: x: 4, y: 4, z: 8, core: 2. Of those that a mesh axis runs over, the one named last changes fastest.
Arguments:
- up_prev: bfloat16 [8, 3072, 3584], P('pipe', 'expert'), may hold values from -60 to 60
- down_prev: bfloat16 [8, 3072, 3584], P('pipe', 'expert'), may hold values from -60 to 60
- enter_up: bfloat16 [3072, 3584], P('expert'), may hold values from -60 to 60
- enter_down: bfloat16 [3072, 3584], P('expert'), may hold values from -60 to 60
- norm_gain: float32 [8, 3584], P('pipe'), may hold values from 0.1 to 1.9
- router: bfloat16 [8, 3584, 8], P('pipe'), may hold values from -0.09375 to 0.09375
- w_gate: bfloat16 [8, 3584, 8192], P('pipe', None, 'expert'), may hold values from -0.09375 to 0.09375
- w_up: bfloat16 [8, 3584, 8192], P('pipe', None, 'expert'), may hold values from -0.09375 to 0.09375
- w_down: bfloat16 [8, 8192, 3584], P('pipe', 'expert'), may hold values from -0.1875 to 0.1875
- ids_up: int32 [8, 3072, 2], P('pipe', 'expert'), may hold values from 0 to 7, all different within a row; in each aligned block of 96 rows (0 to 95, 96 to 191, ..., all dimensions but the last counted through in order) at most 30 rows name the same one
- ids_down: int32 [8, 3072, 2], P('pipe', 'expert'), may hold values from 0 to 7, all different within a row; in each aligned block of 96 rows (0 to 95, 96 to 191, ..., all dimensions but the last counted through in order) at most 30 rows name the same one
Outputs:
- up_next: bfloat16 [8, 3072, 3584], P('pipe', 'expert')
- down_next: bfloat16 [8, 3072, 3584], P('pipe', 'expert')
Inputs may be any that keep to these rules, and one draw needn't show every extreme that they name: `ids_up`: within the 96 tokens of one index of expert (aligned blocks of rows), no expert is named by more than 30 tokens, a bound that some block reaches; a token names 2 different experts. `ids_down`: within the 96 tokens of one index of expert (aligned blocks of rows), no expert is named by more than 30 tokens, a bound that some block reaches; a token names 2 different experts.
All inputs are finite; a program needn't handle non-finite values.
Results may differ from a plain program's by a relative error of at most 0.008.
Values may be sent and summed in bfloat16 or wider, within the bound.
No kernel may reach another device: no remote copies, remote signals or barrier semaphores. Data moves between devices by JAX's collectives and lax.ppermute only.
A program may use at most 128 MiB of HBM per device.

v0:
```python
import jax
import jax.numpy as jnp
from jax import lax
from jax.sharding import PartitionSpec as P

EXPERTS = 8
CAP = 30


def from_behind(value, axis, by):
    devices = lax.axis_size(axis)
    pairs = [(i, i + by) for i in range(devices) if 0 <= i + by < devices]
    return lax.ppermute(value, axis, pairs)


def normalize(stream_in, gain):
    values = stream_in.astype(jnp.float32)
    square_mean = jnp.mean(values * values, axis=-1, keepdims=True)
    return (values * lax.rsqrt(square_mean + 1e-06) * gain).astype(jnp.bfloat16)


def gate_weights(normed, router_mat, routes):
    logits = jnp.dot(normed, router_mat, preferred_element_type=jnp.float32)
    choose = (routes[:, :, None] == jnp.arange(EXPERTS, dtype=jnp.int32)).astype(jnp.float32)
    chosen = jnp.sum(choose * logits[:, None, :], axis=-1)
    affinity = jax.nn.sigmoid(chosen)
    return 2.5 * affinity / jnp.sum(affinity, axis=-1, keepdims=True)


def slot_positions(routes):
    marks = (routes[:, :, None] == jnp.arange(EXPERTS, dtype=jnp.int32)).astype(jnp.int32)
    flat_marks = marks.reshape(-1, EXPERTS)
    before = jnp.cumsum(flat_marks, axis=0) - flat_marks
    slots = jnp.sum(before * flat_marks, axis=-1).reshape(routes.shape)
    return routes * CAP + slots


def prepare(stream_in, gain, router_mat, routes):
    normed = normalize(stream_in, gain)
    weights = gate_weights(normed, router_mat, routes)
    position = slot_positions(routes)
    slot_table = position[:, :, None] == jnp.arange(EXPERTS * CAP, dtype=jnp.int32)
    placing = jnp.sum(slot_table.astype(jnp.int32), axis=1).astype(jnp.bfloat16)
    combine = jnp.sum(slot_table.astype(jnp.float32) * weights[:, :, None], axis=1)
    outgoing = jnp.einsum("ts,td->sd", placing, normed, preferred_element_type=jnp.float32).astype(
        jnp.bfloat16
    )
    return (outgoing, combine)


def spread(outgoing, devices):
    slices = devices // EXPERTS
    width = outgoing.shape[-1]
    shaped = outgoing.reshape(EXPERTS, 1, CAP, width)
    return jnp.broadcast_to(shaped, (EXPERTS, slices, CAP, width)).reshape(devices, CAP, width)


def expert_ffn(rows_in, gate_mat, up_mat, down_mat):
    gate_val = jnp.dot(rows_in, gate_mat, preferred_element_type=jnp.float32)
    up_val = jnp.dot(rows_in, up_mat, preferred_element_type=jnp.float32)
    hidden = (jax.nn.silu(gate_val) * up_val).astype(jnp.bfloat16)
    return jnp.dot(hidden, down_mat, preferred_element_type=jnp.float32).astype(jnp.bfloat16)


def finish(stream_in, combine, returned, devices):
    width = returned.shape[-1]
    summed = (
        returned.reshape(EXPERTS, devices // EXPERTS, CAP, width).astype(jnp.float32).sum(axis=1)
    )
    mixture = jnp.dot(
        combine,
        summed.reshape(EXPERTS * CAP, width),
        precision=lax.Precision.HIGHEST,
        preferred_element_type=jnp.float32,
    )
    return (stream_in.astype(jnp.float32) + mixture).astype(jnp.bfloat16)


def body(
    up_prev,
    down_prev,
    enter_up,
    enter_down,
    norm_gain,
    router,
    w_gate,
    w_up,
    w_down,
    ids_up,
    ids_down,
):
    section_index = lax.axis_index("pipe")
    section_count = lax.axis_size("pipe")
    devices = lax.axis_size("expert")
    from_below = from_behind(up_prev[0], "pipe", 1)
    from_above = from_behind(down_prev[0], "pipe", -1)
    input_up = jnp.where(section_index == 0, enter_up, from_below)
    input_down = jnp.where(section_index == section_count - 1, enter_down, from_above)
    gate_mat = w_gate[0]
    up_mat = w_up[0]
    down_mat = w_down[0]
    out_up, combine_up = prepare(input_up, norm_gain[0], router[0], ids_up[0])
    out_down, combine_down = prepare(input_down, norm_gain[0], router[0], ids_down[0])

    def own_rows(received):
        result = expert_ffn(
            received.reshape(-1, received.shape[-1]), gate_mat, up_mat, down_mat
        ).reshape(received.shape)
        return lax.all_to_all(result, "expert", split_axis=0, concat_axis=0, tiled=True)

    def send_stream(sending):
        return own_rows(lax.all_to_all(sending, "expert", split_axis=0, concat_axis=0, tiled=True))

    back_up = send_stream(spread(out_up, devices))
    back_down = send_stream(spread(out_down, devices))
    up_next = finish(input_up, combine_up, back_up, devices)[None]
    down_next = finish(input_down, combine_down, back_down, devices)[None]
    return (up_next, down_next)


def solution(mesh):
    in_specs = (
        P("pipe", "expert", None),
        P("pipe", "expert", None),
        P("expert", None),
        P("expert", None),
        P("pipe", None),
        P("pipe", None, None),
        P("pipe", None, "expert"),
        P("pipe", None, "expert"),
        P("pipe", "expert", None),
        P("pipe", "expert", None),
        P("pipe", "expert", None),
    )
    out_specs = (P("pipe", "expert", None), P("pipe", "expert", None))
    return jax.shard_map(body, mesh=mesh, in_specs=in_specs, out_specs=out_specs, check_vma=False)
```

profile of v0, /device:TPU:108, one launch (start us, length us, event | category | flops | bytes accessed | tf_op | source)
XLA Modules:
  0.0 517.1 jit_solution(458019932826238847)
XLA Ops:
  0.6 2.1 collective-permute-start.1
  2.8 0.8 copy.29
  3.6 0.1 eq.119
  3.7 0.6 reduce-window.16
  4.3 0.2 slice_reduce_fusion
  4.7 0.1 reshape.167
  4.9 1.4 reduce.1
  6.4 15.1 %collective-permute-done.1 = bf16[96,3584]{1,0:T(8,128)(2,1)S(1)} collective-permute-done((bf16[96,3584]{1,0:T(8,128)(2,1)}, bf16[96,3584]{1,0:T(8,128)(2,1)S(1)}, u32[]{:S(2)}, u32[]{:S(2)}) %collective-permute-start.1) | collective-permute-done | bytes 688160 | tf_op jit(solution)/shard_map/ppermute | solution.py:13
  21.4 0.3 fusion.17
  21.9 0.8 copy-done.2
  22.7 0.7 convolution_convert_fusion.2
  23.4 1.5 broadcast_in_dim.15
  24.9 5.3 %broadcast_in_dim.16 = bf16[8,4,30,3584]{3,2,1,0:T(8,128)(2,1)} broadcast(bf16[8,30,3584]{2,1,0:T(8,128)(2,1)} %broadcast_in_dim.15), dimensions={0,2,3} | broadcast | bytes 8601600 | tf_op jit(solution)/shard_map/broadcast_in_dim | solution.py:55
  30.2 7.7 %all-to-all-start.2 = ((bf16[32,30,3584]{2,1,0:T(8,128)(2,1)}), bf16[32,30,3584]{2,1,0:T(8,128)(2,1)}, u32[]{:S(2)}, u32[]{:S(2)}) async-start(bf16[32,30,3584]{2,1,0:T(8,128)(2,1)} %bitcast.70), calls=%async_computation.2 | async-start | bytes 14680064 | tf_op jit(solution)/shard_map/all_to_all | solution.py:112
  37.9 3.6 collective-permute-start
  41.7 0.1 eq.105
  41.8 0.6 reduce-window.14
  42.4 0.2 slice_reduce_fusion.1
  42.8 0.1 reshape.160
  43.1 14.4 %collective-permute-done = bf16[96,3584]{1,0:T(8,128)(2,1)S(1)} collective-permute-done((bf16[96,3584]{1,0:T(8,128)(2,1)}, bf16[96,3584]{1,0:T(8,128)(2,1)S(1)}, u32[]{:S(2)}, u32[]{:S(2)}) %collective-permute-start) | collective-permute-done | bytes 688160 | tf_op jit(solution)/shard_map/ppermute | solution.py:13
  57.5 0.3 fusion.14
  57.9 0.8 copy-done.4
  58.7 1.4 convolution_convert_fusion.3
  60.1 1.5 broadcast_in_dim.12
  61.6 86.1 %all-to-all-done.2 = bf16[32,30,3584]{2,1,0:T(8,128)(2,1)} async-done(((bf16[32,30,3584]{2,1,0:T(8,128)(2,1)}), bf16[32,30,3584]{2,1,0:T(8,128)(2,1)}, u32[]{:S(2)}, u32[]{:S(2)}) %all-to-all-start.2) | async-done | bytes 6881312 | tf_op jit(solution)/shard_map/all_to_all | solution.py:112
  147.7 5.3 %broadcast_in_dim.13 = bf16[8,4,30,3584]{3,2,1,0:T(8,128)(2,1)} broadcast(bf16[8,30,3584]{2,1,0:T(8,128)(2,1)} %broadcast_in_dim.12), dimensions={0,2,3} | broadcast | bytes 8601600 | tf_op jit(solution)/shard_map/broadcast_in_dim | solution.py:55
  153.0 5.9 %all-to-all-start = ((bf16[32,30,3584]{2,1,0:T(8,128)(2,1)}), bf16[32,30,3584]{2,1,0:T(8,128)(2,1)}, u32[]{:S(2)}, u32[]{:S(2)}) async-start(bf16[32,30,3584]{2,1,0:T(8,128)(2,1)} %bitcast.71), calls=%async_computation | async-start | bytes 14680064 | tf_op jit(solution)/shard_map/all_to_all | solution.py:112
  158.9 8.9 %reshape.169 = bf16[960,3584]{1,0:T(8,128)(2,1)} reshape(bf16[32,30,3584]{2,1,0:T(8,128)(2,1)} %all-to-all-done.2) | data formatting | bytes 13762560 | tf_op jit(solution)/shard_map/reshape | solution.py:107
  167.8 5.4 %fusion.10 = f32[960,256]{1,0:T(8,128)S(1)} fusion(bf16[960,3584]{1,0:T(8,128)(2,1)} %reshape.169, bf16[1,3584,256]{2,1,0:T(8,128)(2,1)} %param.17), kind=kOutput, calls=%fused_computation.22 | convolution fusion | flops 1761607680 | bytes 9699328 | tf_op jit(solution)/shard_map/dot_general | solution.py:59
  173.2 13.4 %convolution_convert_fusion = bf16[960,3584]{1,0:T(8,128)(2,1)} fusion(bf16[1,256,3584]{2,1,0:T(8,128)(2,1)S(1)} %copy-done, bf16[960,3584]{1,0:T(8,128)(2,1)} %reshape.169, bf16[1,3584,256]{2,1,0:T(8,128)(2,1)} %param.18, f32[960,256]{1,0:T(8,128)S(1)} %fusion.10), kind=kOutput, calls=%fused_computation.2 | convolution fusion | flops 3528130560 | bytes 18415616 | tf_op jit(solution)/shard_map/dot_general | solution.py:62
  186.6 8.8 %reshape.170 = bf16[32,30,3584]{2,1,0:T(8,128)(2,1)} reshape(bf16[960,3584]{1,0:T(8,128)(2,1)} %convolution_convert_fusion) | data formatting | bytes 13762560 | tf_op jit(solution)/shard_map/reshape | solution.py:108
  195.4 73.1 %all-to-all-done = bf16[32,30,3584]{2,1,0:T(8,128)(2,1)} async-done(((bf16[32,30,3584]{2,1,0:T(8,128)(2,1)}), bf16[32,30,3584]{2,1,0:T(8,128)(2,1)}, u32[]{:S(2)}, u32[]{:S(2)}) %all-to-all-start) | async-done | bytes 6881312 | tf_op jit(solution)/shard_map/all_to_all | solution.py:112
  268.5 5.9 %all-to-all-start.3 = ((bf16[32,30,3584]{2,1,0:T(8,128)(2,1)}), bf16[32,30,3584]{2,1,0:T(8,128)(2,1)}, u32[]{:S(2)}, u32[]{:S(2)}) async-start(bf16[32,30,3584]{2,1,0:T(8,128)(2,1)} %reshape.170), calls=%async_computation.3 | async-start | bytes 14680064 | tf_op jit(solution)/shard_map/all_to_all | solution.py:109
  274.4 8.9 %reshape.162 = bf16[960,3584]{1,0:T(8,128)(2,1)} reshape(bf16[32,30,3584]{2,1,0:T(8,128)(2,1)} %all-to-all-done) | data formatting | bytes 13762560 | tf_op jit(solution)/shard_map/reshape | solution.py:107
  283.3 5.4 %fusion.12 = f32[960,256]{1,0:T(8,128)S(1)} fusion(bf16[960,3584]{1,0:T(8,128)(2,1)} %reshape.162, bf16[1,3584,256]{2,1,0:T(8,128)(2,1)} %param.17), kind=kOutput, calls=%fused_computation.24 | convolution fusion | flops 1761607680 | bytes 9699328 | tf_op jit(solution)/shard_map/dot_general | solution.py:59
  288.7 13.4 %convolution_convert_fusion.1 = bf16[960,3584]{1,0:T(8,128)(2,1)} fusion(bf16[1,256,3584]{2,1,0:T(8,128)(2,1)S(1)} %copy-done, bf16[960,3584]{1,0:T(8,128)(2,1)} %reshape.162, bf16[1,3584,256]{2,1,0:T(8,128)(2,1)} %param.18, f32[960,256]{1,0:T(8,128)S(1)} %fusion.12), kind=kOutput, calls=%fused_computation.3 | convolution fusion | flops 3528130560 | bytes 18415616 | tf_op jit(solution)/shard_map/dot_general | solution.py:62
  302.1 8.8 %reshape.163 = bf16[32,30,3584]{2,1,0:T(8,128)(2,1)} reshape(bf16[960,3584]{1,0:T(8,128)(2,1)} %convolution_convert_fusion.1) | data formatting | bytes 13762560 | tf_op jit(solution)/shard_map/reshape | solution.py:108
  311.0 72.9 %all-to-all-done.3 = bf16[32,30,3584]{2,1,0:T(8,128)(2,1)} async-done(((bf16[32,30,3584]{2,1,0:T(8,128)(2,1)}), bf16[32,30,3584]{2,1,0:T(8,128)(2,1)}, u32[]{:S(2)}, u32[]{:S(2)}) %all-to-all-start.3) | async-done | bytes 6881312 | tf_op jit(solution)/shard_map/all_to_all | solution.py:109
  383.9 5.9 %all-to-all-start.1 = ((bf16[32,30,3584]{2,1,0:T(8,128)(2,1)}), bf16[32,30,3584]{2,1,0:T(8,128)(2,1)}, u32[]{:S(2)}, u32[]{:S(2)}) async-start(bf16[32,30,3584]{2,1,0:T(8,128)(2,1)} %reshape.163), calls=%async_computation.1 | async-start | bytes 14680064 | tf_op jit(solution)/shard_map/all_to_all | solution.py:109
  390.0 0.4 fusion.52
  390.4 0.4 fusion.49
  391.2 6.5 %convert_reduce_fusion = f32[8,30,3584]{2,1,0:T(8,128)} fusion(bf16[32,30,3584]{2,1,0:T(8,128)(2,1)} %all-to-all-done.3), kind=kLoop, calls=%fused_computation | loop fusion | flops 6021120 | bytes 10321920 | tf_op jit(solution)/shard_map/reduce_sum | solution.py:68
  397.7 3.5 reshape.171
  401.2 98.3 %all-to-all-done.1 = bf16[32,30,3584]{2,1,0:T(8,128)(2,1)} async-done(((bf16[32,30,3584]{2,1,0:T(8,128)(2,1)}), bf16[32,30,3584]{2,1,0:T(8,128)(2,1)}, u32[]{:S(2)}, u32[]{:S(2)}) %all-to-all-start.1) | async-done | bytes 6881312 | tf_op jit(solution)/shard_map/all_to_all | solution.py:109
  499.5 6.4 %convert_reduce_fusion.1 = f32[8,30,3584]{2,1,0:T(8,128)} fusion(bf16[32,30,3584]{2,1,0:T(8,128)(2,1)} %all-to-all-done.1), kind=kLoop, calls=%fused_computation.1 | loop fusion | flops 6021120 | bytes 10321920 | tf_op jit(solution)/shard_map/reduce_sum | solution.py:68
  505.9 3.5 reshape.164
  509.4 4.9 fusion.2
  514.3 2.8 fusion.3
  (74 shorter events, 1.4 us)
Async XLA Ops:
  0.6 172.6 %copy-start = (bf16[1,256,3584]{2,1,0:T(8,128)(2,1)S(1)}, bf16[1,256,3584]{2,1,0:T(8,128)(2,1)}, u32[]{:S(2)}) copy-start(bf16[1,256,3584]{2,1,0:T(8,128)(2,1)} %param.19) | copy-start | bytes 5505028
  0.6 20.8 %collective-permute-start.1 = (bf16[96,3584]{1,0:T(8,128)(2,1)}, bf16[96,3584]{1,0:T(8,128)(2,1)S(1)}, u32[]{:S(2)}, u32[]{:S(2)}) collective-permute-start(bf16[96,3584]{1,0:T(8,128)(2,1)} %bitcast.74), channel_id=1, source_target_pairs={{32,0},{64,32},{96,64},{128,96},{160,128},{192,160},{224,192},{33,... | collective-permute-start | bytes 2064392 | tf_op jit(solution)/shard_map/ppermute | solution.py:13
  3.6 18.2 %copy-start.6 = (s32[1,96,2]{2,1,0:T(8,128)}, s32[1,96,2]{2,1,0:T(8,128)S(1)}, u32[]{:S(2)}) copy-start(s32[1,96,2]{2,1,0:T(8,128)S(1)} %copy.29) | copy-start | bytes 2308
  4.9 16.9 %copy-start.13 = (s32[96,2]{0,1:T(2,128)}, s32[96,2]{0,1:T(2,128)S(1)}, u32[]{:S(2)}) copy-start(s32[96,2]{0,1:T(2,128)S(1)} %copy.31) | copy-start | bytes 2308
  6.3 16.4 %copy-start.11 = (f32[3584]{0:T(1024)S(1)}, f32[3584]{0:T(1024)}, u32[]{:S(2)}) copy-start(f32[3584]{0:T(1024)} %reduce.1) | copy-start | bytes 43012
  21.8 0.9 copy-start.2
  21.8 0.8 copy-start.18
  30.2 11.3 %copy-start.17 = (s32[1,96,2]{1,2,0:T(2,128)S(1)}, s32[1,96,2]{1,2,0:T(2,128)}, u32[]{:S(2)}) copy-start(s32[1,96,2]{1,2,0:T(2,128)} %param.20) | copy-start | bytes 2308
  30.2 27.3 %copy-start.10 = (bf16[96,3584]{1,0:T(8,128)(2,1)S(1)}, bf16[96,3584]{1,0:T(8,128)(2,1)}, u32[]{:S(2)}) copy-start(bf16[96,3584]{1,0:T(8,128)(2,1)} %param.13) | copy-start | bytes 2064388
  30.2 117.5 %all-to-all-start.2 = ((bf16[32,30,3584]{2,1,0:T(8,128)(2,1)}), bf16[32,30,3584]{2,1,0:T(8,128)(2,1)}, u32[]{:S(2)}, u32[]{:S(2)}) async-start(bf16[32,30,3584]{2,1,0:T(8,128)(2,1)} %bitcast.70), calls=%async_computation.2 | async-start | bytes 14680064 | tf_op jit(solution)/shard_map/all_to_all | solution.py:112
  37.9 19.6 %collective-permute-start = (bf16[96,3584]{1,0:T(8,128)(2,1)}, bf16[96,3584]{1,0:T(8,128)(2,1)S(1)}, u32[]{:S(2)}, u32[]{:S(2)}) collective-permute-start(bf16[96,3584]{1,0:T(8,128)(2,1)} %bitcast.75), channel_id=1, source_target_pairs={{0,32},{32,64},{64,96},{96,128},{128,160},{160,192},{192,224},{1,3... | collective-permute-start | bytes 2064392 | tf_op jit(solution)/shard_map/ppermute | solution.py:13
  41.7 16.2 %copy-start.8 = (s32[1,96,2]{2,1,0:T(8,128)}, s32[1,96,2]{2,1,0:T(8,128)S(1)}, u32[]{:S(2)}) copy-start(s32[1,96,2]{2,1,0:T(8,128)S(1)} %copy.25) | copy-start | bytes 2308
  43.0 14.9 %copy-start.15 = (s32[96,2]{0,1:T(2,128)}, s32[96,2]{0,1:T(2,128)S(1)}, u32[]{:S(2)}) copy-start(s32[96,2]{0,1:T(2,128)S(1)} %copy.27) | copy-start | bytes 2308
  57.8 0.9 copy-start.4
  57.9 0.8 copy-start.20
  153.0 115.5 %all-to-all-start = ((bf16[32,30,3584]{2,1,0:T(8,128)(2,1)}), bf16[32,30,3584]{2,1,0:T(8,128)(2,1)}, u32[]{:S(2)}, u32[]{:S(2)}) async-start(bf16[32,30,3584]{2,1,0:T(8,128)(2,1)} %bitcast.71), calls=%async_computation | async-start | bytes 14680064 | tf_op jit(solution)/shard_map/all_to_all | solution.py:112
  268.5 115.4 %all-to-all-start.3 = ((bf16[32,30,3584]{2,1,0:T(8,128)(2,1)}), bf16[32,30,3584]{2,1,0:T(8,128)(2,1)}, u32[]{:S(2)}, u32[]{:S(2)}) async-start(bf16[32,30,3584]{2,1,0:T(8,128)(2,1)} %reshape.170), calls=%async_computation.3 | async-start | bytes 14680064 | tf_op jit(solution)/shard_map/all_to_all | solution.py:109
  310.9 78.9 %copy-start.9 = (s32[1,96,2]{2,1,0:T(8,128)S(1)}, s32[1,96,2]{2,1,0:T(8,128)}, u32[]{:S(2)}) copy-start(s32[1,96,2]{2,1,0:T(8,128)} %copy-done.8) | copy-start | bytes 2308
  310.9 79.0 %copy-start.7 = (s32[1,96,2]{2,1,0:T(8,128)S(1)}, s32[1,96,2]{2,1,0:T(8,128)}, u32[]{:S(2)}) copy-start(s32[1,96,2]{2,1,0:T(8,128)} %copy-done.6) | copy-start | bytes 2308
  310.9 79.1 %copy-start.5 = (bf16[96,3584]{1,0:T(8,128)(2,1)S(1)}, bf16[96,3584]{1,0:T(8,128)(2,1)}, u32[]{:S(2)}) copy-start(bf16[96,3584]{1,0:T(8,128)(2,1)} %copy-done.4) | copy-start | bytes 2064388
  310.9 79.1 %copy-start.12 = (f32[3584]{0:T(1024)S(1)}, f32[3584]{0:T(1024)}, u32[]{:S(2)}) copy-start(f32[3584]{0:T(1024)} %reduce.1) | copy-start | bytes 43012
  310.9 79.1 %copy-start.21 = (f32[96]{0:T(128)S(1)}, f32[96]{0:T(128)}, u32[]{:S(2)}) copy-start(f32[96]{0:T(128)} %copy-done.20) | copy-start | bytes 1156
  311.0 79.1 %copy-start.22 = (bf16[1,3584,8]{1,2,0:T(8,128)(2,1)S(1)}, bf16[1,3584,8]{1,2,0:T(8,128)(2,1)}, u32[]{:S(2)}) copy-start(bf16[1,3584,8]{1,2,0:T(8,128)(2,1)} %param.16) | copy-start | bytes 172036
  311.0 79.5 %copy-start.3 = (bf16[96,3584]{1,0:T(8,128)(2,1)S(1)}, bf16[96,3584]{1,0:T(8,128)(2,1)}, u32[]{:S(2)}) copy-start(bf16[96,3584]{1,0:T(8,128)(2,1)} %copy-done.2) | copy-start | bytes 2064388
  311.0 79.5 %copy-start.19 = (f32[96]{0:T(128)S(1)}, f32[96]{0:T(128)}, u32[]{:S(2)}) copy-start(f32[96]{0:T(128)} %copy-done.18) | copy-start | bytes 1156
  383.9 115.6 %all-to-all-start.1 = ((bf16[32,30,3584]{2,1,0:T(8,128)(2,1)}), bf16[32,30,3584]{2,1,0:T(8,128)(2,1)}, u32[]{:S(2)}, u32[]{:S(2)}) async-start(bf16[32,30,3584]{2,1,0:T(8,128)(2,1)} %reshape.163), calls=%async_computation.1 | async-start | bytes 14680064 | tf_op jit(solution)/shard_map/all_to_all | solution.py:109
  389.8 1.1 copy-start.14
  389.8 1.2 copy-start.16
  509.4 4.9 copy-start.1
where the time goes:
time: 519 us; the launch traced here: 517 us
  waiting for transfers between devices  360 us (69%)
  local copies, waits for them, and re-layouts  59.9 us (12%)
  matrix products  48 us (9%)
  starting transfers between devices  31.2 us (6%)
  other arithmetic  17 us (3%)
    all_to_all x2, waiting for transfers between devices, own_rows(): lax.all_to_all(result, 'expert', split_axis=0, concat_axis=0, tiled=True)  171 us
    all_to_all x2, waiting for transfers between devices, send_stream(): lax.all_to_all(sending, 'expert', split_axis=0, concat_axis=0, tiled=True)  159 us
    ppermute x2, waiting for transfers between devices, from_behind(): return lax.ppermute(value, axis, pairs)  29.4 us
    dot_general x2, matrix products, expert_ffn(): jnp.dot(hidden, down_mat, preferred_element_type=jnp.float32)  26.8 us
    reshape x2, local copies, waits for them, and re-layouts, own_rows(): received.reshape(-1, received.shape[-1])  17.8 us
    reshape x2, local copies, waits for them, and re-layouts, own_rows(): result = expert_ffn(received.reshape(-1, received.shape[-1]), gate_mat, u...  17.6 us
    broadcast_in_dim x4, local copies, waits for them, and re-layouts, spread(): jnp.broadcast_to(shaped, (EXPERTS, slices, CAP, width))  13.7 us
    all_to_all x2, starting transfers between devices, send_stream(): lax.all_to_all(sending, 'expert', split_axis=0, concat_axis=0, tiled=True)  13.6 us
  transfers between devices with their start and end apart: 6, of which 6 were waited for; matrix products, arithmetic and copies ran while one was open for 18% of the time, Pallas kernels for 0%

commit v1 on v0

v1 whole, which is shorter than its diff:
```python
import functools

import jax
import jax.numpy as jnp
from jax import lax
from jax.experimental import pallas as pl
from jax.experimental.pallas import tpu as pltpu
from jax.sharding import PartitionSpec as P

EXPERTS = 8
SLOTS = 32
SIDE = 4
GROUP = EXPERTS * SLOTS
CHUNK = 512
ROOM = 60 * 1024 * 1024
VMEM = pl.BlockSpec(memory_space=pltpu.VMEM)
ANY = pl.BlockSpec(memory_space=pl.ANY)


def place(x, y, core):
    return (x * SIDE + y) * 2 + core


def moved(value, xor_y, xor_core):
    pairs = [
        (place(x, y, c), place(x, y ^ xor_y, c ^ xor_core)) for x in range(SIDE) for y in range(SIDE) for c in range(2)
    ]
    return lax.ppermute(value, "expert", pairs)


ALL_CHIPS = [[place(x, y, c) for x in range(SIDE) for y in range(SIDE)] for c in range(2)]
HALF_CHIPS = [[place(x, y, c) for x in range(SIDE) for y in ys] for ys in ((0, 3), (1, 2)) for c in range(2)]


def all_to_all(value, groups):
    return lax.all_to_all(value, "expert", split_axis=0, concat_axis=0, tiled=True, axis_index_groups=groups)


def from_behind(value, axis, by):
    devices = lax.axis_size(axis)
    pairs = [(i, i + by) for i in range(devices) if 0 <= i + by < devices]
    return lax.ppermute(value, axis, pairs)


def mm(a, b, dims=((1,), (0,))):
    return lax.dot_general(a, b, (dims, ((), ())), preferred_element_type=jnp.float32)


def chunks_of(width):
    return [slice(at, min(at + CHUNK, width)) for at in range(0, width, CHUNK)]


def prepare_kernel(at_end, earlier, recv, enter, gain, router_t, ids, *rest):
    sent, stream, combine, normed = rest[earlier:]
    tokens, width = recv.shape
    edge = lax.axis_index("pipe") == (lax.axis_size("pipe") - 1 if at_end else 0)
    total = jnp.zeros((tokens, 1), jnp.float32)
    for cut in chunks_of(width):
        values = jnp.where(edge, enter[:, cut].astype(jnp.float32), recv[:, cut].astype(jnp.float32))
        stream[:, cut] = values.astype(jnp.bfloat16)
        total += jnp.sum(values * values, axis=-1, keepdims=True)
    scale = lax.rsqrt(total / width + 1e-06)
    logits = jnp.zeros((EXPERTS, tokens), jnp.float32)
    for cut in chunks_of(width):
        part = (stream[:, cut].astype(jnp.float32) * scale * gain[:, cut]).astype(jnp.bfloat16)
        normed[:, cut] = part
        logits += mm(router_t[:, cut], part, ((1,), (1,)))

    row = lax.broadcasted_iota(jnp.int32, (tokens, tokens), 0)
    col = lax.broadcasted_iota(jnp.int32, (tokens, tokens), 1)
    expert = lax.broadcasted_iota(jnp.int32, (EXPERTS, tokens), 0)
    picks = [ids[k : k + 1, :] == expert for k in range(2)]
    marks = jnp.where(picks[0] | picks[1], 1.0, 0.0).astype(jnp.bfloat16)
    at = (expert * SLOTS).astype(jnp.float32) + mm(marks, jnp.where(row < col, 1.0, 0.0).astype(jnp.bfloat16))
    affinity = [jax.nn.sigmoid(jnp.sum(jnp.where(pick, logits, 0.0), axis=0, keepdims=True)) for pick in picks]
    both = affinity[0] + affinity[1]
    slot = lax.broadcasted_iota(jnp.int32, (GROUP, tokens), 0)
    placing = jnp.zeros((GROUP, tokens), jnp.float32)
    weighted = jnp.zeros((GROUP, tokens), jnp.float32)
    for pick, share in zip(picks, affinity):
        where = jnp.sum(jnp.where(pick, at, 0.0), axis=0, keepdims=True).astype(jnp.int32)
        placing += jnp.where(slot == where, 1.0, 0.0)
        weighted += jnp.where(slot == where, 2.5 * share / both, 0.0)
    placing = placing.astype(jnp.bfloat16)
    for cut in chunks_of(width):
        rows = mm(placing, normed[:, cut]).astype(jnp.bfloat16)
        for i in range(EXPERTS):
            block = rows[i * SLOTS : (i + 1) * SLOTS]
            sent[2 * i, :, cut] = block
            sent[2 * i + 1, :, cut] = block
    padded = jnp.concatenate([weighted, jnp.zeros((GROUP, -tokens % 128), jnp.float32)], axis=1)
    combine[...] = padded.T[:tokens]


def prepare(at_end, recv, enter, gain, router_t, ids, earlier):
    tokens, width = recv.shape
    shape = jax.ShapeDtypeStruct
    return pl.pallas_call(
        functools.partial(prepare_kernel, at_end, len(earlier)),
        out_shape=[
            shape((2 * EXPERTS, SLOTS, width), jnp.bfloat16),
            shape((tokens, width), jnp.bfloat16),
            shape((tokens, GROUP), jnp.float32),
        ],
        in_specs=[VMEM] * 5 + [ANY] * len(earlier),
        out_specs=[VMEM] * 3,
        scratch_shapes=[pltpu.VMEM((tokens, width), jnp.bfloat16)],
        compiler_params=pltpu.CompilerParams(vmem_limit_bytes=ROOM),
        cost_estimate=pl.CostEstimate(flops=2 * GROUP * tokens * width, bytes_accessed=18 * tokens * width, transcendentals=0),
        name="prepare",
    )(recv, enter, gain, router_t, ids.T, *earlier)


def hidden_kernel(blocks, gate_a, gate_b, up_a, up_b, kept, sent, gate_sum, up_sum):
    step = pl.program_id(0)

    @pl.when(step == 0)
    def _():
        gate_sum[...] = jnp.zeros_like(gate_sum)
        up_sum[...] = jnp.zeros_like(up_sum)

    rows = jnp.concatenate([blocks[x * SIDE + y] for ys in ((0, 3), (1, 2)) for x in range(SIDE) for y in ys], axis=0)
    half = gate_a.shape[1]
    for total, mats in ((gate_sum, (gate_a, gate_b)), (up_sum, (up_a, up_b))):
        for i, mat in enumerate(mats):
            total[:, i * half : (i + 1) * half] += mm(rows, mat[...])

    @pl.when(step == pl.num_programs(0) - 1)
    def _():
        my_y = lax.rem(lax.div(lax.axis_index("expert"), 2), SIDE)
        outer = (my_y == 0) | (my_y == 3)
        first, second = (
            jax.nn.silu(gate_sum[at : at + GROUP]) * up_sum[at : at + GROUP] for at in (0, GROUP)
        )
        kept[...] = jnp.where(outer, first, second).astype(jnp.bfloat16)
        sent[...] = jnp.where(outer, second, first).astype(jnp.bfloat16)


def hidden(blocks, gate_a, gate_b, up_a, up_b):
    width, half = gate_a.shape
    deep = width // 2
    shape = jax.ShapeDtypeStruct((GROUP, 2 * half), jnp.bfloat16)
    return pl.pallas_call(
        hidden_kernel,
        grid=(width // deep,),
        out_shape=[shape, shape],
        in_specs=[pl.BlockSpec((*blocks.shape[:2], deep), lambda k: (0, 0, k))]
        + [pl.BlockSpec((deep, half), lambda k: (k, 0))] * 4,
        out_specs=[pl.BlockSpec((GROUP, 2 * half), lambda k: (0, 0))] * 2,
        scratch_shapes=[pltpu.VMEM((2 * GROUP, 2 * half), jnp.float32)] * 2,
        compiler_params=pltpu.CompilerParams(vmem_limit_bytes=ROOM),
        cost_estimate=pl.CostEstimate(flops=16 * GROUP * width * half, bytes_accessed=12 * width * half, transcendentals=0),
        name="hidden",
    )(blocks, gate_a, gate_b, up_a, up_b)


def down_kernel(own, other, *rest):
    mats, out = rest[:-1], rest[-1]
    units = jnp.concatenate([own[...], other[...]], axis=1)
    mat = jnp.concatenate([mat[...] for mat in mats], axis=0)
    rows = mm(units, mat).astype(jnp.bfloat16)
    for i in range(EXPERTS):
        out[i] = rows[i * SLOTS : (i + 1) * SLOTS]


def down(own, other, mats):
    half, width = mats[0].shape
    deep = CHUNK
    return pl.pallas_call(
        down_kernel,
        grid=(width // deep,),
        out_shape=jax.ShapeDtypeStruct((EXPERTS, SLOTS, width), jnp.bfloat16),
        in_specs=[pl.BlockSpec(own.shape, lambda k: (0, 0))] * 2 + [pl.BlockSpec((mat.shape[0], deep), lambda k: (0, k)) for mat in mats],
        out_specs=pl.BlockSpec((EXPERTS, SLOTS, deep), lambda k: (0, 0, k)),
        compiler_params=pltpu.CompilerParams(vmem_limit_bytes=ROOM),
        cost_estimate=pl.CostEstimate(flops=8 * GROUP * width * half, bytes_accessed=10 * width * half, transcendentals=0),
        name="down",
    )(own, other, *mats)


def finish_kernel(stream, combine, blocks, out):
    tokens = stream.shape[0]
    weights = combine[...]
    high = weights.astype(jnp.bfloat16)
    left = weights - high.astype(jnp.float32)
    middle = left.astype(jnp.bfloat16)
    low = (left - middle.astype(jnp.float32)).astype(jnp.bfloat16)
    terms = jnp.concatenate([high, middle, low], axis=0)
    rows = jnp.concatenate([blocks[i] for i in range(EXPERTS)], axis=0)
    sums = mm(terms, rows)
    mixture = sums[:tokens] + sums[tokens : 2 * tokens] + sums[2 * tokens :]
    out[...] = (stream[...].astype(jnp.float32) + mixture).astype(jnp.bfloat16)


def finish(stream, combine, blocks):
    tokens, width = stream.shape
    deep = 2 * CHUNK if width % (2 * CHUNK) == 0 else CHUNK
    return pl.pallas_call(
        finish_kernel,
        grid=(width // deep,),
        out_shape=jax.ShapeDtypeStruct((tokens, width), jnp.bfloat16),
        in_specs=[
            pl.BlockSpec((tokens, deep), lambda k: (0, k)),
            pl.BlockSpec((tokens, GROUP), lambda k: (0, 0)),
            pl.BlockSpec((EXPERTS, SLOTS, deep), lambda k: (0, 0, k)),
        ],
        out_specs=pl.BlockSpec((tokens, deep), lambda k: (0, k)),
        compiler_params=pltpu.CompilerParams(vmem_limit_bytes=ROOM),
        cost_estimate=pl.CostEstimate(flops=6 * GROUP * width * tokens, bytes_accessed=10 * tokens * width, transcendentals=0),
        name="finish",
    )(stream, combine, blocks)


def after(value, earlier):
    return pl.pallas_call(
        lambda value, earlier, out: None,
        out_shape=jax.ShapeDtypeStruct(value.shape, value.dtype),
        in_specs=[ANY, ANY],
        out_specs=ANY,
        input_output_aliases={0: 0},
        name="after",
    )(value, earlier)


def body(up_prev, down_prev, enter_up, enter_down, norm_gain, router, w_gate, w_up, w_down, ids_up, ids_down):
    from_below = from_behind(up_prev[0], "pipe", 1)
    from_above = from_behind(down_prev[0], "pipe", -1)
    gate_a, up_a, down_a = w_gate[0], w_up[0], w_down[0]
    gate_b, up_b = moved(gate_a, 0, 1), moved(up_a, 0, 1)
    router_t = router[0].T
    part = down_a.shape[0] // 2
    down_c, down_e = moved(down_a[:part], 1, 0), moved(down_a[part:], 1, 0)
    down_mats = (down_a, moved(down_a, 0, 1), down_c, down_e, moved(down_c, 0, 1), moved(down_e, 0, 1))
    first = prepare(False, from_below, enter_up, norm_gain, router_t, ids_up[0], (gate_b, up_b, down_c))
    second = prepare(True, from_above, enter_down, norm_gain, router_t, ids_down[0], (first[0],))
    rows_first = all_to_all(first[0], ALL_CHIPS)
    rows_second = all_to_all(after(second[0], rows_first), ALL_CHIPS)
    outs = []
    for rows, (_, stream, combine) in ((rows_first, first), (rows_second, second)):
        kept, given = hidden(rows, gate_a, gate_b, up_a, up_b)
        results = down(kept, moved(given, 1, 0), down_mats)
        outs.append(finish(stream, combine, all_to_all(results, HALF_CHIPS))[None])
    return tuple(outs)


def solution(mesh):
    in_specs = (
        P("pipe", "expert", None),
        P("pipe", "expert", None),
        P("expert", None),
        P("expert", None),
        P("pipe", None),
        P("pipe", None, None),
        P("pipe", None, "expert"),
        P("pipe", None, "expert"),
        P("pipe", "expert", None),
        P("pipe", "expert", None),
        P("pipe", "expert", None),
    )
    out_specs = (P("pipe", "expert", None), P("pipe", "expert", None))
    return jax.shard_map(body, mesh=mesh, in_specs=in_specs, out_specs=out_specs, check_vma=False)
```

time: 519 us -> 253 us (0.49)
  the two profiles are of different devices: /device:TPU:108 before, /device:TPU:96 now
where the time goes in v1:
time: 253 us; the launch traced here: 252 us
  waiting for transfers between devices  155 us (61%)
  Pallas kernels  52.4 us (21%)
  starting transfers between devices  35.6 us (14%)
  local copies, waits for them, and re-layouts  7.58 us (3%)
    ppermute x9, waiting for transfers between devices, moved(): return lax.ppermute(value, 'expert', pairs)  76.2 us
    all_to_all x4, waiting for transfers between devices, all_to_all(): lax.all_to_all(value, 'expert', split_axis=0, concat_axis=0, tiled=True,...  46.7 us
    ppermute x2, waiting for transfers between devices, from_behind(): return lax.ppermute(value, axis, pairs)  32.4 us
    all_to_all x4, starting transfers between devices, all_to_all(): lax.all_to_all(value, 'expert', split_axis=0, concat_axis=0, tiled=True,...  23.2 us
    pallas_call x2, Pallas kernels, down(): pl.pallas_call(down_kernel, grid=(width // deep,), out_shape=jax.ShapeDty...  16.2 us
    pallas_call x2, Pallas kernels, hidden(): pl.pallas_call(hidden_kernel, grid=(width // deep,), out_shape=[shape, sh...  15.8 us
    pallas_call x2, Pallas kernels, finish(): pl.pallas_call(finish_kernel, grid=(width // deep,), out_shape=jax.ShapeD...  11.8 us
    pallas_call x2, Pallas kernels, prepare(): pl.pallas_call(functools.partial(prepare_kernel, at_end, len(earlier)), o...  8.64 us
  transfers between devices with their start and end apart: 15, of which 9 were waited for; matrix products, arithmetic and copies ran while one was open for 1% of the time, Pallas kernels for 17%

profile of v1, /device:TPU:96, one launch (start us, length us, event | category | flops | bytes accessed | tf_op | source)
XLA Modules:
  0.0 251.6 jit_solution(14090151447264080869)
XLA Ops:
  0.6 0.1 collective-permute-start.1
  0.7 0.0 copy-start.9
  0.7 0.5 collective-permute-start.2
  1.2 2.6 %slice_bitcast_fusion = (bf16[128,3584]{1,0:T(8,128)(2,1)}, bf16[128,3584]{1,0:T(8,128)(2,1)S(1)}) fusion(bf16[1,256,3584]{2,1,0:T(8,128)(2,1)} %param.19), kind=kLoop, calls=%fused_computation | loop fusion | bytes 3670016 | tf_op jit(solution)/shard_map/slice | solution.py:232
  3.8 1.6 collective-permute-start.3
  5.4 0.0 copy-done.9
  5.4 5.0 %collective-permute-start = (bf16[96,3584]{1,0:T(8,128)(2,1)S(1)}, bf16[96,3584]{1,0:T(8,128)(2,1)S(1)}, u32[]{:S(2)}, u32[]{:S(2)}) collective-permute-start(bf16[96,3584]{1,0:T(8,128)(2,1)S(1)} %bitcast.35), channel_id=1, source_target_pairs={{0,32},{32,64},{64,96},{96,128},{128,160},{160,192},{192,224},{1,3... | collective-permute-start | bytes 2064392 | tf_op jit(solution)/shard_map/ppermute | solution.py:42
  10.4 14.7 %collective-permute-done.recv = bf16[96,3584]{1,0:T(8,128)(2,1)S(1)} collective-permute-done((bf16[96,3584]{1,0:T(8,128)(2,1)S(1)}, bf16[96,3584]{1,0:T(8,128)(2,1)S(1)}, u32[]{:S(2)}, u32[]{:S(2)}) %collective-permute-start) | collective-permute-done | bytes 688160 | tf_op jit(solution)/shard_map/ppermute | solution.py:42
  25.1 1.1 collective-permute-done.3.rest_2_
  26.2 0.0 collective-permute-done.1.rest_0_.gate_b
  26.2 0.0 collective-permute-done.2.rest_1_.up_b
  26.2 0.9 copy-done.1
  27.1 0.6 copy-done.4
  27.7 4.3 %prepare.2 = (bf16[16,32,3584]{2,1,0:T(8,128)(2,1)}, bf16[96,3584]{1,0:T(8,128)(2,1)}, f32[96,256]{1,0:T(8,128)}) custom-call(bf16[96,3584]{1,0:T(8,128)(2,1)} %copy-done.6, bf16[96,3584]{1,0:T(8,128)(2,1)} %enter.2, f32[1,3584]{1,0:T(1,128)} %gain.3, bf16[8,3584]{1,0:T(8,128)(2,1)} %bitcast.25, s32[2,96]{1,0:T(2,128)} %bitcast.28, ...), custom_call_target="tpu_custom_call" | custom-call | flops 176160768 | bytes 6193152 | tf_op jit(solution)/shard_map/prepare/pallas_call | solution.py:98
  32.0 7.2 %all-to-all-start = ((bf16[16,32,3584]{2,1,0:T(8,128)(2,1)}), bf16[16,32,3584]{2,1,0:T(8,128)(2,1)}, u32[]{:S(2)}, u32[]{:S(2)}) async-start(bf16[16,32,3584]{2,1,0:T(8,128)(2,1)} %get-tuple-element.14.rest_0_), calls=%async_computation | async-start | bytes 7340032 | tf_op jit(solution)/shard_map/all_to_all | solution.py:36
  39.2 2.0 collective-permute-start.9
  41.2 17.7 %collective-permute-done.9.recv = bf16[96,3584]{1,0:T(8,128)(2,1)S(1)} collective-permute-done((bf16[96,3584]{1,0:T(8,128)(2,1)S(1)}, bf16[96,3584]{1,0:T(8,128)(2,1)S(1)}, u32[]{:S(2)}, u32[]{:S(2)}) %collective-permute-start.9) | collective-permute-done | bytes 688160 | tf_op jit(solution)/shard_map/ppermute | solution.py:42
  58.9 0.8 copy-done.5
  59.7 4.4 %prepare.3 = (bf16[16,32,3584]{2,1,0:T(8,128)(2,1)}, bf16[96,3584]{1,0:T(8,128)(2,1)}, f32[96,256]{1,0:T(8,128)}) custom-call(bf16[96,3584]{1,0:T(8,128)(2,1)} %copy-done.5, bf16[96,3584]{1,0:T(8,128)(2,1)} %enter.3, f32[1,3584]{1,0:T(1,128)} %gain.3, bf16[8,3584]{1,0:T(8,128)(2,1)} %bitcast.26, s32[2,96]{1,0:T(2,128)} %bitcast.27, ...), custom_call_target="tpu_custom_call" | custom-call | flops 176160768 | bytes 6193152 | tf_op jit(solution)/shard_map/prepare/pallas_call | solution.py:98
  64.1 23.7 %all-to-all-done.blocks.earlier = bf16[16,32,3584]{2,1,0:T(8,128)(2,1)} async-done(((bf16[16,32,3584]{2,1,0:T(8,128)(2,1)}), bf16[16,32,3584]{2,1,0:T(8,128)(2,1)}, u32[]{:S(2)}, u32[]{:S(2)}) %all-to-all-start) | async-done | bytes 3670048 | tf_op jit(solution)/shard_map/all_to_all | solution.py:36
  87.8 7.0 %all-to-all-start.2 = ((bf16[16,32,3584]{2,1,0:T(8,128)(2,1)}), bf16[16,32,3584]{2,1,0:T(8,128)(2,1)}, u32[]{:S(2)}, u32[]{:S(2)}) async-start(bf16[16,32,3584]{2,1,0:T(8,128)(2,1)} %after.1), calls=%async_computation.2 | async-start | bytes 7340032 | tf_op jit(solution)/shard_map/all_to_all | solution.py:36
  94.8 1.9 collective-permute-start.6
  96.7 0.0 collective-permute-start.5
  96.7 0.0 copy-done.2
  96.7 0.5 collective-permute-start.7
  97.2 59.2 %collective-permute-done.6.rest_3_ = bf16[128,3584]{1,0:T(8,128)(2,1)} collective-permute-done((bf16[128,3584]{1,0:T(8,128)(2,1)}, bf16[128,3584]{1,0:T(8,128)(2,1)}, u32[]{:S(2)}, u32[]{:S(2)}) %collective-permute-start.6) | collective-permute-done | bytes 917536 | tf_op jit(solution)/shard_map/ppermute | solution.py:28
  156.5 0.0 collective-permute-start.8
  156.5 7.9 %hidden.2 = (bf16[256,512]{1,0:T(8,128)(2,1)}, bf16[256,512]{1,0:T(8,128)(2,1)}) custom-call(bf16[16,32,3584]{2,1,0:T(8,128)(2,1)} %all-to-all-done.blocks.earlier, bf16[3584,256]{1,0:T(8,128)(2,1)} %bitcast.30, bf16[3584,256]{1,0:T(8,128)(2,1)} %copy-done.4, bf16[3584,256]{1,0:T(8,128)(2,1)} %bitcast.33, bf16[3584,256]{1,0:T(8,128)(2,1)} %collective-permute-done.2.rest_1_.up_b), custom_call_target="tpu_custom_call" | custom-call | flops 3758096384 | bytes 11010048 | tf_op jit(solution)/shard_map/hidden/pallas_call | solution.py:143
  164.4 0.2 collective-permute-start.4
  164.5 0.0 collective-permute-done.7.rest_4_
  164.5 0.0 collective-permute-done.8.rest_5_
  164.5 0.0 collective-permute-done.5.rest_1_
  164.5 8.8 %collective-permute-done.4.other = bf16[256,512]{1,0:T(8,128)(2,1)S(1)} collective-permute-done((bf16[256,512]{1,0:T(8,128)(2,1)}, bf16[256,512]{1,0:T(8,128)(2,1)S(1)}, u32[]{:S(2)}, u32[]{:S(2)}) %collective-permute-start.4) | collective-permute-done | bytes 262176 | tf_op jit(solution)/shard_map/ppermute | solution.py:28
  173.3 0.7 copy-done.7
  174.0 8.1 %down.2 = bf16[8,32,3584]{2,1,0:T(8,128)(2,1)} custom-call(bf16[256,512]{1,0:T(8,128)(2,1)} %get-tuple-element.15.own, bf16[256,512]{1,0:T(8,128)(2,1)} %copy-done.7, bf16[256,3584]{1,0:T(8,128)(2,1)} %bitcast.20, bf16[256,3584]{1,0:T(8,128)(2,1)} %collective-permute-done.5.rest_1_, bf16[128,3584]{1,0:T(8,128)(2,1)} %copy-done.1, ...), custom_call_target="tpu_custom_call" | custom-call | flops 1879048192 | bytes 9175040 | tf_op jit(solution)/shard_map/down/pallas_call | solution.py:169
  182.1 0.0 all-to-all-done.2.blocks
  182.1 4.6 %all-to-all-start.1 = ((bf16[8,32,3584]{2,1,0:T(8,128)(2,1)}), bf16[8,32,3584]{2,1,0:T(8,128)(2,1)S(1)}, u32[]{:S(2)}, u32[]{:S(2)}) async-start(bf16[8,32,3584]{2,1,0:T(8,128)(2,1)} %down.2), calls=%async_computation.1 | async-start | bytes 3670016 | tf_op jit(solution)/shard_map/all_to_all | solution.py:36
  186.7 7.9 %hidden.3 = (bf16[256,512]{1,0:T(8,128)(2,1)}, bf16[256,512]{1,0:T(8,128)(2,1)}) custom-call(bf16[16,32,3584]{2,1,0:T(8,128)(2,1)} %all-to-all-done.2.blocks, bf16[3584,256]{1,0:T(8,128)(2,1)} %bitcast.31, bf16[3584,256]{1,0:T(8,128)(2,1)} %copy-done.4, bf16[3584,256]{1,0:T(8,128)(2,1)} %bitcast.34, bf16[3584,256]{1,0:T(8,128)(2,1)} %collective-permute-done.2.rest_1_.up_b), custom_call_target="tpu_custom_call" | custom-call | flops 3758096384 | bytes 11010048 | tf_op jit(solution)/shard_map/hidden/pallas_call | solution.py:143
  194.6 0.7 collective-permute-start.10
  195.3 7.1 %collective-permute-done.10.other = bf16[256,512]{1,0:T(8,128)(2,1)S(1)} collective-permute-done((bf16[256,512]{1,0:T(8,128)(2,1)}, bf16[256,512]{1,0:T(8,128)(2,1)S(1)}, u32[]{:S(2)}, u32[]{:S(2)}) %collective-permute-start.10) | collective-permute-done | bytes 262176 | tf_op jit(solution)/shard_map/ppermute | solution.py:28
  202.5 0.7 copy-done.8
  203.2 8.1 %down.3 = bf16[8,32,3584]{2,1,0:T(8,128)(2,1)} custom-call(bf16[256,512]{1,0:T(8,128)(2,1)} %get-tuple-element.20.own, bf16[256,512]{1,0:T(8,128)(2,1)} %copy-done.8, bf16[256,3584]{1,0:T(8,128)(2,1)} %bitcast.21, bf16[256,3584]{1,0:T(8,128)(2,1)} %collective-permute-done.5.rest_1_, bf16[128,3584]{1,0:T(8,128)(2,1)} %copy-done.1, ...), custom_call_target="tpu_custom_call" | custom-call | flops 1879048192 | bytes 9175040 | tf_op jit(solution)/shard_map/down/pallas_call | solution.py:169
  211.3 2.6 %all-to-all-done.1.blocks = bf16[8,32,3584]{2,1,0:T(8,128)(2,1)S(1)} async-done(((bf16[8,32,3584]{2,1,0:T(8,128)(2,1)}), bf16[8,32,3584]{2,1,0:T(8,128)(2,1)S(1)}, u32[]{:S(2)}, u32[]{:S(2)}) %all-to-all-start.1) | async-done | bytes 1835040 | tf_op jit(solution)/shard_map/all_to_all | solution.py:36
  213.9 1.3 copy-done.3
  215.2 4.3 %all-to-all-start.3 = ((bf16[8,32,3584]{2,1,0:T(8,128)(2,1)}), bf16[8,32,3584]{2,1,0:T(8,128)(2,1)}, u32[]{:S(2)}, u32[]{:S(2)}) async-start(bf16[8,32,3584]{2,1,0:T(8,128)(2,1)} %down.3), calls=%async_computation.3 | async-start | bytes 3670016 | tf_op jit(solution)/shard_map/all_to_all | solution.py:36
  219.5 5.9 %finish.2 = bf16[96,3584]{1,0:T(8,128)(2,1)} custom-call(bf16[96,3584]{1,0:T(8,128)(2,1)} %get-tuple-element.12.stream, f32[96,256]{1,0:T(8,128)} %get-tuple-element.13.combine, bf16[8,32,3584]{2,1,0:T(8,128)(2,1)} %copy-done.3), custom_call_target="tpu_custom_call" | custom-call | flops 528482304 | bytes 3440640 | tf_op jit(solution)/shard_map/finish/pallas_call | solution.py:198
  225.4 20.3 %all-to-all-done.3.blocks = bf16[8,32,3584]{2,1,0:T(8,128)(2,1)} async-done(((bf16[8,32,3584]{2,1,0:T(8,128)(2,1)}), bf16[8,32,3584]{2,1,0:T(8,128)(2,1)}, u32[]{:S(2)}, u32[]{:S(2)}) %all-to-all-start.3) | async-done | bytes 1835040 | tf_op jit(solution)/shard_map/all_to_all | solution.py:36
  245.7 5.9 %finish.3 = bf16[96,3584]{1,0:T(8,128)(2,1)} custom-call(bf16[96,3584]{1,0:T(8,128)(2,1)} %get-tuple-element.17.stream, f32[96,256]{1,0:T(8,128)} %get-tuple-element.18.combine, bf16[8,32,3584]{2,1,0:T(8,128)(2,1)} %all-to-all-done.3.blocks), custom_call_target="tpu_custom_call" | custom-call | flops 528482304 | bytes 3440640 | tf_op jit(solution)/shard_map/finish/pallas_call | solution.py:198
  (14 shorter events, 0.0 us)
Async XLA Ops:
  0.6 25.6 %collective-permute-start.1 = (bf16[3584,256]{1,0:T(8,128)(2,1)}, bf16[3584,256]{1,0:T(8,128)(2,1)S(1)}, u32[]{:S(2)}, u32[]{:S(2)}) collective-permute-start(bf16[3584,256]{1,0:T(8,128)(2,1)} %bitcast.29), channel_id=1, source_target_pairs={{0,1},{1,0},{2,3},{3,2},{4,5},{5,4},{6,7},{7,6},{8,9},{9,8},{10,11... | collective-permute-start | bytes 5505032 | tf_op jit(solution)/shard_map/ppermute | solution.py:28
  0.7 4.6 %copy-start.9 = (bf16[1,96,3584]{2,1,0:T(8,128)(2,1)S(1)}, bf16[1,96,3584]{2,1,0:T(8,128)(2,1)}, u32[]{:S(2)}) copy-start(bf16[1,96,3584]{2,1,0:T(8,128)(2,1)} %param.11) | copy-start | bytes 2064388
  0.7 25.5 %collective-permute-start.2 = (bf16[3584,256]{1,0:T(8,128)(2,1)}, bf16[3584,256]{1,0:T(8,128)(2,1)}, u32[]{:S(2)}, u32[]{:S(2)}) collective-permute-start(bf16[3584,256]{1,0:T(8,128)(2,1)} %bitcast.32), channel_id=1, source_target_pairs={{0,1},{1,0},{2,3},{3,2},{4,5},{5,4},{6,7},{7,6},{8,9},{9,8},{10,11... | collective-permute-start | bytes 5505032 | tf_op jit(solution)/shard_map/ppermute | solution.py:28
  3.8 22.4 %collective-permute-start.3 = (bf16[128,3584]{1,0:T(8,128)(2,1)S(1)}, bf16[128,3584]{1,0:T(8,128)(2,1)S(1)}, u32[]{:S(2)}, u32[]{:S(2)}) collective-permute-start(bf16[128,3584]{1,0:T(8,128)(2,1)S(1)} %get-tuple-element.23), channel_id=1, source_target_pairs={{0,2},{1,3},{2,0},{3,1},{4,6},{5,7},{6,4},{7,5},{8,10},{9,11},{10,... | collective-permute-start | bytes 2752520 | tf_op jit(solution)/shard_map/ppermute | solution.py:28
  5.4 19.8 %collective-permute-start = (bf16[96,3584]{1,0:T(8,128)(2,1)S(1)}, bf16[96,3584]{1,0:T(8,128)(2,1)S(1)}, u32[]{:S(2)}, u32[]{:S(2)}) collective-permute-start(bf16[96,3584]{1,0:T(8,128)(2,1)S(1)} %bitcast.35), channel_id=1, source_target_pairs={{0,32},{32,64},{64,96},{96,128},{128,160},{160,192},{192,224},{1,3... | collective-permute-start | bytes 2064392 | tf_op jit(solution)/shard_map/ppermute | solution.py:42
  25.1 1.1 copy-start.6
  26.2 0.9 copy-start.1
  26.2 1.5 copy-start.4
  32.0 7.2 %copy-start.10 = (bf16[1,96,3584]{2,1,0:T(8,128)(2,1)S(1)}, bf16[1,96,3584]{2,1,0:T(8,128)(2,1)}, u32[]{:S(2)}) copy-start(bf16[1,96,3584]{2,1,0:T(8,128)(2,1)} %param.12) | copy-start | bytes 2064388
  32.0 55.9 %all-to-all-start = ((bf16[16,32,3584]{2,1,0:T(8,128)(2,1)}), bf16[16,32,3584]{2,1,0:T(8,128)(2,1)}, u32[]{:S(2)}, u32[]{:S(2)}) async-start(bf16[16,32,3584]{2,1,0:T(8,128)(2,1)} %get-tuple-element.14.rest_0_), calls=%async_computation | async-start | bytes 7340032 | tf_op jit(solution)/shard_map/all_to_all | solution.py:36
  39.2 19.7 %collective-permute-start.9 = (bf16[96,3584]{1,0:T(8,128)(2,1)S(1)}, bf16[96,3584]{1,0:T(8,128)(2,1)S(1)}, u32[]{:S(2)}, u32[]{:S(2)}) collective-permute-start(bf16[96,3584]{1,0:T(8,128)(2,1)S(1)} %bitcast.36), channel_id=1, source_target_pairs={{32,0},{64,32},{96,64},{128,96},{160,128},{192,160},{224,192},{33,... | collective-permute-start | bytes 2064392 | tf_op jit(solution)/shard_map/ppermute | solution.py:42
  58.9 0.8 copy-start.5
  87.8 8.9 %copy-start = (bf16[1,256,3584]{2,1,0:T(8,128)(2,1)S(1)}, bf16[1,256,3584]{2,1,0:T(8,128)(2,1)}, u32[]{:S(2)}) copy-start(bf16[1,256,3584]{2,1,0:T(8,128)(2,1)} %param.19) | copy-start | bytes 5505028
  87.8 8.9 %copy-start.2 = (bf16[128,3584]{1,0:T(8,128)(2,1)S(1)}, bf16[128,3584]{1,0:T(8,128)(2,1)}, u32[]{:S(2)}) copy-start(bf16[128,3584]{1,0:T(8,128)(2,1)} %copy-done.1) | copy-start | bytes 2752516
  87.8 94.3 %all-to-all-start.2 = ((bf16[16,32,3584]{2,1,0:T(8,128)(2,1)}), bf16[16,32,3584]{2,1,0:T(8,128)(2,1)}, u32[]{:S(2)}, u32[]{:S(2)}) async-start(bf16[16,32,3584]{2,1,0:T(8,128)(2,1)} %after.1), calls=%async_computation.2 | async-start | bytes 7340032 | tf_op jit(solution)/shard_map/all_to_all | solution.py:36
  94.8 61.6 %collective-permute-start.6 = (bf16[128,3584]{1,0:T(8,128)(2,1)}, bf16[128,3584]{1,0:T(8,128)(2,1)}, u32[]{:S(2)}, u32[]{:S(2)}) collective-permute-start(bf16[128,3584]{1,0:T(8,128)(2,1)} %get-tuple-element.22), channel_id=1, source_target_pairs={{0,2},{1,3},{2,0},{3,1},{4,6},{5,7},{6,4},{7,5},{8,10},{9,11},{10,... | collective-permute-start | bytes 2752520 | tf_op jit(solution)/shard_map/ppermute | solution.py:28
  96.7 67.8 %collective-permute-start.5 = (bf16[256,3584]{1,0:T(8,128)(2,1)S(1)}, bf16[256,3584]{1,0:T(8,128)(2,1)}, u32[]{:S(2)}, u32[]{:S(2)}) collective-permute-start(bf16[256,3584]{1,0:T(8,128)(2,1)S(1)} %bitcast.22), channel_id=1, source_target_pairs={{0,1},{1,0},{2,3},{3,2},{4,5},{5,4},{6,7},{7,6},{8,9},{9,8},{10,11... | collective-permute-start | bytes 5505032 | tf_op jit(solution)/shard_map/ppermute | solution.py:28
  96.7 67.8 %collective-permute-start.7 = (bf16[128,3584]{1,0:T(8,128)(2,1)S(1)}, bf16[128,3584]{1,0:T(8,128)(2,1)}, u32[]{:S(2)}, u32[]{:S(2)}) collective-permute-start(bf16[128,3584]{1,0:T(8,128)(2,1)S(1)} %copy-done.2), channel_id=1, source_target_pairs={{0,1},{1,0},{2,3},{3,2},{4,5},{5,4},{6,7},{7,6},{8,9},{9,8},{10,11... | collective-permute-start | bytes 2752520 | tf_op jit(solution)/shard_map/ppermute | solution.py:28
  156.5 8.0 %collective-permute-start.8 = (bf16[128,3584]{1,0:T(8,128)(2,1)}, bf16[128,3584]{1,0:T(8,128)(2,1)}, u32[]{:S(2)}, u32[]{:S(2)}) collective-permute-start(bf16[128,3584]{1,0:T(8,128)(2,1)} %collective-permute-done.6.rest_3_), channel_id=1, source_target_pairs={{0,1},{1,0},{2,3},{3,2},{4,5},{5,4},{6,7},{7,6},{8,9},{9,8},{10,11... | collective-permute-start | bytes 2752520 | tf_op jit(solution)/shard_map/ppermute | solution.py:28
  164.4 8.9 %collective-permute-start.4 = (bf16[256,512]{1,0:T(8,128)(2,1)}, bf16[256,512]{1,0:T(8,128)(2,1)S(1)}, u32[]{:S(2)}, u32[]{:S(2)}) collective-permute-start(bf16[256,512]{1,0:T(8,128)(2,1)} %get-tuple-element.16), channel_id=1, source_target_pairs={{0,2},{1,3},{2,0},{3,1},{4,6},{5,7},{6,4},{7,5},{8,10},{9,11},{10,... | collective-permute-start | bytes 786440 | tf_op jit(solution)/shard_map/ppermute | solution.py:28
  173.3 0.7 copy-start.7
  182.1 31.8 %all-to-all-start.1 = ((bf16[8,32,3584]{2,1,0:T(8,128)(2,1)}), bf16[8,32,3584]{2,1,0:T(8,128)(2,1)S(1)}, u32[]{:S(2)}, u32[]{:S(2)}) async-start(bf16[8,32,3584]{2,1,0:T(8,128)(2,1)} %down.2), calls=%async_computation.1 | async-start | bytes 3670016 | tf_op jit(solution)/shard_map/all_to_all | solution.py:36
  194.6 7.9 %collective-permute-start.10 = (bf16[256,512]{1,0:T(8,128)(2,1)}, bf16[256,512]{1,0:T(8,128)(2,1)S(1)}, u32[]{:S(2)}, u32[]{:S(2)}) collective-permute-start(bf16[256,512]{1,0:T(8,128)(2,1)} %get-tuple-element.21), channel_id=1, source_target_pairs={{0,2},{1,3},{2,0},{3,1},{4,6},{5,7},{6,4},{7,5},{8,10},{9,11},{10,... | collective-permute-start | bytes 786440 | tf_op jit(solution)/shard_map/ppermute | solution.py:28
  202.5 0.7 copy-start.8
  213.9 1.3 copy-start.3
  215.2 30.6 %all-to-all-start.3 = ((bf16[8,32,3584]{2,1,0:T(8,128)(2,1)}), bf16[8,32,3584]{2,1,0:T(8,128)(2,1)}, u32[]{:S(2)}, u32[]{:S(2)}) async-start(bf16[8,32,3584]{2,1,0:T(8,128)(2,1)} %down.3), calls=%async_computation.3 | async-start | bytes 3670016 | tf_op jit(solution)/shard_map/all_to_all | solution.py:36

commit v2 on v1

v2 whole, which is shorter than its diff:
```python
import functools

import jax
import jax.numpy as jnp
from jax import lax
from jax.experimental import pallas as pl
from jax.experimental.pallas import tpu as pltpu
from jax.sharding import PartitionSpec as P

EXPERTS = 8
SLOTS = 32
SIDE = 4
GROUP = EXPERTS * SLOTS
CHUNK = 512
ROOM = 60 * 1024 * 1024
VMEM = pl.BlockSpec(memory_space=pltpu.VMEM)
ANY = pl.BlockSpec(memory_space=pl.ANY)


def place(x, y, core):
    return (x * SIDE + y) * 2 + core


def moved(value, by_x, xor_y, xor_core=0):
    pairs = [
        (place(x, y, c), place((x + by_x) % SIDE, y ^ xor_y, c ^ xor_core))
        for x in range(SIDE)
        for y in range(SIDE)
        for c in range(2)
    ]
    return lax.ppermute(value, "expert", pairs)


BLOCKS = [(by_x, xor_y) for xor_y in (0, 3) for by_x in range(SIDE)]
ORDER = [1, 3, 4, 2, 5, 7, 6]
ORDER_BACK = [4, 5, 7, 3, 1, 2, 6]


def from_behind(value, axis, by):
    devices = lax.axis_size(axis)
    pairs = [(i, i + by) for i in range(devices) if 0 <= i + by < devices]
    return lax.ppermute(value, axis, pairs)


def mm(a, b, dims=((1,), (0,))):
    return lax.dot_general(a, b, (dims, ((), ())), preferred_element_type=jnp.float32)


def chunks_of(width):
    return [slice(at, min(at + CHUNK, width)) for at in range(0, width, CHUNK)]


def prepare_one(at_end, at_row, recv, enter, gain, router_t, ids, blocks, stream, combine, normed):
    tokens, width = recv.shape
    edge = lax.axis_index("pipe") == (lax.axis_size("pipe") - 1 if at_end else 0)
    total = jnp.zeros((tokens, 1), jnp.float32)
    for cut in chunks_of(width):
        values = jnp.where(edge, enter[:, cut].astype(jnp.float32), recv[:, cut].astype(jnp.float32))
        stream[:, cut] = values.astype(jnp.bfloat16)
        total += jnp.sum(values * values, axis=-1, keepdims=True)
    scale = lax.rsqrt(total / width + 1e-06)
    logits = jnp.zeros((EXPERTS, tokens), jnp.float32)
    for cut in chunks_of(width):
        part = (stream[:, cut].astype(jnp.float32) * scale * gain[:, cut]).astype(jnp.bfloat16)
        normed[:, cut] = part
        logits += mm(router_t[:, cut], part, ((1,), (1,)))

    row = lax.broadcasted_iota(jnp.int32, (tokens, tokens), 0)
    col = lax.broadcasted_iota(jnp.int32, (tokens, tokens), 1)
    expert = lax.broadcasted_iota(jnp.int32, (EXPERTS, tokens), 0)
    picks = [ids[k : k + 1, :] == expert for k in range(2)]
    marks = jnp.where(picks[0] | picks[1], 1.0, 0.0).astype(jnp.bfloat16)
    spot = lax.axis_index("expert")
    my_x, my_half = lax.div(spot, 2 * SIDE), lax.rem(lax.div(spot, 4), 2)
    step = lax.rem(lax.div(expert, 2) - my_x + SIDE, SIDE)
    block = (lax.rem(expert, 2) ^ my_half) * SIDE + step
    at = (block * SLOTS).astype(jnp.float32) + mm(marks, jnp.where(row < col, 1.0, 0.0).astype(jnp.bfloat16))
    affinity = [jax.nn.sigmoid(jnp.sum(jnp.where(pick, logits, 0.0), axis=0, keepdims=True)) for pick in picks]
    both = affinity[0] + affinity[1]
    slot = lax.broadcasted_iota(jnp.int32, (GROUP, tokens), 0)
    placing = jnp.zeros((GROUP, tokens), jnp.float32)
    weighted = jnp.zeros((GROUP, tokens), jnp.float32)
    for pick, share in zip(picks, affinity):
        where = jnp.sum(jnp.where(pick, at, 0.0), axis=0, keepdims=True).astype(jnp.int32)
        placing += jnp.where(slot == where, 1.0, 0.0)
        weighted += jnp.where(slot == where, 2.5 * share / both, 0.0)
    placing = placing.astype(jnp.bfloat16)
    for cut in chunks_of(width):
        rows = mm(placing, normed[:, cut]).astype(jnp.bfloat16)
        for i, out in enumerate(blocks):
            out[at_row : at_row + SLOTS, cut] = rows[i * SLOTS : (i + 1) * SLOTS]
    padded = jnp.concatenate([weighted, jnp.zeros((GROUP, -tokens % 128), jnp.float32)], axis=1)
    combine[...] = padded.T[:tokens]


def prepare_kernel(earlier, recv_up, recv_down, enter_up, enter_down, gain, router_t, ids_up, ids_down, *rest):
    rest = rest[earlier:]
    blocks, (stream_up, stream_down, combine_up, combine_down, normed) = rest[:EXPERTS], rest[EXPERTS:]
    prepare_one(False, 0, recv_up, enter_up, gain, router_t, ids_up, blocks, stream_up, combine_up, normed)
    prepare_one(True, SLOTS, recv_down, enter_down, gain, router_t, ids_down, blocks, stream_down, combine_down, normed)


def prepare(recv_up, recv_down, enter_up, enter_down, gain, router_t, ids_up, ids_down, earlier):
    tokens, width = recv_up.shape
    shape = jax.ShapeDtypeStruct
    out = pl.pallas_call(
        functools.partial(prepare_kernel, len(earlier)),
        out_shape=[shape((2 * SLOTS, width), jnp.bfloat16)] * EXPERTS
        + [shape((tokens, width), jnp.bfloat16)] * 2
        + [shape((tokens, GROUP), jnp.float32)] * 2,
        in_specs=[VMEM] * 8 + [ANY] * len(earlier),
        out_specs=[VMEM] * (EXPERTS + 4),
        scratch_shapes=[pltpu.VMEM((tokens, width), jnp.bfloat16)],
        compiler_params=pltpu.CompilerParams(vmem_limit_bytes=ROOM),
        cost_estimate=pl.CostEstimate(flops=4 * GROUP * tokens * width, bytes_accessed=24 * tokens * width, transcendentals=0),
        name="prepare",
    )(recv_up, recv_down, enter_up, enter_down, gain, router_t, ids_up.T, ids_down.T, *earlier)
    return out[:EXPERTS], out[EXPERTS : EXPERTS + 2], out[EXPERTS + 2 :]


def hidden_kernel(*refs):
    blocks, gates, ups = refs[:EXPERTS], refs[EXPERTS : EXPERTS + 4], refs[EXPERTS + 4 : EXPERTS + 8]
    units, gate_sum, up_sum = refs[EXPERTS + 8 :]
    step = pl.program_id(0)

    @pl.when(step == 0)
    def _():
        gate_sum[...] = jnp.zeros_like(gate_sum)
        up_sum[...] = jnp.zeros_like(up_sum)

    rows = jnp.concatenate([block[...] for block in blocks], axis=0)
    part = gates[0].shape[1]
    for total, mats in ((gate_sum, gates), (up_sum, ups)):
        for i, mat in enumerate(mats):
            total[:, i * part : (i + 1) * part] += mm(rows, mat[...])

    @pl.when(step == pl.num_programs(0) - 1)
    def _():
        units[...] = (jax.nn.silu(gate_sum[...]) * up_sum[...]).astype(jnp.bfloat16)


def hidden(blocks, gates, ups):
    width, part = gates[0].shape
    deep = width // 2
    rows = 2 * GROUP
    return pl.pallas_call(
        hidden_kernel,
        grid=(width // deep,),
        out_shape=jax.ShapeDtypeStruct((rows, 4 * part), jnp.bfloat16),
        in_specs=[pl.BlockSpec((2 * SLOTS, deep), lambda k: (0, k))] * EXPERTS
        + [pl.BlockSpec((deep, part), lambda k: (k, 0))] * 8,
        out_specs=pl.BlockSpec((rows, 4 * part), lambda k: (0, 0)),
        scratch_shapes=[pltpu.VMEM((rows, 4 * part), jnp.float32)] * 2,
        compiler_params=pltpu.CompilerParams(vmem_limit_bytes=ROOM),
        cost_estimate=pl.CostEstimate(flops=0, bytes_accessed=0, transcendentals=0),
        name="hidden",
    )(*blocks, *gates, *ups)


def down_kernel(units, mat_a, mat_b, mat_c, mat_d, *blocks):
    mat = jnp.concatenate([mat_a[...], mat_b[...], mat_c[...], mat_d[...]], axis=0)
    rows = mm(units[...], mat).astype(jnp.bfloat16)
    for i, out in enumerate(blocks):
        out[...] = rows[i * 2 * SLOTS : (i + 1) * 2 * SLOTS]


def down(units, whole, parts, side):
    part, width = parts[0].shape
    deep = width // 2
    return pl.pallas_call(
        down_kernel,
        grid=(2,),
        out_shape=[jax.ShapeDtypeStruct((2 * SLOTS, width), jnp.bfloat16)] * EXPERTS,
        in_specs=[pl.BlockSpec(units.shape, lambda k: (0, 0))]
        + [pl.BlockSpec((part, deep), lambda k: (0, 2 * side + k))] * 2
        + [pl.BlockSpec((part, deep), lambda k: (0, k))] * 2,
        out_specs=[pl.BlockSpec((2 * SLOTS, deep), lambda k: (0, k))] * EXPERTS,
        compiler_params=pltpu.CompilerParams(vmem_limit_bytes=ROOM),
        cost_estimate=pl.CostEstimate(flops=0, bytes_accessed=0, transcendentals=0),
        name="down",
    )(units, *whole, *parts)


def finish_kernel(earlier, *refs):
    streams, combines, blocks, outs = refs[:2], refs[2:4], refs[4 : 4 + EXPERTS], refs[4 + EXPERTS + earlier :]
    tokens = streams[0].shape[0]
    for i in range(2):
        weights = combines[i][...]
        high = weights.astype(jnp.bfloat16)
        left = weights - high.astype(jnp.float32)
        middle = left.astype(jnp.bfloat16)
        low = (left - middle.astype(jnp.float32)).astype(jnp.bfloat16)
        terms = jnp.concatenate([high, middle, low], axis=0)
        rows = jnp.concatenate([block[i * SLOTS : (i + 1) * SLOTS] for block in blocks], axis=0)
        sums = mm(terms, rows)
        mixture = sums[:tokens] + sums[tokens : 2 * tokens] + sums[2 * tokens :]
        outs[i][...] = (streams[i][...].astype(jnp.float32) + mixture).astype(jnp.bfloat16)


def finish(streams, combines, blocks, side, begun):
    tokens, width = streams[0].shape
    deep = width // 4
    steps = blocks[0].shape[1] // deep
    column = pl.BlockSpec((tokens, deep), lambda k: (0, steps * side + k))
    return pl.pallas_call(
        functools.partial(finish_kernel, len(begun)),
        grid=(steps,),
        out_shape=[jax.ShapeDtypeStruct((tokens, width), jnp.bfloat16)] * 2,
        in_specs=[column] * 2
        + [pl.BlockSpec((tokens, GROUP), lambda k: (0, 0))] * 2
        + [pl.BlockSpec((2 * SLOTS, deep), lambda k: (0, k))] * EXPERTS
        + [ANY] * len(begun),
        out_specs=[column] * 2,
        input_output_aliases={4 + EXPERTS + i: i for i in range(len(begun))},
        compiler_params=pltpu.CompilerParams(vmem_limit_bytes=ROOM),
        cost_estimate=pl.CostEstimate(flops=6 * GROUP * width * tokens, bytes_accessed=8 * tokens * width, transcendentals=0),
        name="finish",
    )(*streams, *combines, *blocks, *begun)


def after(value, earlier):
    return pl.pallas_call(
        lambda *refs: None,
        out_shape=jax.ShapeDtypeStruct(value.shape, value.dtype),
        in_specs=[ANY] * (1 + len(earlier)),
        out_specs=ANY,
        input_output_aliases={0: 0},
        cost_estimate=pl.CostEstimate(flops=0, bytes_accessed=0, transcendentals=0),
        name="after",
    )(value, *earlier)


def exchange(blocks, sign, order, depth):
    out = {0: blocks[0]}
    for k, i in enumerate(order):
        block = after(blocks[i], (out[order[k - depth]],)) if k >= depth else blocks[i]
        out[i] = moved(block, sign * BLOCKS[i][0], BLOCKS[i][1])
    return [out[i] for i in range(EXPERTS)]


def body(up_prev, down_prev, enter_up, enter_down, norm_gain, router, w_gate, w_up, w_down, ids_up, ids_down):
    from_below = from_behind(up_prev[0], "pipe", 1)
    from_above = from_behind(down_prev[0], "pipe", -1)

    def of_core(value):
        return moved(value, 0, 0, 1)

    def of_pair(value):
        return moved(value, 0, 1)

    gate, up, whole = w_gate[0], w_up[0], w_down[0]
    gate_core, up_core = of_core(gate), of_core(up)
    blocks, streams, combines = prepare(
        from_below, from_above, enter_up, enter_down, norm_gain, router[0].T, ids_up[0], ids_down[0], (gate_core, up_core)
    )
    gate_pair, up_pair = of_pair(gate), of_pair(up)
    rows = exchange(blocks, 1, ORDER, 3)
    half = whole.shape[1] // 2
    low_pair = of_pair(after(whole[:, :half], (rows[ORDER[2]],)))
    high_pair = of_pair(after(whole[:, half:], (rows[ORDER[5]],)))
    gate_pair, up_pair = after(gate_pair, rows[1:]), after(up_pair, rows[1:])
    units = hidden(rows, (gate, gate_core, gate_pair, of_core(gate_pair)), (up, up_core, up_pair, of_core(up_pair)))
    own = (whole, of_core(whole))
    low_pair = after(low_pair, (units,))
    back = exchange(down(units, own, (low_pair, of_core(low_pair)), 0), -1, ORDER_BACK, 5)
    high_pair = after(high_pair, [back[i] for i in ORDER_BACK[:3]])
    outs = finish(streams, combines, back, 0, ())
    back = exchange(down(units, own, (high_pair, of_core(high_pair)), 1), -1, ORDER_BACK, 5)
    outs = finish(streams, combines, back, 1, outs)
    return outs[0][None], outs[1][None]


def solution(mesh):
    in_specs = (
        P("pipe", "expert", None),
        P("pipe", "expert", None),
        P("expert", None),
        P("expert", None),
        P("pipe", None),
        P("pipe", None, None),
        P("pipe", None, "expert"),
        P("pipe", None, "expert"),
        P("pipe", "expert", None),
        P("pipe", "expert", None),
        P("pipe", "expert", None),
    )
    out_specs = (P("pipe", "expert", None), P("pipe", "expert", None))
    return jax.shard_map(body, mesh=mesh, in_specs=in_specs, out_specs=out_specs, check_vma=False)
```

time: 253 us -> 209 us (0.83)
  waiting for transfers between devices: 155 us -> 96.5 us
  starting transfers between devices: 35.6 us -> 60.4 us
  Pallas kernels: 52.4 us -> 36.6 us
  local copies, waits for them, and re-layouts: 7.58 us -> 13.8 us
    ppermute x9 -> x32, starting transfers between devices: 5.42 us -> 53.4 us  [moved(): return lax.ppermute(value, 'expert', pairs)]
    all_to_all x4 -> x0, waiting for transfers between devices: 46.7 us -> none  [all_to_all(): lax.all_to_all(value, 'expert', split_axis=0, concat_axis=0, tiled=True,...]
    all_to_all x4 -> x0, starting transfers between devices: 23.2 us -> none  [all_to_all(): lax.all_to_all(value, 'expert', split_axis=0, concat_axis=0, tiled=True,...]
    ppermute x2, waiting for transfers between devices: 32.4 us -> 15.3 us  [from_behind(): return lax.ppermute(value, axis, pairs)]
    pallas_call x9 -> x20, Pallas kernels: 52.4 us -> 36.6 us  [the longest x1 13.4 us: hidden(): pl.pallas_call(hidden_kernel, grid=(width // deep,), out_shape=jax.ShapeD...]
    unnamed x22 -> x68, local copies, waits for them, and re-layouts: 5.03 us -> 12.4 us
    ppermute x9 -> x32, waiting for transfers between devices: 76.2 us -> 81.2 us  [moved(): return lax.ppermute(value, 'expert', pairs)]
  transfers between devices with their start and end apart: 15 -> 34, of which waited for: 9 -> 16; matrix products, arithmetic and copies ran while one was open for 1% -> 1% of each run, Pallas kernels for 17% -> 13%
where the time goes in v2:
time: 209 us; the launch traced here: 208 us
  waiting for transfers between devices  96.5 us (46%)
  starting transfers between devices  60.4 us (29%)
  Pallas kernels  36.6 us (18%)
  local copies, waits for them, and re-layouts  13.8 us (7%)
    ppermute x32, waiting for transfers between devices, moved(): return lax.ppermute(value, 'expert', pairs)  81.2 us
    ppermute x32, starting transfers between devices, moved(): return lax.ppermute(value, 'expert', pairs)  53.4 us
    ppermute x2, waiting for transfers between devices, from_behind(): return lax.ppermute(value, axis, pairs)  15.3 us
    pallas_call x1, Pallas kernels, hidden(): pl.pallas_call(hidden_kernel, grid=(width // deep,), out_shape=jax.ShapeD...  13.4 us
    unnamed x68, local copies, waits for them, and re-layouts  12.4 us
    pallas_call x2, Pallas kernels, down(): pl.pallas_call(down_kernel, grid=(2,), out_shape=[jax.ShapeDtypeStruct((2...  10.9 us
    ppermute x2, starting transfers between devices, from_behind(): return lax.ppermute(value, axis, pairs)  6.94 us
    pallas_call x2, Pallas kernels, finish(): pl.pallas_call(functools.partial(finish_kernel, len(begun)), grid=(steps,...  6.63 us
  transfers between devices with their start and end apart: 34, of which 16 were waited for; matrix products, arithmetic and copies ran while one was open for 1% of the time, Pallas kernels for 13%

profile of v2, /device:TPU:96, one launch (start us, length us, event | category | flops | bytes accessed | tf_op | source)
XLA Modules:
  0.0 208.2 jit_solution(8358944994366851278)
XLA Ops:
  1.2 5.0 %collective-permute-start = (bf16[96,3584]{1,0:T(8,128)(2,1)}, bf16[96,3584]{1,0:T(8,128)(2,1)S(1)}, u32[]{:S(2)}, u32[]{:S(2)}) collective-permute-start(bf16[96,3584]{1,0:T(8,128)(2,1)} %bitcast.31), channel_id=1, source_target_pairs={{0,32},{32,64},{64,96},{96,128},{128,160},{160,192},{192,224},{1,3... | collective-permute-start | bytes 2064392 | tf_op jit(solution)/shard_map/ppermute | solution.py:42
  6.3 1.9 collective-permute-start.1
  8.2 1.7 collective-permute-start.11
  9.9 11.7 %collective-permute-done.recv_up = bf16[96,3584]{1,0:T(8,128)(2,1)S(1)} collective-permute-done((bf16[96,3584]{1,0:T(8,128)(2,1)}, bf16[96,3584]{1,0:T(8,128)(2,1)S(1)}, u32[]{:S(2)}, u32[]{:S(2)}) %collective-permute-start) | collective-permute-done | bytes 688160 | tf_op jit(solution)/shard_map/ppermute | solution.py:42
  21.5 1.6 collective-permute-start.13
  23.1 3.6 %collective-permute-done.1.recv_down = bf16[96,3584]{1,0:T(8,128)(2,1)S(1)} collective-permute-done((bf16[96,3584]{1,0:T(8,128)(2,1)}, bf16[96,3584]{1,0:T(8,128)(2,1)S(1)}, u32[]{:S(2)}, u32[]{:S(2)}) %collective-permute-start.1) | collective-permute-done | bytes 688160 | tf_op jit(solution)/shard_map/ppermute | solution.py:42
  28.8 5.7 %prepare.1 = (bf16[64,3584]{1,0:T(8,128)(2,1)}, bf16[64,3584]{1,0:T(8,128)(2,1)}, bf16[64,3584]{1,0:T(8,128)(2,1)}, bf16[64,3584]{1,0:T(8,128)(2,1)}, bf16[64,35...) custom-call(bf16[96,3584]{1,0:T(8,128)(2,1)} %copy-done.18, ...), custom_call_target="tpu_custom_call" | custom-call | flops 352321536 | bytes 8257536 | tf_op jit(solution)/shard_map/prepare/pallas_call | solution.py:106
  34.5 1.6 collective-permute-start.4
  36.1 1.7 collective-permute-start.6
  37.8 3.0 %collective-permute-start.7 = (bf16[64,3584]{1,0:T(8,128)(2,1)}, bf16[64,3584]{1,0:T(8,128)(2,1)S(1)}, u32[]{:S(2)}, u32[]{:S(2)}) collective-permute-start(bf16[64,3584]{1,0:T(8,128)(2,1)} %get-tuple-element.42), channel_id=1, source_target_pairs={{0,6},{1,7},{2,4},{3,5},{4,2},{5,3},{6,0},{7,1},{8,14},{9,15},{10,... | collective-permute-start | bytes 1376264 | tf_op jit(solution)/shard_map/ppermute | solution.py:31
  40.8 6.5 %collective-permute-done.4.refs_1_ = bf16[64,3584]{1,0:T(8,128)(2,1)S(1)} collective-permute-done((bf16[64,3584]{1,0:T(8,128)(2,1)}, bf16[64,3584]{1,0:T(8,128)(2,1)S(1)}, u32[]{:S(2)}, u32[]{:S(2)}) %collective-permute-start.4) | collective-permute-done | bytes 458784 | tf_op jit(solution)/shard_map/ppermute | solution.py:31
  48.1 1.8 collective-permute-start.5
  50.7 3.0 %collective-permute-start.8 = (bf16[64,3584]{1,0:T(8,128)(2,1)}, bf16[64,3584]{1,0:T(8,128)(2,1)S(1)}, u32[]{:S(2)}, u32[]{:S(2)}) collective-permute-start(bf16[64,3584]{1,0:T(8,128)(2,1)} %after.15), channel_id=1, source_target_pairs={{0,14},{1,15},{2,12},{3,13},{4,10},{5,11},{6,8},{7,9},{8,22},{9,23... | collective-permute-start | bytes 1376264 | tf_op jit(solution)/shard_map/ppermute | solution.py:31
  54.6 2.3 %collective-permute-start.10 = (bf16[64,3584]{1,0:T(8,128)(2,1)}, bf16[64,3584]{1,0:T(8,128)(2,1)S(1)}, u32[]{:S(2)}, u32[]{:S(2)}) collective-permute-start(bf16[64,3584]{1,0:T(8,128)(2,1)} %after.17), channel_id=1, source_target_pairs={{0,30},{1,31},{2,28},{3,29},{4,26},{5,27},{6,24},{7,25},{8,6},{9,7... | collective-permute-start | bytes 1376264 | tf_op jit(solution)/shard_map/ppermute | solution.py:31
  56.9 6.5 %collective-permute-done.5.refs_1_.refs_2_ = bf16[64,3584]{1,0:T(8,128)(2,1)S(1)} collective-permute-done((bf16[64,3584]{1,0:T(8,128)(2,1)}, bf16[64,3584]{1,0:T(8,128)(2,1)S(1)}, u32[]{:S(2)}, u32[]{:S(2)}) %collective-permute-start.5) | collective-permute-done | bytes 458784 | tf_op jit(solution)/shard_map/ppermute | solution.py:31
  64.1 4.2 %collective-permute-start.9 = (bf16[64,3584]{1,0:T(8,128)(2,1)}, bf16[64,3584]{1,0:T(8,128)(2,1)S(1)}, u32[]{:S(2)}, u32[]{:S(2)}) collective-permute-start(bf16[64,3584]{1,0:T(8,128)(2,1)} %after.16), channel_id=1, source_target_pairs={{0,22},{1,23},{2,20},{3,21},{4,18},{5,19},{6,16},{7,17},{8,30},{9,... | collective-permute-start | bytes 1376264 | tf_op jit(solution)/shard_map/ppermute | solution.py:31
  68.3 20.4 %collective-permute-done.8.refs_5_ = bf16[64,3584]{1,0:T(8,128)(2,1)S(1)} collective-permute-done((bf16[64,3584]{1,0:T(8,128)(2,1)}, bf16[64,3584]{1,0:T(8,128)(2,1)S(1)}, u32[]{:S(2)}, u32[]{:S(2)}) %collective-permute-start.8) | collective-permute-done | bytes 458784 | tf_op jit(solution)/shard_map/ppermute | solution.py:31
  91.0 1.0 copy-done
  92.0 1.4 fusion
  93.5 1.1 collective-permute-done.12.refs_11_
  94.6 2.6 %collective-permute-done.14.refs_15_ = bf16[3584,256]{1,0:T(8,128)(2,1)} collective-permute-done((bf16[3584,256]{1,0:T(8,128)(2,1)}, bf16[3584,256]{1,0:T(8,128)(2,1)}, u32[]{:S(2)}, u32[]{:S(2)}) %collective-permute-start.14) | collective-permute-done | bytes 1835040 | tf_op jit(solution)/shard_map/ppermute | solution.py:31
  97.2 13.4 %hidden.1.refs_1_.units = bf16[512,1024]{1,0:T(8,128)(2,1)} custom-call(bf16[64,3584]{1,0:T(8,128)(2,1)} %get-tuple-element.38.refs_0_, bf16[64,3584]{1,0:T(8,128)(2,1)} %copy-done.4, bf16[64,3584]{1,0:T(8,128)(2,1)} %copy-done.6, bf16[64,3584]{1,0:T(8,128)(2,1)} %copy-done.5, bf16[64,3584]{1,0:T(8,128)(2,1)} %copy-done.1, bf16[64,3584]{1,0:T(8,128)(2,1)} %copy-done.8, ...), custom_call_target="tpu_custom_call" | custom-call | tf_op jit(solution)/shard_map/hidden/pallas_call | solution.py:146
  110.6 5.2 %collective-permute-done.17.refs_0_ = bf16[256,1792]{1,0:T(8,128)(2,1)S(1)} collective-permute-done((bf16[256,1792]{1,0:T(8,128)(2,1)}, bf16[256,1792]{1,0:T(8,128)(2,1)S(1)}, u32[]{:S(2)}, u32[]{:S(2)}) %collective-permute-start.17) | collective-permute-done | bytes 917536 | tf_op jit(solution)/shard_map/ppermute | solution.py:31
  115.8 0.9 copy-done.11
  117.0 2.5 %collective-permute-done.18.mat_d = bf16[256,1792]{1,0:T(8,128)(2,1)} collective-permute-done((bf16[256,1792]{1,0:T(8,128)(2,1)}, bf16[256,1792]{1,0:T(8,128)(2,1)}, u32[]{:S(2)}, u32[]{:S(2)}) %collective-permute-start.18) | collective-permute-done | bytes 917536 | tf_op jit(solution)/shard_map/ppermute | solution.py:31
  119.5 5.5 %down.2 = (bf16[64,1792]{1,0:T(8,128)(2,1)}, bf16[64,1792]{1,0:T(8,128)(2,1)}, bf16[64,1792]{1,0:T(8,128)(2,1)}, bf16[64,1792]{1,0:T(8,128)(2,1)}, bf16[64,1792]...) custom-call(bf16[512,1024]{1,0:T(8,128)(2,1)} %hidden.1.refs_1_.units, ...), custom_call_target="tpu_custom_call" | custom-call | tf_op jit(solution)/shard_map/down/pallas_call | solution.py:170
  125.0 1.4 collective-permute-start.19
  126.4 2.4 %collective-permute-start.20 = (bf16[64,1792]{1,0:T(8,128)(2,1)}, bf16[64,1792]{1,0:T(8,128)(2,1)S(1)}, u32[]{:S(2)}, u32[]{:S(2)}) collective-permute-start(bf16[64,1792]{1,0:T(8,128)(2,1)} %get-tuple-element.47), channel_id=1, source_target_pairs={{0,30},{1,31},{2,28},{3,29},{4,26},{5,27},{6,24},{7,25},{8,6},{9,7... | collective-permute-start | bytes 688136 | tf_op jit(solution)/shard_map/ppermute | solution.py:31
  128.8 1.7 collective-permute-start.21
  130.5 9.2 %collective-permute-done.16.refs_0_ = bf16[256,1792]{1,0:T(8,128)(2,1)S(1)} collective-permute-done((bf16[256,1792]{1,0:T(8,128)(2,1)}, bf16[256,1792]{1,0:T(8,128)(2,1)S(1)}, u32[]{:S(2)}, u32[]{:S(2)}) %collective-permute-start.16) | collective-permute-done | bytes 917536 | tf_op jit(solution)/shard_map/ppermute | solution.py:31
  139.7 4.3 %collective-permute-done.19.refs_1_.refs_8_ = bf16[64,1792]{1,0:T(8,128)(2,1)S(1)} collective-permute-done((bf16[64,1792]{1,0:T(8,128)(2,1)}, bf16[64,1792]{1,0:T(8,128)(2,1)S(1)}, u32[]{:S(2)}, u32[]{:S(2)}) %collective-permute-start.19) | collective-permute-done | bytes 229408 | tf_op jit(solution)/shard_map/ppermute | solution.py:31
  145.5 2.7 %collective-permute-done.22.mat_d = bf16[256,1792]{1,0:T(8,128)(2,1)S(1)} collective-permute-done((bf16[256,1792]{1,0:T(8,128)(2,1)}, bf16[256,1792]{1,0:T(8,128)(2,1)S(1)}, u32[]{:S(2)}, u32[]{:S(2)}) %collective-permute-start.22) | collective-permute-done | bytes 917536 | tf_op jit(solution)/shard_map/ppermute | solution.py:31
  148.1 0.9 copy-done.14
  149.1 5.4 %down.3 = (bf16[64,1792]{1,0:T(8,128)(2,1)}, bf16[64,1792]{1,0:T(8,128)(2,1)}, bf16[64,1792]{1,0:T(8,128)(2,1)}, bf16[64,1792]{1,0:T(8,128)(2,1)}, bf16[64,1792]...) custom-call(bf16[512,1024]{1,0:T(8,128)(2,1)} %hidden.1.refs_1_.units, ...), custom_call_target="tpu_custom_call" | custom-call | tf_op jit(solution)/shard_map/down/pallas_call | solution.py:170
  154.5 1.4 collective-permute-start.24
  155.9 2.5 %collective-permute-start.27 = (bf16[64,1792]{1,0:T(8,128)(2,1)}, bf16[64,1792]{1,0:T(8,128)(2,1)S(1)}, u32[]{:S(2)}, u32[]{:S(2)}) collective-permute-start(bf16[64,1792]{1,0:T(8,128)(2,1)} %get-tuple-element.54), channel_id=1, source_target_pairs={{0,30},{1,31},{2,28},{3,29},{4,26},{5,27},{6,24},{7,25},{8,6},{9,7... | collective-permute-start | bytes 688136 | tf_op jit(solution)/shard_map/ppermute | solution.py:31
  159.2 1.2 collective-permute-start.32
  160.4 1.0 collective-permute-start.31
  161.4 7.2 %collective-permute-done.24.refs_1_.refs_8_ = bf16[64,1792]{1,0:T(8,128)(2,1)S(1)} collective-permute-done((bf16[64,1792]{1,0:T(8,128)(2,1)}, bf16[64,1792]{1,0:T(8,128)(2,1)S(1)}, u32[]{:S(2)}, u32[]{:S(2)}) %collective-permute-start.24) | collective-permute-done | bytes 229408 | tf_op jit(solution)/shard_map/ppermute | solution.py:31
  168.6 3.7 %collective-permute-start.33 = (bf16[64,1792]{1,0:T(8,128)(2,1)}, bf16[64,1792]{1,0:T(8,128)(2,1)S(1)}, u32[]{:S(2)}, u32[]{:S(2)}) collective-permute-start(bf16[64,1792]{1,0:T(8,128)(2,1)} %after.27), channel_id=1, source_target_pairs={{0,22},{1,23},{2,20},{3,21},{4,18},{5,19},{6,16},{7,17},{8,30},{9,... | collective-permute-start | bytes 688136 | tf_op jit(solution)/shard_map/ppermute | solution.py:31
  172.4 1.2 collective-permute-start.23
  173.6 1.0 collective-permute-start.26
  175.1 12.0 %collective-permute-start.25 = (bf16[64,1792]{1,0:T(8,128)(2,1)}, bf16[64,1792]{1,0:T(8,128)(2,1)S(1)}, u32[]{:S(2)}, u32[]{:S(2)}) collective-permute-start(bf16[64,1792]{1,0:T(8,128)(2,1)} %after.24), channel_id=1, source_target_pairs={{0,16},{1,17},{2,18},{3,19},{4,20},{5,21},{6,22},{7,23},{8,24},{9,... | collective-permute-start | bytes 688136 | tf_op jit(solution)/shard_map/ppermute | solution.py:31
  187.8 3.3 %finish.2 = (bf16[96,3584]{1,0:T(8,128)(2,1)}, bf16[96,3584]{1,0:T(8,128)(2,1)}) custom-call(bf16[96,3584]{1,0:T(8,128)(2,1)} %get-tuple-element.34.refs_0_, bf16[96,3584]{1,0:T(8,128)(2,1)} %get-tuple-element.35.refs_1_, f32[96,256]{1,0:T(8,128)} %get-tuple-element.36.refs_2_, f32[96,256]{1,0:T(8,128)} %get-tuple-element.37.refs_3_, ...), custom_call_target="tpu_custom_call" | custom-call | flops 528482304 | bytes 2752512 | tf_op jit(solution)/shard_map/finish/pallas_call | solution.py:205
  191.1 4.9 %collective-permute-done.29.refs_11_ = bf16[64,1792]{1,0:T(8,128)(2,1)S(1)} collective-permute-done((bf16[64,1792]{1,0:T(8,128)(2,1)S(1)}, bf16[64,1792]{1,0:T(8,128)(2,1)S(1)}, u32[]{:S(2)}, u32[]{:S(2)}) %collective-permute-start.29) | collective-permute-done | bytes 229408 | tf_op jit(solution)/shard_map/ppermute | solution.py:31
  196.0 0.8 collective-permute-done.25.refs_6_
  196.8 7.2 %collective-permute-done.28.refs_10_ = bf16[64,1792]{1,0:T(8,128)(2,1)S(1)} collective-permute-done((bf16[64,1792]{1,0:T(8,128)(2,1)}, bf16[64,1792]{1,0:T(8,128)(2,1)S(1)}, u32[]{:S(2)}, u32[]{:S(2)}) %collective-permute-start.28) | collective-permute-done | bytes 229408 | tf_op jit(solution)/shard_map/ppermute | solution.py:31
  204.7 3.3 %finish.3 = (bf16[96,3584]{1,0:T(8,128)(2,1)}, bf16[96,3584]{1,0:T(8,128)(2,1)}) custom-call(bf16[96,3584]{1,0:T(8,128)(2,1)} %get-tuple-element.34.refs_0_, bf16[96,3584]{1,0:T(8,128)(2,1)} %get-tuple-element.35.refs_1_, f32[96,256]{1,0:T(8,128)} %get-tuple-element.36.refs_2_, ...), custom_call_target="tpu_custom_call", output_to_operand_aliasing={{0}: (12, {}), {1}: (13, {})} | custom-call | flops 528482304 | bytes 2752512 | tf_op jit(solution)/shard_map/finish/pallas_call | solution.py:205
  (109 shorter events, 12.7 us)
Async XLA Ops:
  0.6 26.1 %collective-permute-start.2 = (bf16[3584,256]{1,0:T(8,128)(2,1)}, bf16[3584,256]{1,0:T(8,128)(2,1)S(1)}, u32[]{:S(2)}, u32[]{:S(2)}) collective-permute-start(bf16[3584,256]{1,0:T(8,128)(2,1)} %bitcast.20), channel_id=1, source_target_pairs={{0,1},{1,0},{2,3},{3,2},{4,5},{5,4},{6,7},{7,6},{8,9},{9,8},{10,11... | collective-permute-start | bytes 5505032 | tf_op jit(solution)/shard_map/ppermute | solution.py:31
  0.7 26.0 %collective-permute-start.3 = (bf16[3584,256]{1,0:T(8,128)(2,1)}, bf16[3584,256]{1,0:T(8,128)(2,1)S(1)}, u32[]{:S(2)}, u32[]{:S(2)}) collective-permute-start(bf16[3584,256]{1,0:T(8,128)(2,1)} %bitcast.23), channel_id=1, source_target_pairs={{0,1},{1,0},{2,3},{3,2},{4,5},{5,4},{6,7},{7,6},{8,9},{9,8},{10,11... | collective-permute-start | bytes 5505032 | tf_op jit(solution)/shard_map/ppermute | solution.py:31
  1.2 20.3 %collective-permute-start = (bf16[96,3584]{1,0:T(8,128)(2,1)}, bf16[96,3584]{1,0:T(8,128)(2,1)S(1)}, u32[]{:S(2)}, u32[]{:S(2)}) collective-permute-start(bf16[96,3584]{1,0:T(8,128)(2,1)} %bitcast.31), channel_id=1, source_target_pairs={{0,32},{32,64},{64,96},{96,128},{128,160},{160,192},{192,224},{1,3... | collective-permute-start | bytes 2064392 | tf_op jit(solution)/shard_map/ppermute | solution.py:42
  6.3 20.5 %collective-permute-start.1 = (bf16[96,3584]{1,0:T(8,128)(2,1)}, bf16[96,3584]{1,0:T(8,128)(2,1)S(1)}, u32[]{:S(2)}, u32[]{:S(2)}) collective-permute-start(bf16[96,3584]{1,0:T(8,128)(2,1)} %bitcast.32), channel_id=1, source_target_pairs={{32,0},{64,32},{96,64},{128,96},{160,128},{192,160},{224,192},{33,... | collective-permute-start | bytes 2064392 | tf_op jit(solution)/shard_map/ppermute | solution.py:42
  8.2 60.2 %collective-permute-start.11 = (bf16[3584,256]{1,0:T(8,128)(2,1)}, bf16[3584,256]{1,0:T(8,128)(2,1)}, u32[]{:S(2)}, u32[]{:S(2)}) collective-permute-start(bf16[3584,256]{1,0:T(8,128)(2,1)} %bitcast.21), channel_id=1, source_target_pairs={{0,2},{1,3},{2,0},{3,1},{4,6},{5,7},{6,4},{7,5},{8,10},{9,11},{10,... | collective-permute-start | bytes 5505032 | tf_op jit(solution)/shard_map/ppermute | solution.py:31
  21.5 5.2 %copy-start.18 = (bf16[96,3584]{1,0:T(8,128)(2,1)}, bf16[96,3584]{1,0:T(8,128)(2,1)S(1)}, u32[]{:S(2)}) copy-start(bf16[96,3584]{1,0:T(8,128)(2,1)S(1)} %collective-permute-done.recv_up) | copy-start | bytes 2064388
  21.5 68.9 %collective-permute-start.13 = (bf16[3584,256]{1,0:T(8,128)(2,1)}, bf16[3584,256]{1,0:T(8,128)(2,1)}, u32[]{:S(2)}, u32[]{:S(2)}) collective-permute-start(bf16[3584,256]{1,0:T(8,128)(2,1)} %bitcast.24), channel_id=1, source_target_pairs={{0,2},{1,3},{2,0},{3,1},{4,6},{5,7},{6,4},{7,5},{8,10},{9,11},{10,... | collective-permute-start | bytes 5505032 | tf_op jit(solution)/shard_map/ppermute | solution.py:31
  34.5 12.9 %collective-permute-start.4 = (bf16[64,3584]{1,0:T(8,128)(2,1)}, bf16[64,3584]{1,0:T(8,128)(2,1)S(1)}, u32[]{:S(2)}, u32[]{:S(2)}) collective-permute-start(bf16[64,3584]{1,0:T(8,128)(2,1)} %get-tuple-element.39), channel_id=1, source_target_pairs={{0,8},{1,9},{2,10},{3,11},{4,12},{5,13},{6,14},{7,15},{8,16},{9,17... | collective-permute-start | bytes 1376264 | tf_op jit(solution)/shard_map/ppermute | solution.py:31
  36.1 13.9 %collective-permute-start.6 = (bf16[64,3584]{1,0:T(8,128)(2,1)}, bf16[64,3584]{1,0:T(8,128)(2,1)S(1)}, u32[]{:S(2)}, u32[]{:S(2)}) collective-permute-start(bf16[64,3584]{1,0:T(8,128)(2,1)} %get-tuple-element.41), channel_id=1, source_target_pairs={{0,24},{1,25},{2,26},{3,27},{4,28},{5,29},{6,30},{7,31},{8,0},{9,1... | collective-permute-start | bytes 1376264 | tf_op jit(solution)/shard_map/ppermute | solution.py:31
  37.8 16.0 %collective-permute-start.7 = (bf16[64,3584]{1,0:T(8,128)(2,1)}, bf16[64,3584]{1,0:T(8,128)(2,1)S(1)}, u32[]{:S(2)}, u32[]{:S(2)}) collective-permute-start(bf16[64,3584]{1,0:T(8,128)(2,1)} %get-tuple-element.42), channel_id=1, source_target_pairs={{0,6},{1,7},{2,4},{3,5},{4,2},{5,3},{6,0},{7,1},{8,14},{9,15},{10,... | collective-permute-start | bytes 1376264 | tf_op jit(solution)/shard_map/ppermute | solution.py:31
  48.1 15.2 %collective-permute-start.5 = (bf16[64,3584]{1,0:T(8,128)(2,1)}, bf16[64,3584]{1,0:T(8,128)(2,1)S(1)}, u32[]{:S(2)}, u32[]{:S(2)}) collective-permute-start(bf16[64,3584]{1,0:T(8,128)(2,1)} %after.14), channel_id=1, source_target_pairs={{0,16},{1,17},{2,18},{3,19},{4,20},{5,21},{6,22},{7,23},{8,24},{9,... | collective-permute-start | bytes 1376264 | tf_op jit(solution)/shard_map/ppermute | solution.py:31
  50.7 38.0 %collective-permute-start.8 = (bf16[64,3584]{1,0:T(8,128)(2,1)}, bf16[64,3584]{1,0:T(8,128)(2,1)S(1)}, u32[]{:S(2)}, u32[]{:S(2)}) collective-permute-start(bf16[64,3584]{1,0:T(8,128)(2,1)} %after.15), channel_id=1, source_target_pairs={{0,14},{1,15},{2,12},{3,13},{4,10},{5,11},{6,8},{7,9},{8,22},{9,23... | collective-permute-start | bytes 1376264 | tf_op jit(solution)/shard_map/ppermute | solution.py:31
  54.6 34.2 %collective-permute-start.10 = (bf16[64,3584]{1,0:T(8,128)(2,1)}, bf16[64,3584]{1,0:T(8,128)(2,1)S(1)}, u32[]{:S(2)}, u32[]{:S(2)}) collective-permute-start(bf16[64,3584]{1,0:T(8,128)(2,1)} %after.17), channel_id=1, source_target_pairs={{0,30},{1,31},{2,28},{3,29},{4,26},{5,27},{6,24},{7,25},{8,6},{9,7... | collective-permute-start | bytes 1376264 | tf_op jit(solution)/shard_map/ppermute | solution.py:31
  64.1 24.6 %collective-permute-start.9 = (bf16[64,3584]{1,0:T(8,128)(2,1)}, bf16[64,3584]{1,0:T(8,128)(2,1)S(1)}, u32[]{:S(2)}, u32[]{:S(2)}) collective-permute-start(bf16[64,3584]{1,0:T(8,128)(2,1)} %after.16), channel_id=1, source_target_pairs={{0,22},{1,23},{2,20},{3,21},{4,18},{5,19},{6,16},{7,17},{8,30},{9,... | collective-permute-start | bytes 1376264 | tf_op jit(solution)/shard_map/ppermute | solution.py:31
  90.5 4.1 %collective-permute-start.12 = (bf16[3584,256]{1,0:T(8,128)(2,1)}, bf16[3584,256]{1,0:T(8,128)(2,1)}, u32[]{:S(2)}, u32[]{:S(2)}) collective-permute-start(bf16[3584,256]{1,0:T(8,128)(2,1)} %after.18.refs_10_), channel_id=1, source_target_pairs={{0,1},{1,0},{2,3},{3,2},{4,5},{5,4},{6,7},{7,6},{8,9},{9,8},{10,11... | collective-permute-start | bytes 5505032 | tf_op jit(solution)/shard_map/ppermute | solution.py:31
  90.5 6.7 %collective-permute-start.14 = (bf16[3584,256]{1,0:T(8,128)(2,1)}, bf16[3584,256]{1,0:T(8,128)(2,1)}, u32[]{:S(2)}, u32[]{:S(2)}) collective-permute-start(bf16[3584,256]{1,0:T(8,128)(2,1)} %after.19.refs_14_), channel_id=1, source_target_pairs={{0,1},{1,0},{2,3},{3,2},{4,5},{5,4},{6,7},{7,6},{8,9},{9,8},{10,11... | collective-permute-start | bytes 5505032 | tf_op jit(solution)/shard_map/ppermute | solution.py:31
  93.3 22.4 %collective-permute-start.17 = (bf16[256,1792]{1,0:T(8,128)(2,1)}, bf16[256,1792]{1,0:T(8,128)(2,1)S(1)}, u32[]{:S(2)}, u32[]{:S(2)}) collective-permute-start(bf16[256,1792]{1,0:T(8,128)(2,1)} %after.21), channel_id=1, source_target_pairs={{0,2},{1,3},{2,0},{3,1},{4,6},{5,7},{6,4},{7,5},{8,10},{9,11},{10,... | collective-permute-start | bytes 2752520 | tf_op jit(solution)/shard_map/ppermute | solution.py:31
  93.5 23.5 %collective-permute-start.15 = (bf16[256,3584]{1,0:T(8,128)(2,1)S(1)}, bf16[256,3584]{1,0:T(8,128)(2,1)}, u32[]{:S(2)}, u32[]{:S(2)}) collective-permute-start(bf16[256,3584]{1,0:T(8,128)(2,1)S(1)} %bitcast.19), channel_id=1, source_target_pairs={{0,1},{1,0},{2,3},{3,2},{4,5},{5,4},{6,7},{7,6},{8,9},{9,8},{10,11... | collective-permute-start | bytes 5505032 | tf_op jit(solution)/shard_map/ppermute | solution.py:31
  116.7 2.8 %collective-permute-start.18 = (bf16[256,1792]{1,0:T(8,128)(2,1)}, bf16[256,1792]{1,0:T(8,128)(2,1)}, u32[]{:S(2)}, u32[]{:S(2)}) collective-permute-start(bf16[256,1792]{1,0:T(8,128)(2,1)} %after.22.mat_c), channel_id=1, source_target_pairs={{0,1},{1,0},{2,3},{3,2},{4,5},{5,4},{6,7},{7,6},{8,9},{9,8},{10,11... | collective-permute-start | bytes 2752520 | tf_op jit(solution)/shard_map/ppermute | solution.py:31
  116.7 23.0 %collective-permute-start.16 = (bf16[256,1792]{1,0:T(8,128)(2,1)}, bf16[256,1792]{1,0:T(8,128)(2,1)S(1)}, u32[]{:S(2)}, u32[]{:S(2)}) collective-permute-start(bf16[256,1792]{1,0:T(8,128)(2,1)} %after.20), channel_id=1, source_target_pairs={{0,2},{1,3},{2,0},{3,1},{4,6},{5,7},{6,4},{7,5},{8,10},{9,11},{10,... | collective-permute-start | bytes 2752520 | tf_op jit(solution)/shard_map/ppermute | solution.py:31
  125.0 19.0 %collective-permute-start.19 = (bf16[64,1792]{1,0:T(8,128)(2,1)}, bf16[64,1792]{1,0:T(8,128)(2,1)S(1)}, u32[]{:S(2)}, u32[]{:S(2)}) collective-permute-start(bf16[64,1792]{1,0:T(8,128)(2,1)} %get-tuple-element.46), channel_id=1, source_target_pairs={{0,6},{1,7},{2,4},{3,5},{4,2},{5,3},{6,0},{7,1},{8,14},{9,15},{10,... | collective-permute-start | bytes 688136 | tf_op jit(solution)/shard_map/ppermute | solution.py:31
  126.4 17.6 %collective-permute-start.20 = (bf16[64,1792]{1,0:T(8,128)(2,1)}, bf16[64,1792]{1,0:T(8,128)(2,1)S(1)}, u32[]{:S(2)}, u32[]{:S(2)}) collective-permute-start(bf16[64,1792]{1,0:T(8,128)(2,1)} %get-tuple-element.47), channel_id=1, source_target_pairs={{0,30},{1,31},{2,28},{3,29},{4,26},{5,27},{6,24},{7,25},{8,6},{9,7... | collective-permute-start | bytes 688136 | tf_op jit(solution)/shard_map/ppermute | solution.py:31
  128.8 15.2 %collective-permute-start.21 = (bf16[64,1792]{1,0:T(8,128)(2,1)}, bf16[64,1792]{1,0:T(8,128)(2,1)S(1)}, u32[]{:S(2)}, u32[]{:S(2)}) collective-permute-start(bf16[64,1792]{1,0:T(8,128)(2,1)} %get-tuple-element.48), channel_id=1, source_target_pairs={{0,14},{1,15},{2,12},{3,13},{4,10},{5,11},{6,8},{7,9},{8,22},{9,23... | collective-permute-start | bytes 688136 | tf_op jit(solution)/shard_map/ppermute | solution.py:31
  139.7 4.3 %copy-start.10 = (bf16[256,1792]{1,0:T(8,128)(2,1)}, bf16[256,1792]{1,0:T(8,128)(2,1)S(1)}, u32[]{:S(2)}) copy-start(bf16[256,1792]{1,0:T(8,128)(2,1)S(1)} %collective-permute-done.16.refs_0_) | copy-start | bytes 2752516
  145.4 12.9 %copy-start.32 = (bf16[64,1792]{1,0:T(8,128)(2,1)S(1)}, bf16[64,1792]{1,0:T(8,128)(2,1)}, u32[]{:S(2)}) copy-start(bf16[64,1792]{1,0:T(8,128)(2,1)} %get-tuple-element.58) | copy-start | bytes 688132
  145.4 13.8 %copy-start.29 = (bf16[64,1792]{1,0:T(8,128)(2,1)S(1)}, bf16[64,1792]{1,0:T(8,128)(2,1)}, u32[]{:S(2)}) copy-start(bf16[64,1792]{1,0:T(8,128)(2,1)} %get-tuple-element.60) | copy-start | bytes 688132
  145.4 2.7 %collective-permute-start.22 = (bf16[256,1792]{1,0:T(8,128)(2,1)}, bf16[256,1792]{1,0:T(8,128)(2,1)S(1)}, u32[]{:S(2)}, u32[]{:S(2)}) collective-permute-start(bf16[256,1792]{1,0:T(8,128)(2,1)} %after.23.mat_c), channel_id=1, source_target_pairs={{0,1},{1,0},{2,3},{3,2},{4,5},{5,4},{6,7},{7,6},{8,9},{9,8},{10,11... | collective-permute-start | bytes 2752520 | tf_op jit(solution)/shard_map/ppermute | solution.py:31
  154.5 17.9 %copy-start.33 = (bf16[64,1792]{1,0:T(8,128)(2,1)S(1)}, bf16[64,1792]{1,0:T(8,128)(2,1)}, u32[]{:S(2)}) copy-start(bf16[64,1792]{1,0:T(8,128)(2,1)} %get-tuple-element.50) | copy-start | bytes 688132
  154.5 19.1 %copy-start.31 = (bf16[64,1792]{1,0:T(8,128)(2,1)S(1)}, bf16[64,1792]{1,0:T(8,128)(2,1)}, u32[]{:S(2)}) copy-start(bf16[64,1792]{1,0:T(8,128)(2,1)} %get-tuple-element.53) | copy-start | bytes 688132
  154.5 20.0 %copy-start.30 = (bf16[64,1792]{1,0:T(8,128)(2,1)S(1)}, bf16[64,1792]{1,0:T(8,128)(2,1)}, u32[]{:S(2)}) copy-start(bf16[64,1792]{1,0:T(8,128)(2,1)} %get-tuple-element.56) | copy-start | bytes 688132
  154.5 14.1 %collective-permute-start.24 = (bf16[64,1792]{1,0:T(8,128)(2,1)}, bf16[64,1792]{1,0:T(8,128)(2,1)S(1)}, u32[]{:S(2)}, u32[]{:S(2)}) collective-permute-start(bf16[64,1792]{1,0:T(8,128)(2,1)} %get-tuple-element.52), channel_id=1, source_target_pairs={{0,6},{1,7},{2,4},{3,5},{4,2},{5,3},{6,0},{7,1},{8,14},{9,15},{10,... | collective-permute-start | bytes 688136 | tf_op jit(solution)/shard_map/ppermute | solution.py:31
  155.9 16.5 %collective-permute-start.27 = (bf16[64,1792]{1,0:T(8,128)(2,1)}, bf16[64,1792]{1,0:T(8,128)(2,1)S(1)}, u32[]{:S(2)}, u32[]{:S(2)}) collective-permute-start(bf16[64,1792]{1,0:T(8,128)(2,1)} %get-tuple-element.54), channel_id=1, source_target_pairs={{0,30},{1,31},{2,28},{3,29},{4,26},{5,27},{6,24},{7,25},{8,6},{9,7... | collective-permute-start | bytes 688136 | tf_op jit(solution)/shard_map/ppermute | solution.py:31
  158.4 15.2 %collective-permute-start.30 = (bf16[64,1792]{1,0:T(8,128)(2,1)S(1)}, bf16[64,1792]{1,0:T(8,128)(2,1)S(1)}, u32[]{:S(2)}, u32[]{:S(2)}) collective-permute-start(bf16[64,1792]{1,0:T(8,128)(2,1)S(1)} %copy-done.32), channel_id=1, source_target_pairs={{0,24},{1,25},{2,26},{3,27},{4,28},{5,29},{6,30},{7,31},{8,0},{9,1... | collective-permute-start | bytes 688136 | tf_op jit(solution)/shard_map/ppermute | solution.py:31
  159.2 15.4 %collective-permute-start.32 = (bf16[64,1792]{1,0:T(8,128)(2,1)S(1)}, bf16[64,1792]{1,0:T(8,128)(2,1)S(1)}, u32[]{:S(2)}, u32[]{:S(2)}) collective-permute-start(bf16[64,1792]{1,0:T(8,128)(2,1)S(1)} %copy-done.29), channel_id=1, source_target_pairs={{0,8},{1,9},{2,10},{3,11},{4,12},{5,13},{6,14},{7,15},{8,16},{9,17... | collective-permute-start | bytes 688136 | tf_op jit(solution)/shard_map/ppermute | solution.py:31
  160.4 14.7 %collective-permute-start.31 = (bf16[64,1792]{1,0:T(8,128)(2,1)}, bf16[64,1792]{1,0:T(8,128)(2,1)S(1)}, u32[]{:S(2)}, u32[]{:S(2)}) collective-permute-start(bf16[64,1792]{1,0:T(8,128)(2,1)} %after.26), channel_id=1, source_target_pairs={{0,16},{1,17},{2,18},{3,19},{4,20},{5,21},{6,22},{7,23},{8,24},{9,... | collective-permute-start | bytes 688136 | tf_op jit(solution)/shard_map/ppermute | solution.py:31
  168.6 18.5 %collective-permute-start.33 = (bf16[64,1792]{1,0:T(8,128)(2,1)}, bf16[64,1792]{1,0:T(8,128)(2,1)S(1)}, u32[]{:S(2)}, u32[]{:S(2)}) collective-permute-start(bf16[64,1792]{1,0:T(8,128)(2,1)} %after.27), channel_id=1, source_target_pairs={{0,22},{1,23},{2,20},{3,21},{4,18},{5,19},{6,16},{7,17},{8,30},{9,... | collective-permute-start | bytes 688136 | tf_op jit(solution)/shard_map/ppermute | solution.py:31
  172.4 18.7 %collective-permute-start.23 = (bf16[64,1792]{1,0:T(8,128)(2,1)S(1)}, bf16[64,1792]{1,0:T(8,128)(2,1)S(1)}, u32[]{:S(2)}, u32[]{:S(2)}) collective-permute-start(bf16[64,1792]{1,0:T(8,128)(2,1)S(1)} %copy-done.33), channel_id=1, source_target_pairs={{0,24},{1,25},{2,26},{3,27},{4,28},{5,29},{6,30},{7,31},{8,0},{9,1... | collective-permute-start | bytes 688136 | tf_op jit(solution)/shard_map/ppermute | solution.py:31
  173.6 13.7 %copy-start.21 = (bf16[64,1792]{1,0:T(8,128)(2,1)}, bf16[64,1792]{1,0:T(8,128)(2,1)S(1)}, u32[]{:S(2)}) copy-start(bf16[64,1792]{1,0:T(8,128)(2,1)S(1)} %collective-permute-done.30.refs_5_) | copy-start | bytes 688132
  173.6 17.5 %collective-permute-start.26 = (bf16[64,1792]{1,0:T(8,128)(2,1)S(1)}, bf16[64,1792]{1,0:T(8,128)(2,1)S(1)}, u32[]{:S(2)}, u32[]{:S(2)}) collective-permute-start(bf16[64,1792]{1,0:T(8,128)(2,1)S(1)} %copy-done.31), channel_id=1, source_target_pairs={{0,8},{1,9},{2,10},{3,11},{4,12},{5,13},{6,14},{7,15},{8,16},{9,17... | collective-permute-start | bytes 688136 | tf_op jit(solution)/shard_map/ppermute | solution.py:31
  174.6 12.7 %copy-start.22 = (bf16[64,1792]{1,0:T(8,128)(2,1)}, bf16[64,1792]{1,0:T(8,128)(2,1)S(1)}, u32[]{:S(2)}) copy-start(bf16[64,1792]{1,0:T(8,128)(2,1)S(1)} %collective-permute-done.32.refs_7_) | copy-start | bytes 688132
  174.6 21.4 %collective-permute-start.29 = (bf16[64,1792]{1,0:T(8,128)(2,1)S(1)}, bf16[64,1792]{1,0:T(8,128)(2,1)S(1)}, u32[]{:S(2)}, u32[]{:S(2)}) collective-permute-start(bf16[64,1792]{1,0:T(8,128)(2,1)S(1)} %copy-done.30), channel_id=1, source_target_pairs={{0,14},{1,15},{2,12},{3,13},{4,10},{5,11},{6,8},{7,9},{8,22},{9,23... | collective-permute-start | bytes 688136 | tf_op jit(solution)/shard_map/ppermute | solution.py:31
  175.1 12.2 %copy-start.24 = (bf16[64,1792]{1,0:T(8,128)(2,1)}, bf16[64,1792]{1,0:T(8,128)(2,1)S(1)}, u32[]{:S(2)}) copy-start(bf16[64,1792]{1,0:T(8,128)(2,1)S(1)} %collective-permute-done.31.refs_6_) | copy-start | bytes 688132
  175.1 21.8 %collective-permute-start.25 = (bf16[64,1792]{1,0:T(8,128)(2,1)}, bf16[64,1792]{1,0:T(8,128)(2,1)S(1)}, u32[]{:S(2)}, u32[]{:S(2)}) collective-permute-start(bf16[64,1792]{1,0:T(8,128)(2,1)} %after.24), channel_id=1, source_target_pairs={{0,16},{1,17},{2,18},{3,19},{4,20},{5,21},{6,22},{7,23},{8,24},{9,... | collective-permute-start | bytes 688136 | tf_op jit(solution)/shard_map/ppermute | solution.py:31
  187.1 17.0 %collective-permute-start.28 = (bf16[64,1792]{1,0:T(8,128)(2,1)}, bf16[64,1792]{1,0:T(8,128)(2,1)S(1)}, u32[]{:S(2)}, u32[]{:S(2)}) collective-permute-start(bf16[64,1792]{1,0:T(8,128)(2,1)} %after.25), channel_id=1, source_target_pairs={{0,22},{1,23},{2,20},{3,21},{4,18},{5,19},{6,16},{7,17},{8,30},{9,... | collective-permute-start | bytes 688136 | tf_op jit(solution)/shard_map/ppermute | solution.py:31
  191.1 13.0 %copy-start.20 = (bf16[64,1792]{1,0:T(8,128)(2,1)}, bf16[64,1792]{1,0:T(8,128)(2,1)S(1)}, u32[]{:S(2)}) copy-start(bf16[64,1792]{1,0:T(8,128)(2,1)S(1)} %collective-permute-done.23.refs_5_) | copy-start | bytes 688132
  191.1 13.0 %copy-start.23 = (bf16[64,1792]{1,0:T(8,128)(2,1)}, bf16[64,1792]{1,0:T(8,128)(2,1)S(1)}, u32[]{:S(2)}) copy-start(bf16[64,1792]{1,0:T(8,128)(2,1)S(1)} %collective-permute-done.26.refs_7_) | copy-start | bytes 688132
  196.0 8.1 %copy-start.25 = (bf16[64,1792]{1,0:T(8,128)(2,1)}, bf16[64,1792]{1,0:T(8,128)(2,1)S(1)}, u32[]{:S(2)}) copy-start(bf16[64,1792]{1,0:T(8,128)(2,1)S(1)} %collective-permute-done.29.refs_11_) | copy-start | bytes 688132
  196.8 7.2 %copy-start.27 = (bf16[64,1792]{1,0:T(8,128)(2,1)}, bf16[64,1792]{1,0:T(8,128)(2,1)S(1)}, u32[]{:S(2)}) copy-start(bf16[64,1792]{1,0:T(8,128)(2,1)S(1)} %collective-permute-done.25.refs_6_) | copy-start | bytes 688132
  (20 other events, 21.9 us)

commit v3 on v2

--- a/solution.py
+++ b/solution.py
@@ -33,7 +33,8 @@
 
 BLOCKS = [(by_x, xor_y) for xor_y in (0, 3) for by_x in range(SIDE)]
 ORDER = [1, 3, 4, 2, 5, 7, 6]
-ORDER_BACK = [4, 5, 7, 3, 1, 2, 6]
+ORDER_LOW = [5, 7, 2, 4, 1, 3, 6]
+ORDER_HIGH = [6, 2, 5, 7, 1, 3, 4]
 
 
 def from_behind(value, axis, by):
@@ -262,10 +263,10 @@
     units = hidden(rows, (gate, gate_core, gate_pair, of_core(gate_pair)), (up, up_core, up_pair, of_core(up_pair)))
     own = (whole, of_core(whole))
     low_pair = after(low_pair, (units,))
-    back = exchange(down(units, own, (low_pair, of_core(low_pair)), 0), -1, ORDER_BACK, 5)
-    high_pair = after(high_pair, [back[i] for i in ORDER_BACK[:3]])
+    back = exchange(down(units, own, (low_pair, of_core(low_pair)), 0), -1, ORDER_LOW, 5)
+    high_pair = after(high_pair, [back[i] for i in ORDER_LOW[:4]])
     outs = finish(streams, combines, back, 0, ())
-    back = exchange(down(units, own, (high_pair, of_core(high_pair)), 1), -1, ORDER_BACK, 5)
+    back = exchange(down(units, own, (high_pair, of_core(high_pair)), 1), -1, ORDER_HIGH, 5)
     outs = finish(streams, combines, back, 1, outs)
     return outs[0][None], outs[1][None]
 

time: 209 us -> 200 us (0.957)
  starting transfers between devices: 60.4 us -> 56.2 us
  waiting for transfers between devices: 96.5 us -> 93.7 us
    ppermute x32, starting transfers between devices: 53.4 us -> 49.3 us  [moved(): return lax.ppermute(value, 'expert', pairs)]
    ppermute x32, waiting for transfers between devices: 81.2 us -> 78.4 us  [moved(): return lax.ppermute(value, 'expert', pairs)]
    unnamed x68 -> x64, local copies, waits for them, and re-layouts: 12.4 us -> 11.1 us
  transfers between devices with their start and end apart: 34 -> 34, of which waited for: 16 -> 21; matrix products, arithmetic and copies ran while one was open for 1% -> 1% of each run, Pallas kernels for 13% -> 14%
where the time goes in v3:
time: 200 us
  waiting for transfers between devices  93.7 us (47%)
  starting transfers between devices  56.2 us (28%)
  Pallas kernels  36.5 us (18%)
  local copies, waits for them, and re-layouts  12.5 us (6%)
    ppermute x32, waiting for transfers between devices, moved(): return lax.ppermute(value, 'expert', pairs)  78.4 us
    ppermute x32, starting transfers between devices, moved(): return lax.ppermute(value, 'expert', pairs)  49.3 us
    ppermute x2, waiting for transfers between devices, from_behind(): return lax.ppermute(value, axis, pairs)  15.3 us
    pallas_call x1, Pallas kernels, hidden(): pl.pallas_call(hidden_kernel, grid=(width // deep,), out_shape=jax.ShapeD...  13.4 us
    unnamed x64, local copies, waits for them, and re-layouts  11.1 us
    pallas_call x2, Pallas kernels, down(): pl.pallas_call(down_kernel, grid=(2,), out_shape=[jax.ShapeDtypeStruct((2...  10.8 us
    ppermute x2, starting transfers between devices, from_behind(): return lax.ppermute(value, axis, pairs)  6.94 us
    pallas_call x2, Pallas kernels, finish(): pl.pallas_call(functools.partial(finish_kernel, len(begun)), grid=(steps,...  6.64 us
  transfers between devices with their start and end apart: 34, of which 21 were waited for; matrix products, arithmetic and copies ran while one was open for 1% of the time, Pallas kernels for 14%

profile of v3, /device:TPU:96, one launch (start us, length us, event | category | flops | bytes accessed | tf_op | source)
XLA Modules:
  0.0 199.9 jit_solution(15022324079724979317)
XLA Ops:
  1.2 5.0 %collective-permute-start = (bf16[96,3584]{1,0:T(8,128)(2,1)}, bf16[96,3584]{1,0:T(8,128)(2,1)S(1)}, u32[]{:S(2)}, u32[]{:S(2)}) collective-permute-start(bf16[96,3584]{1,0:T(8,128)(2,1)} %bitcast.31), channel_id=1, source_target_pairs={{0,32},{32,64},{64,96},{96,128},{128,160},{160,192},{192,224},{1,3... | collective-permute-start | bytes 2064392 | tf_op jit(solution)/shard_map/ppermute | solution.py:43
  6.3 1.9 collective-permute-start.1
  8.2 1.7 collective-permute-start.11
  9.9 11.7 %collective-permute-done.recv_up = bf16[96,3584]{1,0:T(8,128)(2,1)S(1)} collective-permute-done((bf16[96,3584]{1,0:T(8,128)(2,1)}, bf16[96,3584]{1,0:T(8,128)(2,1)S(1)}, u32[]{:S(2)}, u32[]{:S(2)}) %collective-permute-start) | collective-permute-done | bytes 688160 | tf_op jit(solution)/shard_map/ppermute | solution.py:43
  21.5 1.6 collective-permute-start.13
  23.1 3.6 %collective-permute-done.1.recv_down = bf16[96,3584]{1,0:T(8,128)(2,1)S(1)} collective-permute-done((bf16[96,3584]{1,0:T(8,128)(2,1)}, bf16[96,3584]{1,0:T(8,128)(2,1)S(1)}, u32[]{:S(2)}, u32[]{:S(2)}) %collective-permute-start.1) | collective-permute-done | bytes 688160 | tf_op jit(solution)/shard_map/ppermute | solution.py:43
  28.8 5.7 %prepare.1 = (bf16[64,3584]{1,0:T(8,128)(2,1)}, bf16[64,3584]{1,0:T(8,128)(2,1)}, bf16[64,3584]{1,0:T(8,128)(2,1)}, bf16[64,3584]{1,0:T(8,128)(2,1)}, bf16[64,35...) custom-call(bf16[96,3584]{1,0:T(8,128)(2,1)} %copy-done.19, ...), custom_call_target="tpu_custom_call" | custom-call | flops 352321536 | bytes 8257536 | tf_op jit(solution)/shard_map/prepare/pallas_call | solution.py:107
  34.5 1.6 collective-permute-start.4
  36.1 1.7 collective-permute-start.6
  37.8 3.0 %collective-permute-start.7 = (bf16[64,3584]{1,0:T(8,128)(2,1)}, bf16[64,3584]{1,0:T(8,128)(2,1)S(1)}, u32[]{:S(2)}, u32[]{:S(2)}) collective-permute-start(bf16[64,3584]{1,0:T(8,128)(2,1)} %get-tuple-element.42), channel_id=1, source_target_pairs={{0,6},{1,7},{2,4},{3,5},{4,2},{5,3},{6,0},{7,1},{8,14},{9,15},{10,... | collective-permute-start | bytes 1376264 | tf_op jit(solution)/shard_map/ppermute | solution.py:31
  40.8 6.5 %collective-permute-done.4.refs_1_ = bf16[64,3584]{1,0:T(8,128)(2,1)S(1)} collective-permute-done((bf16[64,3584]{1,0:T(8,128)(2,1)}, bf16[64,3584]{1,0:T(8,128)(2,1)S(1)}, u32[]{:S(2)}, u32[]{:S(2)}) %collective-permute-start.4) | collective-permute-done | bytes 458784 | tf_op jit(solution)/shard_map/ppermute | solution.py:31
  48.1 1.8 collective-permute-start.5
  50.7 3.0 %collective-permute-start.8 = (bf16[64,3584]{1,0:T(8,128)(2,1)}, bf16[64,3584]{1,0:T(8,128)(2,1)S(1)}, u32[]{:S(2)}, u32[]{:S(2)}) collective-permute-start(bf16[64,3584]{1,0:T(8,128)(2,1)} %after.15), channel_id=1, source_target_pairs={{0,14},{1,15},{2,12},{3,13},{4,10},{5,11},{6,8},{7,9},{8,22},{9,23... | collective-permute-start | bytes 1376264 | tf_op jit(solution)/shard_map/ppermute | solution.py:31
  54.6 2.3 %collective-permute-start.10 = (bf16[64,3584]{1,0:T(8,128)(2,1)}, bf16[64,3584]{1,0:T(8,128)(2,1)S(1)}, u32[]{:S(2)}, u32[]{:S(2)}) collective-permute-start(bf16[64,3584]{1,0:T(8,128)(2,1)} %after.17), channel_id=1, source_target_pairs={{0,30},{1,31},{2,28},{3,29},{4,26},{5,27},{6,24},{7,25},{8,6},{9,7... | collective-permute-start | bytes 1376264 | tf_op jit(solution)/shard_map/ppermute | solution.py:31
  56.9 6.5 %collective-permute-done.5.refs_1_.refs_2_ = bf16[64,3584]{1,0:T(8,128)(2,1)S(1)} collective-permute-done((bf16[64,3584]{1,0:T(8,128)(2,1)}, bf16[64,3584]{1,0:T(8,128)(2,1)S(1)}, u32[]{:S(2)}, u32[]{:S(2)}) %collective-permute-start.5) | collective-permute-done | bytes 458784 | tf_op jit(solution)/shard_map/ppermute | solution.py:31
  64.1 4.2 %collective-permute-start.9 = (bf16[64,3584]{1,0:T(8,128)(2,1)}, bf16[64,3584]{1,0:T(8,128)(2,1)S(1)}, u32[]{:S(2)}, u32[]{:S(2)}) collective-permute-start(bf16[64,3584]{1,0:T(8,128)(2,1)} %after.16), channel_id=1, source_target_pairs={{0,22},{1,23},{2,20},{3,21},{4,18},{5,19},{6,16},{7,17},{8,30},{9,... | collective-permute-start | bytes 1376264 | tf_op jit(solution)/shard_map/ppermute | solution.py:31
  68.3 20.4 %collective-permute-done.8.refs_5_ = bf16[64,3584]{1,0:T(8,128)(2,1)S(1)} collective-permute-done((bf16[64,3584]{1,0:T(8,128)(2,1)}, bf16[64,3584]{1,0:T(8,128)(2,1)S(1)}, u32[]{:S(2)}, u32[]{:S(2)}) %collective-permute-start.8) | collective-permute-done | bytes 458784 | tf_op jit(solution)/shard_map/ppermute | solution.py:31
  92.0 1.3 fusion
  93.5 1.1 collective-permute-done.12.refs_11_
  94.6 2.6 %collective-permute-done.14.refs_15_ = bf16[3584,256]{1,0:T(8,128)(2,1)} collective-permute-done((bf16[3584,256]{1,0:T(8,128)(2,1)}, bf16[3584,256]{1,0:T(8,128)(2,1)}, u32[]{:S(2)}, u32[]{:S(2)}) %collective-permute-start.14) | collective-permute-done | bytes 1835040 | tf_op jit(solution)/shard_map/ppermute | solution.py:31
  97.2 13.4 %hidden.1.refs_1_.units = bf16[512,1024]{1,0:T(8,128)(2,1)} custom-call(bf16[64,3584]{1,0:T(8,128)(2,1)} %get-tuple-element.38.refs_0_, bf16[64,3584]{1,0:T(8,128)(2,1)} %copy-done.4, bf16[64,3584]{1,0:T(8,128)(2,1)} %copy-done.6, bf16[64,3584]{1,0:T(8,128)(2,1)} %copy-done.5, bf16[64,3584]{1,0:T(8,128)(2,1)} %copy-done.1, bf16[64,3584]{1,0:T(8,128)(2,1)} %copy-done.8, ...), custom_call_target="tpu_custom_call" | custom-call | tf_op jit(solution)/shard_map/hidden/pallas_call | solution.py:147
  110.6 5.2 %collective-permute-done.17.refs_0_ = bf16[256,1792]{1,0:T(8,128)(2,1)S(1)} collective-permute-done((bf16[256,1792]{1,0:T(8,128)(2,1)}, bf16[256,1792]{1,0:T(8,128)(2,1)S(1)}, u32[]{:S(2)}, u32[]{:S(2)}) %collective-permute-start.17) | collective-permute-done | bytes 917536 | tf_op jit(solution)/shard_map/ppermute | solution.py:31
  117.0 2.5 %collective-permute-done.18.mat_d = bf16[256,1792]{1,0:T(8,128)(2,1)} collective-permute-done((bf16[256,1792]{1,0:T(8,128)(2,1)}, bf16[256,1792]{1,0:T(8,128)(2,1)}, u32[]{:S(2)}, u32[]{:S(2)}) %collective-permute-start.18) | collective-permute-done | bytes 917536 | tf_op jit(solution)/shard_map/ppermute | solution.py:31
  119.5 5.5 %down.2 = (bf16[64,1792]{1,0:T(8,128)(2,1)}, bf16[64,1792]{1,0:T(8,128)(2,1)}, bf16[64,1792]{1,0:T(8,128)(2,1)}, bf16[64,1792]{1,0:T(8,128)(2,1)}, bf16[64,1792]...) custom-call(bf16[512,1024]{1,0:T(8,128)(2,1)} %hidden.1.refs_1_.units, ...), custom_call_target="tpu_custom_call" | custom-call | tf_op jit(solution)/shard_map/down/pallas_call | solution.py:171
  125.0 3.5 %collective-permute-start.19 = (bf16[64,1792]{1,0:T(8,128)(2,1)}, bf16[64,1792]{1,0:T(8,128)(2,1)S(1)}, u32[]{:S(2)}, u32[]{:S(2)}) collective-permute-start(bf16[64,1792]{1,0:T(8,128)(2,1)} %get-tuple-element.46), channel_id=1, source_target_pairs={{0,30},{1,31},{2,28},{3,29},{4,26},{5,27},{6,24},{7,25},{8,6},{9,7... | collective-permute-start | bytes 688136 | tf_op jit(solution)/shard_map/ppermute | solution.py:31
  129.2 1.3 collective-permute-start.21
  130.5 3.0 %collective-permute-start.22 = (bf16[64,1792]{1,0:T(8,128)(2,1)}, bf16[64,1792]{1,0:T(8,128)(2,1)S(1)}, u32[]{:S(2)}, u32[]{:S(2)}) collective-permute-start(bf16[64,1792]{1,0:T(8,128)(2,1)} %get-tuple-element.49), channel_id=1, source_target_pairs={{0,6},{1,7},{2,4},{3,5},{4,2},{5,3},{6,0},{7,1},{8,14},{9,15},{10,... | collective-permute-start | bytes 688136 | tf_op jit(solution)/shard_map/ppermute | solution.py:31
  133.5 6.2 %collective-permute-done.16.refs_0_ = bf16[256,1792]{1,0:T(8,128)(2,1)S(1)} collective-permute-done((bf16[256,1792]{1,0:T(8,128)(2,1)}, bf16[256,1792]{1,0:T(8,128)(2,1)S(1)}, u32[]{:S(2)}, u32[]{:S(2)}) %collective-permute-start.16) | collective-permute-done | bytes 917536 | tf_op jit(solution)/shard_map/ppermute | solution.py:31
  140.0 3.7 %collective-permute-done.21.refs_3_.refs_6_ = bf16[64,1792]{1,0:T(8,128)(2,1)S(1)} collective-permute-done((bf16[64,1792]{1,0:T(8,128)(2,1)}, bf16[64,1792]{1,0:T(8,128)(2,1)S(1)}, u32[]{:S(2)}, u32[]{:S(2)}) %collective-permute-start.21) | collective-permute-done | bytes 229408 | tf_op jit(solution)/shard_map/ppermute | solution.py:31
  143.8 1.1 collective-permute-done.22.refs_4_.refs_8_
  145.6 2.7 %collective-permute-done.23.mat_d = bf16[256,1792]{1,0:T(8,128)(2,1)S(1)} collective-permute-done((bf16[256,1792]{1,0:T(8,128)(2,1)}, bf16[256,1792]{1,0:T(8,128)(2,1)S(1)}, u32[]{:S(2)}, u32[]{:S(2)}) %collective-permute-start.23) | collective-permute-done | bytes 917536 | tf_op jit(solution)/shard_map/ppermute | solution.py:31
  149.2 5.3 %down.3 = (bf16[64,1792]{1,0:T(8,128)(2,1)}, bf16[64,1792]{1,0:T(8,128)(2,1)}, bf16[64,1792]{1,0:T(8,128)(2,1)}, bf16[64,1792]{1,0:T(8,128)(2,1)}, bf16[64,1792]...) custom-call(bf16[512,1024]{1,0:T(8,128)(2,1)} %hidden.1.refs_1_.units, ...), custom_call_target="tpu_custom_call" | custom-call | tf_op jit(solution)/shard_map/down/pallas_call | solution.py:171
  154.5 3.8 %collective-permute-start.26 = (bf16[64,1792]{1,0:T(8,128)(2,1)}, bf16[64,1792]{1,0:T(8,128)(2,1)S(1)}, u32[]{:S(2)}, u32[]{:S(2)}) collective-permute-start(bf16[64,1792]{1,0:T(8,128)(2,1)} %get-tuple-element.54), channel_id=1, source_target_pairs={{0,22},{1,23},{2,20},{3,21},{4,18},{5,19},{6,16},{7,17},{8,30},{9,... | collective-permute-start | bytes 688136 | tf_op jit(solution)/shard_map/ppermute | solution.py:31
  158.3 2.0 %collective-permute-start.25 = (bf16[64,1792]{1,0:T(8,128)(2,1)}, bf16[64,1792]{1,0:T(8,128)(2,1)S(1)}, u32[]{:S(2)}, u32[]{:S(2)}) collective-permute-start(bf16[64,1792]{1,0:T(8,128)(2,1)} %get-tuple-element.52), channel_id=1, source_target_pairs={{0,16},{1,17},{2,18},{3,19},{4,20},{5,21},{6,22},{7,23},{8,24},{9,... | collective-permute-start | bytes 688136 | tf_op jit(solution)/shard_map/ppermute | solution.py:31
  160.4 1.4 collective-permute-start.31
  162.4 1.8 collective-permute-start.33
  164.2 2.8 %collective-permute-done.26.refs_1_.refs_10_ = bf16[64,1792]{1,0:T(8,128)(2,1)S(1)} collective-permute-done((bf16[64,1792]{1,0:T(8,128)(2,1)}, bf16[64,1792]{1,0:T(8,128)(2,1)S(1)}, u32[]{:S(2)}, u32[]{:S(2)}) %collective-permute-start.26) | collective-permute-done | bytes 229408 | tf_op jit(solution)/shard_map/ppermute | solution.py:31
  167.0 2.2 %collective-permute-start.24 = (bf16[64,1792]{1,0:T(8,128)(2,1)}, bf16[64,1792]{1,0:T(8,128)(2,1)S(1)}, u32[]{:S(2)}, u32[]{:S(2)}) collective-permute-start(bf16[64,1792]{1,0:T(8,128)(2,1)} %get-tuple-element.51), channel_id=1, source_target_pairs={{0,24},{1,25},{2,26},{3,27},{4,28},{5,29},{6,30},{7,31},{8,0},{9,1... | collective-permute-start | bytes 688136 | tf_op jit(solution)/shard_map/ppermute | solution.py:31
  169.2 2.8 %collective-permute-done.25.refs_1_.refs_6_ = bf16[64,1792]{1,0:T(8,128)(2,1)S(1)} collective-permute-done((bf16[64,1792]{1,0:T(8,128)(2,1)}, bf16[64,1792]{1,0:T(8,128)(2,1)S(1)}, u32[]{:S(2)}, u32[]{:S(2)}) %collective-permute-start.25) | collective-permute-done | bytes 229408 | tf_op jit(solution)/shard_map/ppermute | solution.py:31
  172.0 2.1 %collective-permute-start.29 = (bf16[64,1792]{1,0:T(8,128)(2,1)S(1)}, bf16[64,1792]{1,0:T(8,128)(2,1)S(1)}, u32[]{:S(2)}, u32[]{:S(2)}) collective-permute-start(bf16[64,1792]{1,0:T(8,128)(2,1)S(1)} %copy-done.31), channel_id=1, source_target_pairs={{0,30},{1,31},{2,28},{3,29},{4,26},{5,27},{6,24},{7,25},{8,6},{9,7... | collective-permute-start | bytes 688136 | tf_op jit(solution)/shard_map/ppermute | solution.py:31
  174.1 1.6 collective-permute-done.31.refs_5_
  175.7 1.0 collective-permute-start.30
  177.2 3.8 %collective-permute-done.33.refs_10_ = bf16[64,1792]{1,0:T(8,128)(2,1)S(1)} collective-permute-done((bf16[64,1792]{1,0:T(8,128)(2,1)}, bf16[64,1792]{1,0:T(8,128)(2,1)S(1)}, u32[]{:S(2)}, u32[]{:S(2)}) %collective-permute-start.33) | collective-permute-done | bytes 229408 | tf_op jit(solution)/shard_map/ppermute | solution.py:31
  181.0 2.9 %collective-permute-start.28 = (bf16[64,1792]{1,0:T(8,128)(2,1)}, bf16[64,1792]{1,0:T(8,128)(2,1)S(1)}, u32[]{:S(2)}, u32[]{:S(2)}) collective-permute-start(bf16[64,1792]{1,0:T(8,128)(2,1)} %after.25), channel_id=1, source_target_pairs={{0,6},{1,7},{2,4},{3,5},{4,2},{5,3},{6,0},{7,1},{8,14},{9,15},{10,... | collective-permute-start | bytes 688136 | tf_op jit(solution)/shard_map/ppermute | solution.py:31
  183.9 3.3 %finish.2 = (bf16[96,3584]{1,0:T(8,128)(2,1)}, bf16[96,3584]{1,0:T(8,128)(2,1)}) custom-call(bf16[96,3584]{1,0:T(8,128)(2,1)} %get-tuple-element.34.refs_0_, bf16[96,3584]{1,0:T(8,128)(2,1)} %get-tuple-element.35.refs_1_, f32[96,256]{1,0:T(8,128)} %get-tuple-element.36.refs_2_, f32[96,256]{1,0:T(8,128)} %get-tuple-element.37.refs_3_, ...), custom_call_target="tpu_custom_call" | custom-call | flops 528482304 | bytes 2752512 | tf_op jit(solution)/shard_map/finish/pallas_call | solution.py:206
  187.2 3.9 %collective-permute-done.29.refs_9_ = bf16[64,1792]{1,0:T(8,128)(2,1)S(1)} collective-permute-done((bf16[64,1792]{1,0:T(8,128)(2,1)S(1)}, bf16[64,1792]{1,0:T(8,128)(2,1)S(1)}, u32[]{:S(2)}, u32[]{:S(2)}) %collective-permute-start.29) | collective-permute-done | bytes 229408 | tf_op jit(solution)/shard_map/ppermute | solution.py:31
  191.1 4.6 %collective-permute-done.28.refs_8_ = bf16[64,1792]{1,0:T(8,128)(2,1)S(1)} collective-permute-done((bf16[64,1792]{1,0:T(8,128)(2,1)}, bf16[64,1792]{1,0:T(8,128)(2,1)S(1)}, u32[]{:S(2)}, u32[]{:S(2)}) %collective-permute-start.28) | collective-permute-done | bytes 229408 | tf_op jit(solution)/shard_map/ppermute | solution.py:31
  196.4 3.3 %finish.3 = (bf16[96,3584]{1,0:T(8,128)(2,1)}, bf16[96,3584]{1,0:T(8,128)(2,1)}) custom-call(bf16[96,3584]{1,0:T(8,128)(2,1)} %get-tuple-element.34.refs_0_, bf16[96,3584]{1,0:T(8,128)(2,1)} %get-tuple-element.35.refs_1_, f32[96,256]{1,0:T(8,128)} %get-tuple-element.36.refs_2_, ...), custom_call_target="tpu_custom_call", output_to_operand_aliasing={{0}: (12, {}), {1}: (13, {})} | custom-call | flops 528482304 | bytes 2752512 | tf_op jit(solution)/shard_map/finish/pallas_call | solution.py:206
  (105 shorter events, 14.9 us)
Async XLA Ops:
  0.6 26.1 %collective-permute-start.2 = (bf16[3584,256]{1,0:T(8,128)(2,1)}, bf16[3584,256]{1,0:T(8,128)(2,1)S(1)}, u32[]{:S(2)}, u32[]{:S(2)}) collective-permute-start(bf16[3584,256]{1,0:T(8,128)(2,1)} %bitcast.20), channel_id=1, source_target_pairs={{0,1},{1,0},{2,3},{3,2},{4,5},{5,4},{6,7},{7,6},{8,9},{9,8},{10,11... | collective-permute-start | bytes 5505032 | tf_op jit(solution)/shard_map/ppermute | solution.py:31
  0.7 26.0 %collective-permute-start.3 = (bf16[3584,256]{1,0:T(8,128)(2,1)}, bf16[3584,256]{1,0:T(8,128)(2,1)S(1)}, u32[]{:S(2)}, u32[]{:S(2)}) collective-permute-start(bf16[3584,256]{1,0:T(8,128)(2,1)} %bitcast.23), channel_id=1, source_target_pairs={{0,1},{1,0},{2,3},{3,2},{4,5},{5,4},{6,7},{7,6},{8,9},{9,8},{10,11... | collective-permute-start | bytes 5505032 | tf_op jit(solution)/shard_map/ppermute | solution.py:31
  1.2 20.3 %collective-permute-start = (bf16[96,3584]{1,0:T(8,128)(2,1)}, bf16[96,3584]{1,0:T(8,128)(2,1)S(1)}, u32[]{:S(2)}, u32[]{:S(2)}) collective-permute-start(bf16[96,3584]{1,0:T(8,128)(2,1)} %bitcast.31), channel_id=1, source_target_pairs={{0,32},{32,64},{64,96},{96,128},{128,160},{160,192},{192,224},{1,3... | collective-permute-start | bytes 2064392 | tf_op jit(solution)/shard_map/ppermute | solution.py:43
  6.3 20.5 %collective-permute-start.1 = (bf16[96,3584]{1,0:T(8,128)(2,1)}, bf16[96,3584]{1,0:T(8,128)(2,1)S(1)}, u32[]{:S(2)}, u32[]{:S(2)}) collective-permute-start(bf16[96,3584]{1,0:T(8,128)(2,1)} %bitcast.32), channel_id=1, source_target_pairs={{32,0},{64,32},{96,64},{128,96},{160,128},{192,160},{224,192},{33,... | collective-permute-start | bytes 2064392 | tf_op jit(solution)/shard_map/ppermute | solution.py:43
  8.2 60.2 %collective-permute-start.11 = (bf16[3584,256]{1,0:T(8,128)(2,1)}, bf16[3584,256]{1,0:T(8,128)(2,1)}, u32[]{:S(2)}, u32[]{:S(2)}) collective-permute-start(bf16[3584,256]{1,0:T(8,128)(2,1)} %bitcast.21), channel_id=1, source_target_pairs={{0,2},{1,3},{2,0},{3,1},{4,6},{5,7},{6,4},{7,5},{8,10},{9,11},{10,... | collective-permute-start | bytes 5505032 | tf_op jit(solution)/shard_map/ppermute | solution.py:31
  21.5 5.2 %copy-start.19 = (bf16[96,3584]{1,0:T(8,128)(2,1)}, bf16[96,3584]{1,0:T(8,128)(2,1)S(1)}, u32[]{:S(2)}) copy-start(bf16[96,3584]{1,0:T(8,128)(2,1)S(1)} %collective-permute-done.recv_up) | copy-start | bytes 2064388
  21.5 68.9 %collective-permute-start.13 = (bf16[3584,256]{1,0:T(8,128)(2,1)}, bf16[3584,256]{1,0:T(8,128)(2,1)}, u32[]{:S(2)}, u32[]{:S(2)}) collective-permute-start(bf16[3584,256]{1,0:T(8,128)(2,1)} %bitcast.24), channel_id=1, source_target_pairs={{0,2},{1,3},{2,0},{3,1},{4,6},{5,7},{6,4},{7,5},{8,10},{9,11},{10,... | collective-permute-start | bytes 5505032 | tf_op jit(solution)/shard_map/ppermute | solution.py:31
  34.5 12.9 %collective-permute-start.4 = (bf16[64,3584]{1,0:T(8,128)(2,1)}, bf16[64,3584]{1,0:T(8,128)(2,1)S(1)}, u32[]{:S(2)}, u32[]{:S(2)}) collective-permute-start(bf16[64,3584]{1,0:T(8,128)(2,1)} %get-tuple-element.39), channel_id=1, source_target_pairs={{0,8},{1,9},{2,10},{3,11},{4,12},{5,13},{6,14},{7,15},{8,16},{9,17... | collective-permute-start | bytes 1376264 | tf_op jit(solution)/shard_map/ppermute | solution.py:31
  36.1 13.9 %collective-permute-start.6 = (bf16[64,3584]{1,0:T(8,128)(2,1)}, bf16[64,3584]{1,0:T(8,128)(2,1)S(1)}, u32[]{:S(2)}, u32[]{:S(2)}) collective-permute-start(bf16[64,3584]{1,0:T(8,128)(2,1)} %get-tuple-element.41), channel_id=1, source_target_pairs={{0,24},{1,25},{2,26},{3,27},{4,28},{5,29},{6,30},{7,31},{8,0},{9,1... | collective-permute-start | bytes 1376264 | tf_op jit(solution)/shard_map/ppermute | solution.py:31
  37.8 16.0 %collective-permute-start.7 = (bf16[64,3584]{1,0:T(8,128)(2,1)}, bf16[64,3584]{1,0:T(8,128)(2,1)S(1)}, u32[]{:S(2)}, u32[]{:S(2)}) collective-permute-start(bf16[64,3584]{1,0:T(8,128)(2,1)} %get-tuple-element.42), channel_id=1, source_target_pairs={{0,6},{1,7},{2,4},{3,5},{4,2},{5,3},{6,0},{7,1},{8,14},{9,15},{10,... | collective-permute-start | bytes 1376264 | tf_op jit(solution)/shard_map/ppermute | solution.py:31
  48.1 15.2 %collective-permute-start.5 = (bf16[64,3584]{1,0:T(8,128)(2,1)}, bf16[64,3584]{1,0:T(8,128)(2,1)S(1)}, u32[]{:S(2)}, u32[]{:S(2)}) collective-permute-start(bf16[64,3584]{1,0:T(8,128)(2,1)} %after.14), channel_id=1, source_target_pairs={{0,16},{1,17},{2,18},{3,19},{4,20},{5,21},{6,22},{7,23},{8,24},{9,... | collective-permute-start | bytes 1376264 | tf_op jit(solution)/shard_map/ppermute | solution.py:31
  50.7 38.0 %collective-permute-start.8 = (bf16[64,3584]{1,0:T(8,128)(2,1)}, bf16[64,3584]{1,0:T(8,128)(2,1)S(1)}, u32[]{:S(2)}, u32[]{:S(2)}) collective-permute-start(bf16[64,3584]{1,0:T(8,128)(2,1)} %after.15), channel_id=1, source_target_pairs={{0,14},{1,15},{2,12},{3,13},{4,10},{5,11},{6,8},{7,9},{8,22},{9,23... | collective-permute-start | bytes 1376264 | tf_op jit(solution)/shard_map/ppermute | solution.py:31
  54.6 34.2 %collective-permute-start.10 = (bf16[64,3584]{1,0:T(8,128)(2,1)}, bf16[64,3584]{1,0:T(8,128)(2,1)S(1)}, u32[]{:S(2)}, u32[]{:S(2)}) collective-permute-start(bf16[64,3584]{1,0:T(8,128)(2,1)} %after.17), channel_id=1, source_target_pairs={{0,30},{1,31},{2,28},{3,29},{4,26},{5,27},{6,24},{7,25},{8,6},{9,7... | collective-permute-start | bytes 1376264 | tf_op jit(solution)/shard_map/ppermute | solution.py:31
  64.1 24.6 %collective-permute-start.9 = (bf16[64,3584]{1,0:T(8,128)(2,1)}, bf16[64,3584]{1,0:T(8,128)(2,1)S(1)}, u32[]{:S(2)}, u32[]{:S(2)}) collective-permute-start(bf16[64,3584]{1,0:T(8,128)(2,1)} %after.16), channel_id=1, source_target_pairs={{0,22},{1,23},{2,20},{3,21},{4,18},{5,19},{6,16},{7,17},{8,30},{9,... | collective-permute-start | bytes 1376264 | tf_op jit(solution)/shard_map/ppermute | solution.py:31
  90.5 4.1 %collective-permute-start.12 = (bf16[3584,256]{1,0:T(8,128)(2,1)}, bf16[3584,256]{1,0:T(8,128)(2,1)}, u32[]{:S(2)}, u32[]{:S(2)}) collective-permute-start(bf16[3584,256]{1,0:T(8,128)(2,1)} %after.18.refs_10_), channel_id=1, source_target_pairs={{0,1},{1,0},{2,3},{3,2},{4,5},{5,4},{6,7},{7,6},{8,9},{9,8},{10,11... | collective-permute-start | bytes 5505032 | tf_op jit(solution)/shard_map/ppermute | solution.py:31
  90.5 6.7 %collective-permute-start.14 = (bf16[3584,256]{1,0:T(8,128)(2,1)}, bf16[3584,256]{1,0:T(8,128)(2,1)}, u32[]{:S(2)}, u32[]{:S(2)}) collective-permute-start(bf16[3584,256]{1,0:T(8,128)(2,1)} %after.19.refs_14_), channel_id=1, source_target_pairs={{0,1},{1,0},{2,3},{3,2},{4,5},{5,4},{6,7},{7,6},{8,9},{9,8},{10,11... | collective-permute-start | bytes 5505032 | tf_op jit(solution)/shard_map/ppermute | solution.py:31
  93.3 22.4 %collective-permute-start.17 = (bf16[256,1792]{1,0:T(8,128)(2,1)}, bf16[256,1792]{1,0:T(8,128)(2,1)S(1)}, u32[]{:S(2)}, u32[]{:S(2)}) collective-permute-start(bf16[256,1792]{1,0:T(8,128)(2,1)} %after.21), channel_id=1, source_target_pairs={{0,2},{1,3},{2,0},{3,1},{4,6},{5,7},{6,4},{7,5},{8,10},{9,11},{10,... | collective-permute-start | bytes 2752520 | tf_op jit(solution)/shard_map/ppermute | solution.py:31
  93.5 23.5 %collective-permute-start.15 = (bf16[256,3584]{1,0:T(8,128)(2,1)S(1)}, bf16[256,3584]{1,0:T(8,128)(2,1)}, u32[]{:S(2)}, u32[]{:S(2)}) collective-permute-start(bf16[256,3584]{1,0:T(8,128)(2,1)S(1)} %bitcast.19), channel_id=1, source_target_pairs={{0,1},{1,0},{2,3},{3,2},{4,5},{5,4},{6,7},{7,6},{8,9},{9,8},{10,11... | collective-permute-start | bytes 5505032 | tf_op jit(solution)/shard_map/ppermute | solution.py:31
  116.7 2.8 %collective-permute-start.18 = (bf16[256,1792]{1,0:T(8,128)(2,1)}, bf16[256,1792]{1,0:T(8,128)(2,1)}, u32[]{:S(2)}, u32[]{:S(2)}) collective-permute-start(bf16[256,1792]{1,0:T(8,128)(2,1)} %after.22.mat_c), channel_id=1, source_target_pairs={{0,1},{1,0},{2,3},{3,2},{4,5},{5,4},{6,7},{7,6},{8,9},{9,8},{10,11... | collective-permute-start | bytes 2752520 | tf_op jit(solution)/shard_map/ppermute | solution.py:31
  116.7 23.0 %collective-permute-start.16 = (bf16[256,1792]{1,0:T(8,128)(2,1)}, bf16[256,1792]{1,0:T(8,128)(2,1)S(1)}, u32[]{:S(2)}, u32[]{:S(2)}) collective-permute-start(bf16[256,1792]{1,0:T(8,128)(2,1)} %after.20), channel_id=1, source_target_pairs={{0,2},{1,3},{2,0},{3,1},{4,6},{5,7},{6,4},{7,5},{8,10},{9,11},{10,... | collective-permute-start | bytes 2752520 | tf_op jit(solution)/shard_map/ppermute | solution.py:31
  125.0 14.7 %collective-permute-start.19 = (bf16[64,1792]{1,0:T(8,128)(2,1)}, bf16[64,1792]{1,0:T(8,128)(2,1)S(1)}, u32[]{:S(2)}, u32[]{:S(2)}) collective-permute-start(bf16[64,1792]{1,0:T(8,128)(2,1)} %get-tuple-element.46), channel_id=1, source_target_pairs={{0,30},{1,31},{2,28},{3,29},{4,26},{5,27},{6,24},{7,25},{8,6},{9,7... | collective-permute-start | bytes 688136 | tf_op jit(solution)/shard_map/ppermute | solution.py:31
  128.5 11.5 %collective-permute-start.20 = (bf16[64,1792]{1,0:T(8,128)(2,1)}, bf16[64,1792]{1,0:T(8,128)(2,1)S(1)}, u32[]{:S(2)}, u32[]{:S(2)}) collective-permute-start(bf16[64,1792]{1,0:T(8,128)(2,1)} %get-tuple-element.47), channel_id=1, source_target_pairs={{0,14},{1,15},{2,12},{3,13},{4,10},{5,11},{6,8},{7,9},{8,22},{9,23... | collective-permute-start | bytes 688136 | tf_op jit(solution)/shard_map/ppermute | solution.py:31
  129.2 14.6 %collective-permute-start.21 = (bf16[64,1792]{1,0:T(8,128)(2,1)}, bf16[64,1792]{1,0:T(8,128)(2,1)S(1)}, u32[]{:S(2)}, u32[]{:S(2)}) collective-permute-start(bf16[64,1792]{1,0:T(8,128)(2,1)} %get-tuple-element.48), channel_id=1, source_target_pairs={{0,16},{1,17},{2,18},{3,19},{4,20},{5,21},{6,22},{7,23},{8,24},{9,... | collective-permute-start | bytes 688136 | tf_op jit(solution)/shard_map/ppermute | solution.py:31
  130.5 14.4 %collective-permute-start.22 = (bf16[64,1792]{1,0:T(8,128)(2,1)}, bf16[64,1792]{1,0:T(8,128)(2,1)S(1)}, u32[]{:S(2)}, u32[]{:S(2)}) collective-permute-start(bf16[64,1792]{1,0:T(8,128)(2,1)} %get-tuple-element.49), channel_id=1, source_target_pairs={{0,6},{1,7},{2,4},{3,5},{4,2},{5,3},{6,0},{7,1},{8,14},{9,15},{10,... | collective-permute-start | bytes 688136 | tf_op jit(solution)/shard_map/ppermute | solution.py:31
  139.7 5.2 %copy-start.11 = (bf16[256,1792]{1,0:T(8,128)(2,1)}, bf16[256,1792]{1,0:T(8,128)(2,1)S(1)}, u32[]{:S(2)}) copy-start(bf16[256,1792]{1,0:T(8,128)(2,1)S(1)} %collective-permute-done.16.refs_0_) | copy-start | bytes 2752516
  139.7 5.2 %copy-start.12 = (bf16[64,1792]{1,0:T(8,128)(2,1)}, bf16[64,1792]{1,0:T(8,128)(2,1)S(1)}, u32[]{:S(2)}) copy-start(bf16[64,1792]{1,0:T(8,128)(2,1)S(1)} %collective-permute-done.19.refs_1_.refs_9_) | copy-start | bytes 688132
  140.0 4.8 %copy-start.13 = (bf16[64,1792]{1,0:T(8,128)(2,1)}, bf16[64,1792]{1,0:T(8,128)(2,1)S(1)}, u32[]{:S(2)}) copy-start(bf16[64,1792]{1,0:T(8,128)(2,1)S(1)} %collective-permute-done.20.refs_2_.refs_1_.refs_11_) | copy-start | bytes 688132
  145.6 14.8 %copy-start.29 = (bf16[64,1792]{1,0:T(8,128)(2,1)S(1)}, bf16[64,1792]{1,0:T(8,128)(2,1)}, u32[]{:S(2)}) copy-start(bf16[64,1792]{1,0:T(8,128)(2,1)} %get-tuple-element.59) | copy-start | bytes 688132
  145.6 2.7 %collective-permute-start.23 = (bf16[256,1792]{1,0:T(8,128)(2,1)}, bf16[256,1792]{1,0:T(8,128)(2,1)S(1)}, u32[]{:S(2)}, u32[]{:S(2)}) collective-permute-start(bf16[256,1792]{1,0:T(8,128)(2,1)} %after.23.mat_c), channel_id=1, source_target_pairs={{0,1},{1,0},{2,3},{3,2},{4,5},{5,4},{6,7},{7,6},{8,9},{9,8},{10,11... | collective-permute-start | bytes 2752520 | tf_op jit(solution)/shard_map/ppermute | solution.py:31
  154.5 17.5 %copy-start.31 = (bf16[64,1792]{1,0:T(8,128)(2,1)S(1)}, bf16[64,1792]{1,0:T(8,128)(2,1)}, u32[]{:S(2)}) copy-start(bf16[64,1792]{1,0:T(8,128)(2,1)} %get-tuple-element.56) | copy-start | bytes 688132
  154.5 21.1 %copy-start.30 = (bf16[64,1792]{1,0:T(8,128)(2,1)S(1)}, bf16[64,1792]{1,0:T(8,128)(2,1)}, u32[]{:S(2)}) copy-start(bf16[64,1792]{1,0:T(8,128)(2,1)} %get-tuple-element.57) | copy-start | bytes 688132
  154.5 12.5 %collective-permute-start.26 = (bf16[64,1792]{1,0:T(8,128)(2,1)}, bf16[64,1792]{1,0:T(8,128)(2,1)S(1)}, u32[]{:S(2)}, u32[]{:S(2)}) collective-permute-start(bf16[64,1792]{1,0:T(8,128)(2,1)} %get-tuple-element.54), channel_id=1, source_target_pairs={{0,22},{1,23},{2,20},{3,21},{4,18},{5,19},{6,16},{7,17},{8,30},{9,... | collective-permute-start | bytes 688136 | tf_op jit(solution)/shard_map/ppermute | solution.py:31
  158.3 13.6 %collective-permute-start.25 = (bf16[64,1792]{1,0:T(8,128)(2,1)}, bf16[64,1792]{1,0:T(8,128)(2,1)S(1)}, u32[]{:S(2)}, u32[]{:S(2)}) collective-permute-start(bf16[64,1792]{1,0:T(8,128)(2,1)} %get-tuple-element.52), channel_id=1, source_target_pairs={{0,16},{1,17},{2,18},{3,19},{4,20},{5,21},{6,22},{7,23},{8,24},{9,... | collective-permute-start | bytes 688136 | tf_op jit(solution)/shard_map/ppermute | solution.py:31
  160.4 15.3 %collective-permute-start.31 = (bf16[64,1792]{1,0:T(8,128)(2,1)S(1)}, bf16[64,1792]{1,0:T(8,128)(2,1)S(1)}, u32[]{:S(2)}, u32[]{:S(2)}) collective-permute-start(bf16[64,1792]{1,0:T(8,128)(2,1)S(1)} %copy-done.29), channel_id=1, source_target_pairs={{0,24},{1,25},{2,26},{3,27},{4,28},{5,29},{6,30},{7,31},{8,0},{9,1... | collective-permute-start | bytes 688136 | tf_op jit(solution)/shard_map/ppermute | solution.py:31
  161.8 15.0 %collective-permute-start.32 = (bf16[64,1792]{1,0:T(8,128)(2,1)}, bf16[64,1792]{1,0:T(8,128)(2,1)S(1)}, u32[]{:S(2)}, u32[]{:S(2)}) collective-permute-start(bf16[64,1792]{1,0:T(8,128)(2,1)} %after.26), channel_id=1, source_target_pairs={{0,8},{1,9},{2,10},{3,11},{4,12},{5,13},{6,14},{7,15},{8,16},{9,17... | collective-permute-start | bytes 688136 | tf_op jit(solution)/shard_map/ppermute | solution.py:31
  162.4 18.5 %collective-permute-start.33 = (bf16[64,1792]{1,0:T(8,128)(2,1)}, bf16[64,1792]{1,0:T(8,128)(2,1)S(1)}, u32[]{:S(2)}, u32[]{:S(2)}) collective-permute-start(bf16[64,1792]{1,0:T(8,128)(2,1)} %after.27), channel_id=1, source_target_pairs={{0,22},{1,23},{2,20},{3,21},{4,18},{5,19},{6,16},{7,17},{8,30},{9,... | collective-permute-start | bytes 688136 | tf_op jit(solution)/shard_map/ppermute | solution.py:31
  167.0 20.2 %collective-permute-start.24 = (bf16[64,1792]{1,0:T(8,128)(2,1)}, bf16[64,1792]{1,0:T(8,128)(2,1)S(1)}, u32[]{:S(2)}, u32[]{:S(2)}) collective-permute-start(bf16[64,1792]{1,0:T(8,128)(2,1)} %get-tuple-element.51), channel_id=1, source_target_pairs={{0,24},{1,25},{2,26},{3,27},{4,28},{5,29},{6,30},{7,31},{8,0},{9,1... | collective-permute-start | bytes 688136 | tf_op jit(solution)/shard_map/ppermute | solution.py:31
  172.0 19.1 %collective-permute-start.29 = (bf16[64,1792]{1,0:T(8,128)(2,1)S(1)}, bf16[64,1792]{1,0:T(8,128)(2,1)S(1)}, u32[]{:S(2)}, u32[]{:S(2)}) collective-permute-start(bf16[64,1792]{1,0:T(8,128)(2,1)S(1)} %copy-done.31), channel_id=1, source_target_pairs={{0,30},{1,31},{2,28},{3,29},{4,26},{5,27},{6,24},{7,25},{8,6},{9,7... | collective-permute-start | bytes 688136 | tf_op jit(solution)/shard_map/ppermute | solution.py:31
  175.7 8.2 %copy-start.23 = (bf16[64,1792]{1,0:T(8,128)(2,1)}, bf16[64,1792]{1,0:T(8,128)(2,1)S(1)}, u32[]{:S(2)}) copy-start(bf16[64,1792]{1,0:T(8,128)(2,1)S(1)} %collective-permute-done.31.refs_5_) | copy-start | bytes 688132
  175.7 15.4 %collective-permute-start.30 = (bf16[64,1792]{1,0:T(8,128)(2,1)S(1)}, bf16[64,1792]{1,0:T(8,128)(2,1)S(1)}, u32[]{:S(2)}, u32[]{:S(2)}) collective-permute-start(bf16[64,1792]{1,0:T(8,128)(2,1)S(1)} %copy-done.30), channel_id=1, source_target_pairs={{0,14},{1,15},{2,12},{3,13},{4,10},{5,11},{6,8},{7,9},{8,22},{9,23... | collective-permute-start | bytes 688136 | tf_op jit(solution)/shard_map/ppermute | solution.py:31
  176.8 7.0 %copy-start.25 = (bf16[64,1792]{1,0:T(8,128)(2,1)}, bf16[64,1792]{1,0:T(8,128)(2,1)S(1)}, u32[]{:S(2)}) copy-start(bf16[64,1792]{1,0:T(8,128)(2,1)S(1)} %collective-permute-done.32.refs_7_) | copy-start | bytes 688132
  176.8 14.3 %collective-permute-start.27 = (bf16[64,1792]{1,0:T(8,128)(2,1)}, bf16[64,1792]{1,0:T(8,128)(2,1)S(1)}, u32[]{:S(2)}, u32[]{:S(2)}) collective-permute-start(bf16[64,1792]{1,0:T(8,128)(2,1)} %after.24), channel_id=1, source_target_pairs={{0,8},{1,9},{2,10},{3,11},{4,12},{5,13},{6,14},{7,15},{8,16},{9,17... | collective-permute-start | bytes 688136 | tf_op jit(solution)/shard_map/ppermute | solution.py:31
  181.0 2.9 %copy-start.26 = (bf16[64,1792]{1,0:T(8,128)(2,1)}, bf16[64,1792]{1,0:T(8,128)(2,1)S(1)}, u32[]{:S(2)}) copy-start(bf16[64,1792]{1,0:T(8,128)(2,1)S(1)} %collective-permute-done.33.refs_10_) | copy-start | bytes 688132
  181.0 14.7 %collective-permute-start.28 = (bf16[64,1792]{1,0:T(8,128)(2,1)}, bf16[64,1792]{1,0:T(8,128)(2,1)S(1)}, u32[]{:S(2)}, u32[]{:S(2)}) collective-permute-start(bf16[64,1792]{1,0:T(8,128)(2,1)} %after.25), channel_id=1, source_target_pairs={{0,6},{1,7},{2,4},{3,5},{4,2},{5,3},{6,0},{7,1},{8,14},{9,15},{10,... | collective-permute-start | bytes 688136 | tf_op jit(solution)/shard_map/ppermute | solution.py:31
  187.2 8.5 %copy-start.21 = (bf16[64,1792]{1,0:T(8,128)(2,1)}, bf16[64,1792]{1,0:T(8,128)(2,1)S(1)}, u32[]{:S(2)}) copy-start(bf16[64,1792]{1,0:T(8,128)(2,1)S(1)} %collective-permute-done.24.refs_5_) | copy-start | bytes 688132
  191.1 4.6 %copy-start.22 = (bf16[64,1792]{1,0:T(8,128)(2,1)}, bf16[64,1792]{1,0:T(8,128)(2,1)S(1)}, u32[]{:S(2)}) copy-start(bf16[64,1792]{1,0:T(8,128)(2,1)S(1)} %collective-permute-done.29.refs_9_) | copy-start | bytes 688132
  191.1 4.6 %copy-start.24 = (bf16[64,1792]{1,0:T(8,128)(2,1)}, bf16[64,1792]{1,0:T(8,128)(2,1)S(1)}, u32[]{:S(2)}) copy-start(bf16[64,1792]{1,0:T(8,128)(2,1)S(1)} %collective-permute-done.30.refs_11_) | copy-start | bytes 688132
  191.1 4.6 %copy-start.27 = (bf16[64,1792]{1,0:T(8,128)(2,1)}, bf16[64,1792]{1,0:T(8,128)(2,1)S(1)}, u32[]{:S(2)}) copy-start(bf16[64,1792]{1,0:T(8,128)(2,1)S(1)} %collective-permute-done.27.refs_7_) | copy-start | bytes 688132
  (18 other events, 20.1 us)

commit v4 on v3

--- a/solution.py
+++ b/solution.py
@@ -32,7 +32,7 @@
 
 
 BLOCKS = [(by_x, xor_y) for xor_y in (0, 3) for by_x in range(SIDE)]
-ORDER = [1, 3, 4, 2, 5, 7, 6]
+ORDER = [5, 7, 2, 4, 1, 3, 6]
 ORDER_LOW = [5, 7, 2, 4, 1, 3, 6]
 ORDER_HIGH = [6, 2, 5, 7, 1, 3, 4]
 

time: 200 us -> 202 us (1.010)
  starting transfers between devices: 56.2 us -> 61.4 us
  waiting for transfers between devices: 93.7 us -> 90 us
    ppermute x32, starting transfers between devices: 49.3 us -> 54.4 us  [moved(): return lax.ppermute(value, 'expert', pairs)]
    ppermute x32, waiting for transfers between devices: 78.4 us -> 74.7 us  [moved(): return lax.ppermute(value, 'expert', pairs)]
  transfers between devices with their start and end apart: 34 -> 34, of which waited for: 21 -> 22; matrix products, arithmetic and copies ran while one was open for 1% -> 1% of each run, Pallas kernels for 14% -> 14%
where the time goes in v4:
time: 202 us; the launch traced here: 201 us
  waiting for transfers between devices  90 us (45%)
  starting transfers between devices  61.4 us (30%)
  Pallas kernels  36.5 us (18%)
  local copies, waits for them, and re-layouts  12.5 us (6%)
    ppermute x32, waiting for transfers between devices, moved(): return lax.ppermute(value, 'expert', pairs)  74.7 us
    ppermute x32, starting transfers between devices, moved(): return lax.ppermute(value, 'expert', pairs)  54.4 us
    ppermute x2, waiting for transfers between devices, from_behind(): return lax.ppermute(value, axis, pairs)  15.3 us
    pallas_call x1, Pallas kernels, hidden(): pl.pallas_call(hidden_kernel, grid=(width // deep,), out_shape=jax.ShapeD...  13.4 us
    unnamed x64, local copies, waits for them, and re-layouts  11.2 us
    pallas_call x2, Pallas kernels, down(): pl.pallas_call(down_kernel, grid=(2,), out_shape=[jax.ShapeDtypeStruct((2...  10.8 us
    ppermute x2, starting transfers between devices, from_behind(): return lax.ppermute(value, axis, pairs)  6.94 us
    pallas_call x2, Pallas kernels, finish(): pl.pallas_call(functools.partial(finish_kernel, len(begun)), grid=(steps,...  6.64 us
  transfers between devices with their start and end apart: 34, of which 22 were waited for; matrix products, arithmetic and copies ran while one was open for 1% of the time, Pallas kernels for 14%

profile of v4, /device:TPU:96, one launch (start us, length us, event | category | flops | bytes accessed | tf_op | source)
XLA Modules:
  0.0 201.4 jit_solution(901105599603001750)
XLA Ops:
  1.2 5.0 %collective-permute-start = (bf16[96,3584]{1,0:T(8,128)(2,1)}, bf16[96,3584]{1,0:T(8,128)(2,1)S(1)}, u32[]{:S(2)}, u32[]{:S(2)}) collective-permute-start(bf16[96,3584]{1,0:T(8,128)(2,1)} %bitcast.31), channel_id=1, source_target_pairs={{0,32},{32,64},{64,96},{96,128},{128,160},{160,192},{192,224},{1,3... | collective-permute-start | bytes 2064392 | tf_op jit(solution)/shard_map/ppermute | solution.py:43
  6.3 1.9 collective-permute-start.1
  8.2 1.7 collective-permute-start.11
  9.9 11.7 %collective-permute-done.recv_up = bf16[96,3584]{1,0:T(8,128)(2,1)S(1)} collective-permute-done((bf16[96,3584]{1,0:T(8,128)(2,1)}, bf16[96,3584]{1,0:T(8,128)(2,1)S(1)}, u32[]{:S(2)}, u32[]{:S(2)}) %collective-permute-start) | collective-permute-done | bytes 688160 | tf_op jit(solution)/shard_map/ppermute | solution.py:43
  21.5 1.6 collective-permute-start.13
  23.1 3.6 %collective-permute-done.1.recv_down = bf16[96,3584]{1,0:T(8,128)(2,1)S(1)} collective-permute-done((bf16[96,3584]{1,0:T(8,128)(2,1)}, bf16[96,3584]{1,0:T(8,128)(2,1)S(1)}, u32[]{:S(2)}, u32[]{:S(2)}) %collective-permute-start.1) | collective-permute-done | bytes 688160 | tf_op jit(solution)/shard_map/ppermute | solution.py:43
  28.8 5.7 %prepare.1 = (bf16[64,3584]{1,0:T(8,128)(2,1)}, bf16[64,3584]{1,0:T(8,128)(2,1)}, bf16[64,3584]{1,0:T(8,128)(2,1)}, bf16[64,3584]{1,0:T(8,128)(2,1)}, bf16[64,35...) custom-call(bf16[96,3584]{1,0:T(8,128)(2,1)} %copy-done.19, ...), custom_call_target="tpu_custom_call" | custom-call | flops 352321536 | bytes 8257536 | tf_op jit(solution)/shard_map/prepare/pallas_call | solution.py:107
  34.6 4.0 %collective-permute-start.8 = (bf16[64,3584]{1,0:T(8,128)(2,1)}, bf16[64,3584]{1,0:T(8,128)(2,1)S(1)}, u32[]{:S(2)}, u32[]{:S(2)}) collective-permute-start(bf16[64,3584]{1,0:T(8,128)(2,1)} %get-tuple-element.44), channel_id=1, source_target_pairs={{0,14},{1,15},{2,12},{3,13},{4,10},{5,11},{6,8},{7,9},{8,22},{9,23... | collective-permute-start | bytes 1376264 | tf_op jit(solution)/shard_map/ppermute | solution.py:31
  38.6 1.4 collective-permute-start.4
  40.0 1.8 collective-permute-start.6
  41.8 13.9 %collective-permute-done.8.refs_1_.refs_5_ = bf16[64,3584]{1,0:T(8,128)(2,1)S(1)} collective-permute-done((bf16[64,3584]{1,0:T(8,128)(2,1)}, bf16[64,3584]{1,0:T(8,128)(2,1)S(1)}, u32[]{:S(2)}, u32[]{:S(2)}) %collective-permute-start.8) | collective-permute-done | bytes 458784 | tf_op jit(solution)/shard_map/ppermute | solution.py:31
  56.5 3.6 %collective-permute-start.9 = (bf16[64,3584]{1,0:T(8,128)(2,1)}, bf16[64,3584]{1,0:T(8,128)(2,1)S(1)}, u32[]{:S(2)}, u32[]{:S(2)}) collective-permute-start(bf16[64,3584]{1,0:T(8,128)(2,1)} %after.16), channel_id=1, source_target_pairs={{0,6},{1,7},{2,4},{3,5},{4,2},{5,3},{6,0},{7,1},{8,14},{9,15},{10,... | collective-permute-start | bytes 1376264 | tf_op jit(solution)/shard_map/ppermute | solution.py:31
  60.1 1.1 collective-permute-done.4.refs_1_.refs_7_
  61.9 1.4 collective-permute-start.5
  63.4 8.0 %collective-permute-done.6.refs_1_.refs_2_ = bf16[64,3584]{1,0:T(8,128)(2,1)S(1)} collective-permute-done((bf16[64,3584]{1,0:T(8,128)(2,1)}, bf16[64,3584]{1,0:T(8,128)(2,1)S(1)}, u32[]{:S(2)}, u32[]{:S(2)}) %collective-permute-start.6) | collective-permute-done | bytes 458784 | tf_op jit(solution)/shard_map/ppermute | solution.py:31
  73.5 5.8 %collective-permute-start.10 = (bf16[64,3584]{1,0:T(8,128)(2,1)}, bf16[64,3584]{1,0:T(8,128)(2,1)S(1)}, u32[]{:S(2)}, u32[]{:S(2)}) collective-permute-start(bf16[64,3584]{1,0:T(8,128)(2,1)} %after.17), channel_id=1, source_target_pairs={{0,22},{1,23},{2,20},{3,21},{4,18},{5,19},{6,16},{7,17},{8,30},{9,... | collective-permute-start | bytes 1376264 | tf_op jit(solution)/shard_map/ppermute | solution.py:31
  79.3 2.2 %collective-permute-done.5.refs_1_ = bf16[64,3584]{1,0:T(8,128)(2,1)S(1)} collective-permute-done((bf16[64,3584]{1,0:T(8,128)(2,1)}, bf16[64,3584]{1,0:T(8,128)(2,1)S(1)}, u32[]{:S(2)}, u32[]{:S(2)}) %collective-permute-start.5) | collective-permute-done | bytes 458784 | tf_op jit(solution)/shard_map/ppermute | solution.py:31
  81.5 9.6 %collective-permute-done.7.refs_3_.refs_1_ = bf16[64,3584]{1,0:T(8,128)(2,1)S(1)} collective-permute-done((bf16[64,3584]{1,0:T(8,128)(2,1)}, bf16[64,3584]{1,0:T(8,128)(2,1)S(1)}, u32[]{:S(2)}, u32[]{:S(2)}) %collective-permute-start.7) | collective-permute-done | bytes 458784 | tf_op jit(solution)/shard_map/ppermute | solution.py:31
  93.2 1.0 copy-done
  94.1 1.3 fusion
  95.8 0.9 collective-permute-done.12.refs_11_
  96.8 2.6 %collective-permute-done.14.refs_15_ = bf16[3584,256]{1,0:T(8,128)(2,1)} collective-permute-done((bf16[3584,256]{1,0:T(8,128)(2,1)}, bf16[3584,256]{1,0:T(8,128)(2,1)}, u32[]{:S(2)}, u32[]{:S(2)}) %collective-permute-start.14) | collective-permute-done | bytes 1835040 | tf_op jit(solution)/shard_map/ppermute | solution.py:31
  99.4 13.4 %hidden.1.refs_1_.units = bf16[512,1024]{1,0:T(8,128)(2,1)} custom-call(bf16[64,3584]{1,0:T(8,128)(2,1)} %get-tuple-element.38.refs_0_, bf16[64,3584]{1,0:T(8,128)(2,1)} %copy-done.8, bf16[64,3584]{1,0:T(8,128)(2,1)} %copy-done.1, bf16[64,3584]{1,0:T(8,128)(2,1)} %copy-done.7, bf16[64,3584]{1,0:T(8,128)(2,1)} %copy-done.6, bf16[64,3584]{1,0:T(8,128)(2,1)} %copy-done.4, ...), custom_call_target="tpu_custom_call" | custom-call | tf_op jit(solution)/shard_map/hidden/pallas_call | solution.py:147
  112.7 4.3 %collective-permute-done.17.refs_0_ = bf16[256,1792]{1,0:T(8,128)(2,1)S(1)} collective-permute-done((bf16[256,1792]{1,0:T(8,128)(2,1)}, bf16[256,1792]{1,0:T(8,128)(2,1)S(1)}, u32[]{:S(2)}, u32[]{:S(2)}) %collective-permute-start.17) | collective-permute-done | bytes 917536 | tf_op jit(solution)/shard_map/ppermute | solution.py:31
  118.4 2.5 %collective-permute-done.18.mat_d = bf16[256,1792]{1,0:T(8,128)(2,1)} collective-permute-done((bf16[256,1792]{1,0:T(8,128)(2,1)}, bf16[256,1792]{1,0:T(8,128)(2,1)}, u32[]{:S(2)}, u32[]{:S(2)}) %collective-permute-start.18) | collective-permute-done | bytes 917536 | tf_op jit(solution)/shard_map/ppermute | solution.py:31
  120.8 5.5 %down.2 = (bf16[64,1792]{1,0:T(8,128)(2,1)}, bf16[64,1792]{1,0:T(8,128)(2,1)}, bf16[64,1792]{1,0:T(8,128)(2,1)}, bf16[64,1792]{1,0:T(8,128)(2,1)}, bf16[64,1792]...) custom-call(bf16[512,1024]{1,0:T(8,128)(2,1)} %hidden.1.refs_1_.units, ...), custom_call_target="tpu_custom_call" | custom-call | tf_op jit(solution)/shard_map/down/pallas_call | solution.py:171
  126.3 3.8 %collective-permute-start.19 = (bf16[64,1792]{1,0:T(8,128)(2,1)}, bf16[64,1792]{1,0:T(8,128)(2,1)S(1)}, u32[]{:S(2)}, u32[]{:S(2)}) collective-permute-start(bf16[64,1792]{1,0:T(8,128)(2,1)} %get-tuple-element.46), channel_id=1, source_target_pairs={{0,30},{1,31},{2,28},{3,29},{4,26},{5,27},{6,24},{7,25},{8,6},{9,7... | collective-permute-start | bytes 688136 | tf_op jit(solution)/shard_map/ppermute | solution.py:31
  130.5 1.1 collective-permute-start.21
  131.7 2.5 %collective-permute-start.22 = (bf16[64,1792]{1,0:T(8,128)(2,1)}, bf16[64,1792]{1,0:T(8,128)(2,1)S(1)}, u32[]{:S(2)}, u32[]{:S(2)}) collective-permute-start(bf16[64,1792]{1,0:T(8,128)(2,1)} %get-tuple-element.49), channel_id=1, source_target_pairs={{0,6},{1,7},{2,4},{3,5},{4,2},{5,3},{6,0},{7,1},{8,14},{9,15},{10,... | collective-permute-start | bytes 688136 | tf_op jit(solution)/shard_map/ppermute | solution.py:31
  134.2 6.8 %collective-permute-done.16.refs_0_ = bf16[256,1792]{1,0:T(8,128)(2,1)S(1)} collective-permute-done((bf16[256,1792]{1,0:T(8,128)(2,1)}, bf16[256,1792]{1,0:T(8,128)(2,1)S(1)}, u32[]{:S(2)}, u32[]{:S(2)}) %collective-permute-start.16) | collective-permute-done | bytes 917536 | tf_op jit(solution)/shard_map/ppermute | solution.py:31
  141.8 3.9 %collective-permute-done.21.refs_3_.refs_6_ = bf16[64,1792]{1,0:T(8,128)(2,1)S(1)} collective-permute-done((bf16[64,1792]{1,0:T(8,128)(2,1)}, bf16[64,1792]{1,0:T(8,128)(2,1)S(1)}, u32[]{:S(2)}, u32[]{:S(2)}) %collective-permute-start.21) | collective-permute-done | bytes 229408 | tf_op jit(solution)/shard_map/ppermute | solution.py:31
  147.1 2.7 %collective-permute-done.23.mat_d = bf16[256,1792]{1,0:T(8,128)(2,1)S(1)} collective-permute-done((bf16[256,1792]{1,0:T(8,128)(2,1)}, bf16[256,1792]{1,0:T(8,128)(2,1)S(1)}, u32[]{:S(2)}, u32[]{:S(2)}) %collective-permute-start.23) | collective-permute-done | bytes 917536 | tf_op jit(solution)/shard_map/ppermute | solution.py:31
  150.7 5.3 %down.3 = (bf16[64,1792]{1,0:T(8,128)(2,1)}, bf16[64,1792]{1,0:T(8,128)(2,1)}, bf16[64,1792]{1,0:T(8,128)(2,1)}, bf16[64,1792]{1,0:T(8,128)(2,1)}, bf16[64,1792]...) custom-call(bf16[512,1024]{1,0:T(8,128)(2,1)} %hidden.1.refs_1_.units, ...), custom_call_target="tpu_custom_call" | custom-call | tf_op jit(solution)/shard_map/down/pallas_call | solution.py:171
  156.1 3.2 %collective-permute-start.26 = (bf16[64,1792]{1,0:T(8,128)(2,1)}, bf16[64,1792]{1,0:T(8,128)(2,1)S(1)}, u32[]{:S(2)}, u32[]{:S(2)}) collective-permute-start(bf16[64,1792]{1,0:T(8,128)(2,1)} %get-tuple-element.54), channel_id=1, source_target_pairs={{0,22},{1,23},{2,20},{3,21},{4,18},{5,19},{6,16},{7,17},{8,30},{9,... | collective-permute-start | bytes 688136 | tf_op jit(solution)/shard_map/ppermute | solution.py:31
  159.3 2.7 %collective-permute-start.25 = (bf16[64,1792]{1,0:T(8,128)(2,1)}, bf16[64,1792]{1,0:T(8,128)(2,1)S(1)}, u32[]{:S(2)}, u32[]{:S(2)}) collective-permute-start(bf16[64,1792]{1,0:T(8,128)(2,1)} %get-tuple-element.52), channel_id=1, source_target_pairs={{0,16},{1,17},{2,18},{3,19},{4,20},{5,21},{6,22},{7,23},{8,24},{9,... | collective-permute-start | bytes 688136 | tf_op jit(solution)/shard_map/ppermute | solution.py:31
  162.0 1.3 collective-permute-start.31
  164.0 2.7 %collective-permute-start.33 = (bf16[64,1792]{1,0:T(8,128)(2,1)}, bf16[64,1792]{1,0:T(8,128)(2,1)S(1)}, u32[]{:S(2)}, u32[]{:S(2)}) collective-permute-start(bf16[64,1792]{1,0:T(8,128)(2,1)} %after.27), channel_id=1, source_target_pairs={{0,22},{1,23},{2,20},{3,21},{4,18},{5,19},{6,16},{7,17},{8,30},{9,... | collective-permute-start | bytes 688136 | tf_op jit(solution)/shard_map/ppermute | solution.py:31
  166.7 1.7 collective-permute-done.26.refs_1_.refs_10_
  168.4 3.6 %collective-permute-start.24 = (bf16[64,1792]{1,0:T(8,128)(2,1)}, bf16[64,1792]{1,0:T(8,128)(2,1)S(1)}, u32[]{:S(2)}, u32[]{:S(2)}) collective-permute-start(bf16[64,1792]{1,0:T(8,128)(2,1)} %get-tuple-element.51), channel_id=1, source_target_pairs={{0,24},{1,25},{2,26},{3,27},{4,28},{5,29},{6,30},{7,31},{8,0},{9,1... | collective-permute-start | bytes 688136 | tf_op jit(solution)/shard_map/ppermute | solution.py:31
  172.0 1.6 collective-permute-done.25.refs_1_.refs_6_
  173.6 3.3 %collective-permute-start.29 = (bf16[64,1792]{1,0:T(8,128)(2,1)S(1)}, bf16[64,1792]{1,0:T(8,128)(2,1)S(1)}, u32[]{:S(2)}, u32[]{:S(2)}) collective-permute-start(bf16[64,1792]{1,0:T(8,128)(2,1)S(1)} %copy-done.31), channel_id=1, source_target_pairs={{0,30},{1,31},{2,28},{3,29},{4,26},{5,27},{6,24},{7,25},{8,6},{9,7... | collective-permute-start | bytes 688136 | tf_op jit(solution)/shard_map/ppermute | solution.py:31
  177.1 1.9 collective-permute-start.30
  179.5 2.9 %collective-permute-done.33.refs_10_ = bf16[64,1792]{1,0:T(8,128)(2,1)S(1)} collective-permute-done((bf16[64,1792]{1,0:T(8,128)(2,1)}, bf16[64,1792]{1,0:T(8,128)(2,1)S(1)}, u32[]{:S(2)}, u32[]{:S(2)}) %collective-permute-start.33) | collective-permute-done | bytes 229408 | tf_op jit(solution)/shard_map/ppermute | solution.py:31
  182.4 3.0 %collective-permute-start.28 = (bf16[64,1792]{1,0:T(8,128)(2,1)}, bf16[64,1792]{1,0:T(8,128)(2,1)S(1)}, u32[]{:S(2)}, u32[]{:S(2)}) collective-permute-start(bf16[64,1792]{1,0:T(8,128)(2,1)} %after.25), channel_id=1, source_target_pairs={{0,6},{1,7},{2,4},{3,5},{4,2},{5,3},{6,0},{7,1},{8,14},{9,15},{10,... | collective-permute-start | bytes 688136 | tf_op jit(solution)/shard_map/ppermute | solution.py:31
  185.4 3.3 %finish.2 = (bf16[96,3584]{1,0:T(8,128)(2,1)}, bf16[96,3584]{1,0:T(8,128)(2,1)}) custom-call(bf16[96,3584]{1,0:T(8,128)(2,1)} %get-tuple-element.34.refs_0_, bf16[96,3584]{1,0:T(8,128)(2,1)} %get-tuple-element.35.refs_1_, f32[96,256]{1,0:T(8,128)} %get-tuple-element.36.refs_2_, f32[96,256]{1,0:T(8,128)} %get-tuple-element.37.refs_3_, ...), custom_call_target="tpu_custom_call" | custom-call | flops 528482304 | bytes 2752512 | tf_op jit(solution)/shard_map/finish/pallas_call | solution.py:206
  188.8 4.4 %collective-permute-done.29.refs_9_ = bf16[64,1792]{1,0:T(8,128)(2,1)S(1)} collective-permute-done((bf16[64,1792]{1,0:T(8,128)(2,1)S(1)}, bf16[64,1792]{1,0:T(8,128)(2,1)S(1)}, u32[]{:S(2)}, u32[]{:S(2)}) %collective-permute-start.29) | collective-permute-done | bytes 229408 | tf_op jit(solution)/shard_map/ppermute | solution.py:31
  193.2 4.0 %collective-permute-done.28.refs_8_ = bf16[64,1792]{1,0:T(8,128)(2,1)S(1)} collective-permute-done((bf16[64,1792]{1,0:T(8,128)(2,1)}, bf16[64,1792]{1,0:T(8,128)(2,1)S(1)}, u32[]{:S(2)}, u32[]{:S(2)}) %collective-permute-start.28) | collective-permute-done | bytes 229408 | tf_op jit(solution)/shard_map/ppermute | solution.py:31
  197.9 3.3 %finish.3 = (bf16[96,3584]{1,0:T(8,128)(2,1)}, bf16[96,3584]{1,0:T(8,128)(2,1)}) custom-call(bf16[96,3584]{1,0:T(8,128)(2,1)} %get-tuple-element.34.refs_0_, bf16[96,3584]{1,0:T(8,128)(2,1)} %get-tuple-element.35.refs_1_, f32[96,256]{1,0:T(8,128)} %get-tuple-element.36.refs_2_, ...), custom_call_target="tpu_custom_call", output_to_operand_aliasing={{0}: (12, {}), {1}: (13, {})} | custom-call | flops 528482304 | bytes 2752512 | tf_op jit(solution)/shard_map/finish/pallas_call | solution.py:206
  (105 shorter events, 15.7 us)
Async XLA Ops:
  0.6 26.1 %collective-permute-start.2 = (bf16[3584,256]{1,0:T(8,128)(2,1)}, bf16[3584,256]{1,0:T(8,128)(2,1)S(1)}, u32[]{:S(2)}, u32[]{:S(2)}) collective-permute-start(bf16[3584,256]{1,0:T(8,128)(2,1)} %bitcast.20), channel_id=1, source_target_pairs={{0,1},{1,0},{2,3},{3,2},{4,5},{5,4},{6,7},{7,6},{8,9},{9,8},{10,11... | collective-permute-start | bytes 5505032 | tf_op jit(solution)/shard_map/ppermute | solution.py:31
  0.7 26.0 %collective-permute-start.3 = (bf16[3584,256]{1,0:T(8,128)(2,1)}, bf16[3584,256]{1,0:T(8,128)(2,1)S(1)}, u32[]{:S(2)}, u32[]{:S(2)}) collective-permute-start(bf16[3584,256]{1,0:T(8,128)(2,1)} %bitcast.23), channel_id=1, source_target_pairs={{0,1},{1,0},{2,3},{3,2},{4,5},{5,4},{6,7},{7,6},{8,9},{9,8},{10,11... | collective-permute-start | bytes 5505032 | tf_op jit(solution)/shard_map/ppermute | solution.py:31
  1.2 20.3 %collective-permute-start = (bf16[96,3584]{1,0:T(8,128)(2,1)}, bf16[96,3584]{1,0:T(8,128)(2,1)S(1)}, u32[]{:S(2)}, u32[]{:S(2)}) collective-permute-start(bf16[96,3584]{1,0:T(8,128)(2,1)} %bitcast.31), channel_id=1, source_target_pairs={{0,32},{32,64},{64,96},{96,128},{128,160},{160,192},{192,224},{1,3... | collective-permute-start | bytes 2064392 | tf_op jit(solution)/shard_map/ppermute | solution.py:43
  6.3 20.5 %collective-permute-start.1 = (bf16[96,3584]{1,0:T(8,128)(2,1)}, bf16[96,3584]{1,0:T(8,128)(2,1)S(1)}, u32[]{:S(2)}, u32[]{:S(2)}) collective-permute-start(bf16[96,3584]{1,0:T(8,128)(2,1)} %bitcast.32), channel_id=1, source_target_pairs={{32,0},{64,32},{96,64},{128,96},{160,128},{192,160},{224,192},{33,... | collective-permute-start | bytes 2064392 | tf_op jit(solution)/shard_map/ppermute | solution.py:43
  8.2 71.1 %collective-permute-start.11 = (bf16[3584,256]{1,0:T(8,128)(2,1)}, bf16[3584,256]{1,0:T(8,128)(2,1)}, u32[]{:S(2)}, u32[]{:S(2)}) collective-permute-start(bf16[3584,256]{1,0:T(8,128)(2,1)} %bitcast.21), channel_id=1, source_target_pairs={{0,2},{1,3},{2,0},{3,1},{4,6},{5,7},{6,4},{7,5},{8,10},{9,11},{10,... | collective-permute-start | bytes 5505032 | tf_op jit(solution)/shard_map/ppermute | solution.py:31
  21.5 5.2 %copy-start.19 = (bf16[96,3584]{1,0:T(8,128)(2,1)}, bf16[96,3584]{1,0:T(8,128)(2,1)S(1)}, u32[]{:S(2)}) copy-start(bf16[96,3584]{1,0:T(8,128)(2,1)S(1)} %collective-permute-done.recv_up) | copy-start | bytes 2064388
  21.5 71.1 %collective-permute-start.13 = (bf16[3584,256]{1,0:T(8,128)(2,1)}, bf16[3584,256]{1,0:T(8,128)(2,1)}, u32[]{:S(2)}, u32[]{:S(2)}) collective-permute-start(bf16[3584,256]{1,0:T(8,128)(2,1)} %bitcast.24), channel_id=1, source_target_pairs={{0,2},{1,3},{2,0},{3,1},{4,6},{5,7},{6,4},{7,5},{8,10},{9,11},{10,... | collective-permute-start | bytes 5505032 | tf_op jit(solution)/shard_map/ppermute | solution.py:31
  34.6 21.2 %collective-permute-start.8 = (bf16[64,3584]{1,0:T(8,128)(2,1)}, bf16[64,3584]{1,0:T(8,128)(2,1)S(1)}, u32[]{:S(2)}, u32[]{:S(2)}) collective-permute-start(bf16[64,3584]{1,0:T(8,128)(2,1)} %get-tuple-element.44), channel_id=1, source_target_pairs={{0,14},{1,15},{2,12},{3,13},{4,10},{5,11},{6,8},{7,9},{8,22},{9,23... | collective-permute-start | bytes 1376264 | tf_op jit(solution)/shard_map/ppermute | solution.py:31
  38.6 22.6 %collective-permute-start.4 = (bf16[64,3584]{1,0:T(8,128)(2,1)}, bf16[64,3584]{1,0:T(8,128)(2,1)S(1)}, u32[]{:S(2)}, u32[]{:S(2)}) collective-permute-start(bf16[64,3584]{1,0:T(8,128)(2,1)} %get-tuple-element.40), channel_id=1, source_target_pairs={{0,30},{1,31},{2,28},{3,29},{4,26},{5,27},{6,24},{7,25},{8,6},{9,7... | collective-permute-start | bytes 1376264 | tf_op jit(solution)/shard_map/ppermute | solution.py:31
  40.0 31.3 %collective-permute-start.6 = (bf16[64,3584]{1,0:T(8,128)(2,1)}, bf16[64,3584]{1,0:T(8,128)(2,1)S(1)}, u32[]{:S(2)}, u32[]{:S(2)}) collective-permute-start(bf16[64,3584]{1,0:T(8,128)(2,1)} %get-tuple-element.41), channel_id=1, source_target_pairs={{0,16},{1,17},{2,18},{3,19},{4,20},{5,21},{6,22},{7,23},{8,24},{9,... | collective-permute-start | bytes 1376264 | tf_op jit(solution)/shard_map/ppermute | solution.py:31
  56.5 16.2 %collective-permute-start.9 = (bf16[64,3584]{1,0:T(8,128)(2,1)}, bf16[64,3584]{1,0:T(8,128)(2,1)S(1)}, u32[]{:S(2)}, u32[]{:S(2)}) collective-permute-start(bf16[64,3584]{1,0:T(8,128)(2,1)} %after.16), channel_id=1, source_target_pairs={{0,6},{1,7},{2,4},{3,5},{4,2},{5,3},{6,0},{7,1},{8,14},{9,15},{10,... | collective-permute-start | bytes 1376264 | tf_op jit(solution)/shard_map/ppermute | solution.py:31
  61.9 19.5 %collective-permute-start.5 = (bf16[64,3584]{1,0:T(8,128)(2,1)}, bf16[64,3584]{1,0:T(8,128)(2,1)S(1)}, u32[]{:S(2)}, u32[]{:S(2)}) collective-permute-start(bf16[64,3584]{1,0:T(8,128)(2,1)} %after.14), channel_id=1, source_target_pairs={{0,8},{1,9},{2,10},{3,11},{4,12},{5,13},{6,14},{7,15},{8,16},{9,17... | collective-permute-start | bytes 1376264 | tf_op jit(solution)/shard_map/ppermute | solution.py:31
  72.1 19.0 %collective-permute-start.7 = (bf16[64,3584]{1,0:T(8,128)(2,1)}, bf16[64,3584]{1,0:T(8,128)(2,1)S(1)}, u32[]{:S(2)}, u32[]{:S(2)}) collective-permute-start(bf16[64,3584]{1,0:T(8,128)(2,1)} %after.15), channel_id=1, source_target_pairs={{0,24},{1,25},{2,26},{3,27},{4,28},{5,29},{6,30},{7,31},{8,0},{9,1... | collective-permute-start | bytes 1376264 | tf_op jit(solution)/shard_map/ppermute | solution.py:31
  73.5 17.6 %collective-permute-start.10 = (bf16[64,3584]{1,0:T(8,128)(2,1)}, bf16[64,3584]{1,0:T(8,128)(2,1)S(1)}, u32[]{:S(2)}, u32[]{:S(2)}) collective-permute-start(bf16[64,3584]{1,0:T(8,128)(2,1)} %after.17), channel_id=1, source_target_pairs={{0,22},{1,23},{2,20},{3,21},{4,18},{5,19},{6,16},{7,17},{8,30},{9,... | collective-permute-start | bytes 1376264 | tf_op jit(solution)/shard_map/ppermute | solution.py:31
  81.5 9.6 %copy-start.8 = (bf16[64,3584]{1,0:T(8,128)(2,1)}, bf16[64,3584]{1,0:T(8,128)(2,1)S(1)}, u32[]{:S(2)}) copy-start(bf16[64,3584]{1,0:T(8,128)(2,1)S(1)} %collective-permute-done.5.refs_1_) | copy-start | bytes 1376260
  92.6 4.1 %collective-permute-start.12 = (bf16[3584,256]{1,0:T(8,128)(2,1)}, bf16[3584,256]{1,0:T(8,128)(2,1)}, u32[]{:S(2)}, u32[]{:S(2)}) collective-permute-start(bf16[3584,256]{1,0:T(8,128)(2,1)} %after.18.refs_10_), channel_id=1, source_target_pairs={{0,1},{1,0},{2,3},{3,2},{4,5},{5,4},{6,7},{7,6},{8,9},{9,8},{10,11... | collective-permute-start | bytes 5505032 | tf_op jit(solution)/shard_map/ppermute | solution.py:31
  92.7 6.7 %collective-permute-start.14 = (bf16[3584,256]{1,0:T(8,128)(2,1)}, bf16[3584,256]{1,0:T(8,128)(2,1)}, u32[]{:S(2)}, u32[]{:S(2)}) collective-permute-start(bf16[3584,256]{1,0:T(8,128)(2,1)} %after.19.refs_14_), channel_id=1, source_target_pairs={{0,1},{1,0},{2,3},{3,2},{4,5},{5,4},{6,7},{7,6},{8,9},{9,8},{10,11... | collective-permute-start | bytes 5505032 | tf_op jit(solution)/shard_map/ppermute | solution.py:31
  95.5 21.6 %collective-permute-start.17 = (bf16[256,1792]{1,0:T(8,128)(2,1)}, bf16[256,1792]{1,0:T(8,128)(2,1)S(1)}, u32[]{:S(2)}, u32[]{:S(2)}) collective-permute-start(bf16[256,1792]{1,0:T(8,128)(2,1)} %after.21), channel_id=1, source_target_pairs={{0,2},{1,3},{2,0},{3,1},{4,6},{5,7},{6,4},{7,5},{8,10},{9,11},{10,... | collective-permute-start | bytes 2752520 | tf_op jit(solution)/shard_map/ppermute | solution.py:31
  95.8 22.5 %collective-permute-start.15 = (bf16[256,3584]{1,0:T(8,128)(2,1)S(1)}, bf16[256,3584]{1,0:T(8,128)(2,1)}, u32[]{:S(2)}, u32[]{:S(2)}) collective-permute-start(bf16[256,3584]{1,0:T(8,128)(2,1)S(1)} %bitcast.19), channel_id=1, source_target_pairs={{0,1},{1,0},{2,3},{3,2},{4,5},{5,4},{6,7},{7,6},{8,9},{9,8},{10,11... | collective-permute-start | bytes 5505032 | tf_op jit(solution)/shard_map/ppermute | solution.py:31
  118.0 2.8 %collective-permute-start.18 = (bf16[256,1792]{1,0:T(8,128)(2,1)}, bf16[256,1792]{1,0:T(8,128)(2,1)}, u32[]{:S(2)}, u32[]{:S(2)}) collective-permute-start(bf16[256,1792]{1,0:T(8,128)(2,1)} %after.22.mat_c), channel_id=1, source_target_pairs={{0,1},{1,0},{2,3},{3,2},{4,5},{5,4},{6,7},{7,6},{8,9},{9,8},{10,11... | collective-permute-start | bytes 2752520 | tf_op jit(solution)/shard_map/ppermute | solution.py:31
  118.0 23.0 %collective-permute-start.16 = (bf16[256,1792]{1,0:T(8,128)(2,1)}, bf16[256,1792]{1,0:T(8,128)(2,1)S(1)}, u32[]{:S(2)}, u32[]{:S(2)}) collective-permute-start(bf16[256,1792]{1,0:T(8,128)(2,1)} %after.20), channel_id=1, source_target_pairs={{0,2},{1,3},{2,0},{3,1},{4,6},{5,7},{6,4},{7,5},{8,10},{9,11},{10,... | collective-permute-start | bytes 2752520 | tf_op jit(solution)/shard_map/ppermute | solution.py:31
  126.3 15.5 %collective-permute-start.19 = (bf16[64,1792]{1,0:T(8,128)(2,1)}, bf16[64,1792]{1,0:T(8,128)(2,1)S(1)}, u32[]{:S(2)}, u32[]{:S(2)}) collective-permute-start(bf16[64,1792]{1,0:T(8,128)(2,1)} %get-tuple-element.46), channel_id=1, source_target_pairs={{0,30},{1,31},{2,28},{3,29},{4,26},{5,27},{6,24},{7,25},{8,6},{9,7... | collective-permute-start | bytes 688136 | tf_op jit(solution)/shard_map/ppermute | solution.py:31
  130.1 11.7 %collective-permute-start.20 = (bf16[64,1792]{1,0:T(8,128)(2,1)}, bf16[64,1792]{1,0:T(8,128)(2,1)S(1)}, u32[]{:S(2)}, u32[]{:S(2)}) collective-permute-start(bf16[64,1792]{1,0:T(8,128)(2,1)} %get-tuple-element.47), channel_id=1, source_target_pairs={{0,14},{1,15},{2,12},{3,13},{4,10},{5,11},{6,8},{7,9},{8,22},{9,23... | collective-permute-start | bytes 688136 | tf_op jit(solution)/shard_map/ppermute | solution.py:31
  130.5 15.2 %collective-permute-start.21 = (bf16[64,1792]{1,0:T(8,128)(2,1)}, bf16[64,1792]{1,0:T(8,128)(2,1)S(1)}, u32[]{:S(2)}, u32[]{:S(2)}) collective-permute-start(bf16[64,1792]{1,0:T(8,128)(2,1)} %get-tuple-element.48), channel_id=1, source_target_pairs={{0,16},{1,17},{2,18},{3,19},{4,20},{5,21},{6,22},{7,23},{8,24},{9,... | collective-permute-start | bytes 688136 | tf_op jit(solution)/shard_map/ppermute | solution.py:31
  131.7 14.5 %collective-permute-start.22 = (bf16[64,1792]{1,0:T(8,128)(2,1)}, bf16[64,1792]{1,0:T(8,128)(2,1)S(1)}, u32[]{:S(2)}, u32[]{:S(2)}) collective-permute-start(bf16[64,1792]{1,0:T(8,128)(2,1)} %get-tuple-element.49), channel_id=1, source_target_pairs={{0,6},{1,7},{2,4},{3,5},{4,2},{5,3},{6,0},{7,1},{8,14},{9,15},{10,... | collective-permute-start | bytes 688136 | tf_op jit(solution)/shard_map/ppermute | solution.py:31
  141.0 5.2 %copy-start.11 = (bf16[256,1792]{1,0:T(8,128)(2,1)}, bf16[256,1792]{1,0:T(8,128)(2,1)S(1)}, u32[]{:S(2)}) copy-start(bf16[256,1792]{1,0:T(8,128)(2,1)S(1)} %collective-permute-done.16.refs_0_) | copy-start | bytes 2752516
  141.8 4.4 %copy-start.12 = (bf16[64,1792]{1,0:T(8,128)(2,1)}, bf16[64,1792]{1,0:T(8,128)(2,1)S(1)}, u32[]{:S(2)}) copy-start(bf16[64,1792]{1,0:T(8,128)(2,1)S(1)} %collective-permute-done.19.refs_1_.refs_9_) | copy-start | bytes 688132
  141.8 4.4 %copy-start.13 = (bf16[64,1792]{1,0:T(8,128)(2,1)}, bf16[64,1792]{1,0:T(8,128)(2,1)S(1)}, u32[]{:S(2)}) copy-start(bf16[64,1792]{1,0:T(8,128)(2,1)S(1)} %collective-permute-done.20.refs_2_.refs_1_.refs_11_) | copy-start | bytes 688132
  147.1 14.9 %copy-start.29 = (bf16[64,1792]{1,0:T(8,128)(2,1)S(1)}, bf16[64,1792]{1,0:T(8,128)(2,1)}, u32[]{:S(2)}) copy-start(bf16[64,1792]{1,0:T(8,128)(2,1)} %get-tuple-element.59) | copy-start | bytes 688132
  147.1 2.7 %collective-permute-start.23 = (bf16[256,1792]{1,0:T(8,128)(2,1)}, bf16[256,1792]{1,0:T(8,128)(2,1)S(1)}, u32[]{:S(2)}, u32[]{:S(2)}) collective-permute-start(bf16[256,1792]{1,0:T(8,128)(2,1)} %after.23.mat_c), channel_id=1, source_target_pairs={{0,1},{1,0},{2,3},{3,2},{4,5},{5,4},{6,7},{7,6},{8,9},{9,8},{10,11... | collective-permute-start | bytes 2752520 | tf_op jit(solution)/shard_map/ppermute | solution.py:31
  156.0 17.6 %copy-start.31 = (bf16[64,1792]{1,0:T(8,128)(2,1)S(1)}, bf16[64,1792]{1,0:T(8,128)(2,1)}, u32[]{:S(2)}) copy-start(bf16[64,1792]{1,0:T(8,128)(2,1)} %get-tuple-element.56) | copy-start | bytes 688132
  156.0 21.1 %copy-start.30 = (bf16[64,1792]{1,0:T(8,128)(2,1)S(1)}, bf16[64,1792]{1,0:T(8,128)(2,1)}, u32[]{:S(2)}) copy-start(bf16[64,1792]{1,0:T(8,128)(2,1)} %get-tuple-element.57) | copy-start | bytes 688132
  156.1 12.4 %collective-permute-start.26 = (bf16[64,1792]{1,0:T(8,128)(2,1)}, bf16[64,1792]{1,0:T(8,128)(2,1)S(1)}, u32[]{:S(2)}, u32[]{:S(2)}) collective-permute-start(bf16[64,1792]{1,0:T(8,128)(2,1)} %get-tuple-element.54), channel_id=1, source_target_pairs={{0,22},{1,23},{2,20},{3,21},{4,18},{5,19},{6,16},{7,17},{8,30},{9,... | collective-permute-start | bytes 688136 | tf_op jit(solution)/shard_map/ppermute | solution.py:31
  159.3 14.3 %collective-permute-start.25 = (bf16[64,1792]{1,0:T(8,128)(2,1)}, bf16[64,1792]{1,0:T(8,128)(2,1)S(1)}, u32[]{:S(2)}, u32[]{:S(2)}) collective-permute-start(bf16[64,1792]{1,0:T(8,128)(2,1)} %get-tuple-element.52), channel_id=1, source_target_pairs={{0,16},{1,17},{2,18},{3,19},{4,20},{5,21},{6,22},{7,23},{8,24},{9,... | collective-permute-start | bytes 688136 | tf_op jit(solution)/shard_map/ppermute | solution.py:31
  162.0 15.1 %collective-permute-start.31 = (bf16[64,1792]{1,0:T(8,128)(2,1)S(1)}, bf16[64,1792]{1,0:T(8,128)(2,1)S(1)}, u32[]{:S(2)}, u32[]{:S(2)}) collective-permute-start(bf16[64,1792]{1,0:T(8,128)(2,1)S(1)} %copy-done.29), channel_id=1, source_target_pairs={{0,24},{1,25},{2,26},{3,27},{4,28},{5,29},{6,30},{7,31},{8,0},{9,1... | collective-permute-start | bytes 688136 | tf_op jit(solution)/shard_map/ppermute | solution.py:31
  163.3 15.7 %collective-permute-start.32 = (bf16[64,1792]{1,0:T(8,128)(2,1)}, bf16[64,1792]{1,0:T(8,128)(2,1)S(1)}, u32[]{:S(2)}, u32[]{:S(2)}) collective-permute-start(bf16[64,1792]{1,0:T(8,128)(2,1)} %after.26), channel_id=1, source_target_pairs={{0,8},{1,9},{2,10},{3,11},{4,12},{5,13},{6,14},{7,15},{8,16},{9,17... | collective-permute-start | bytes 688136 | tf_op jit(solution)/shard_map/ppermute | solution.py:31
  164.0 18.4 %collective-permute-start.33 = (bf16[64,1792]{1,0:T(8,128)(2,1)}, bf16[64,1792]{1,0:T(8,128)(2,1)S(1)}, u32[]{:S(2)}, u32[]{:S(2)}) collective-permute-start(bf16[64,1792]{1,0:T(8,128)(2,1)} %after.27), channel_id=1, source_target_pairs={{0,22},{1,23},{2,20},{3,21},{4,18},{5,19},{6,16},{7,17},{8,30},{9,... | collective-permute-start | bytes 688136 | tf_op jit(solution)/shard_map/ppermute | solution.py:31
  168.4 20.3 %collective-permute-start.24 = (bf16[64,1792]{1,0:T(8,128)(2,1)}, bf16[64,1792]{1,0:T(8,128)(2,1)S(1)}, u32[]{:S(2)}, u32[]{:S(2)}) collective-permute-start(bf16[64,1792]{1,0:T(8,128)(2,1)} %get-tuple-element.51), channel_id=1, source_target_pairs={{0,24},{1,25},{2,26},{3,27},{4,28},{5,29},{6,30},{7,31},{8,0},{9,1... | collective-permute-start | bytes 688136 | tf_op jit(solution)/shard_map/ppermute | solution.py:31
  173.6 19.6 %collective-permute-start.29 = (bf16[64,1792]{1,0:T(8,128)(2,1)S(1)}, bf16[64,1792]{1,0:T(8,128)(2,1)S(1)}, u32[]{:S(2)}, u32[]{:S(2)}) collective-permute-start(bf16[64,1792]{1,0:T(8,128)(2,1)S(1)} %copy-done.31), channel_id=1, source_target_pairs={{0,30},{1,31},{2,28},{3,29},{4,26},{5,27},{6,24},{7,25},{8,6},{9,7... | collective-permute-start | bytes 688136 | tf_op jit(solution)/shard_map/ppermute | solution.py:31
  177.1 8.3 %copy-start.23 = (bf16[64,1792]{1,0:T(8,128)(2,1)}, bf16[64,1792]{1,0:T(8,128)(2,1)S(1)}, u32[]{:S(2)}) copy-start(bf16[64,1792]{1,0:T(8,128)(2,1)S(1)} %collective-permute-done.31.refs_5_) | copy-start | bytes 688132
  177.1 16.0 %collective-permute-start.30 = (bf16[64,1792]{1,0:T(8,128)(2,1)S(1)}, bf16[64,1792]{1,0:T(8,128)(2,1)S(1)}, u32[]{:S(2)}, u32[]{:S(2)}) collective-permute-start(bf16[64,1792]{1,0:T(8,128)(2,1)S(1)} %copy-done.30), channel_id=1, source_target_pairs={{0,14},{1,15},{2,12},{3,13},{4,10},{5,11},{6,8},{7,9},{8,22},{9,23... | collective-permute-start | bytes 688136 | tf_op jit(solution)/shard_map/ppermute | solution.py:31
  179.0 6.4 %copy-start.25 = (bf16[64,1792]{1,0:T(8,128)(2,1)}, bf16[64,1792]{1,0:T(8,128)(2,1)S(1)}, u32[]{:S(2)}) copy-start(bf16[64,1792]{1,0:T(8,128)(2,1)S(1)} %collective-permute-done.32.refs_7_) | copy-start | bytes 688132
  179.0 14.1 %collective-permute-start.27 = (bf16[64,1792]{1,0:T(8,128)(2,1)}, bf16[64,1792]{1,0:T(8,128)(2,1)S(1)}, u32[]{:S(2)}, u32[]{:S(2)}) collective-permute-start(bf16[64,1792]{1,0:T(8,128)(2,1)} %after.24), channel_id=1, source_target_pairs={{0,8},{1,9},{2,10},{3,11},{4,12},{5,13},{6,14},{7,15},{8,16},{9,17... | collective-permute-start | bytes 688136 | tf_op jit(solution)/shard_map/ppermute | solution.py:31
  182.4 14.8 %collective-permute-start.28 = (bf16[64,1792]{1,0:T(8,128)(2,1)}, bf16[64,1792]{1,0:T(8,128)(2,1)S(1)}, u32[]{:S(2)}, u32[]{:S(2)}) collective-permute-start(bf16[64,1792]{1,0:T(8,128)(2,1)} %after.25), channel_id=1, source_target_pairs={{0,6},{1,7},{2,4},{3,5},{4,2},{5,3},{6,0},{7,1},{8,14},{9,15},{10,... | collective-permute-start | bytes 688136 | tf_op jit(solution)/shard_map/ppermute | solution.py:31
  188.7 8.5 %copy-start.21 = (bf16[64,1792]{1,0:T(8,128)(2,1)}, bf16[64,1792]{1,0:T(8,128)(2,1)S(1)}, u32[]{:S(2)}) copy-start(bf16[64,1792]{1,0:T(8,128)(2,1)S(1)} %collective-permute-done.24.refs_5_) | copy-start | bytes 688132
  193.2 4.1 %copy-start.22 = (bf16[64,1792]{1,0:T(8,128)(2,1)}, bf16[64,1792]{1,0:T(8,128)(2,1)S(1)}, u32[]{:S(2)}) copy-start(bf16[64,1792]{1,0:T(8,128)(2,1)S(1)} %collective-permute-done.29.refs_9_) | copy-start | bytes 688132
  193.2 4.1 %copy-start.24 = (bf16[64,1792]{1,0:T(8,128)(2,1)}, bf16[64,1792]{1,0:T(8,128)(2,1)S(1)}, u32[]{:S(2)}) copy-start(bf16[64,1792]{1,0:T(8,128)(2,1)S(1)} %collective-permute-done.30.refs_11_) | copy-start | bytes 688132
  193.2 4.1 %copy-start.27 = (bf16[64,1792]{1,0:T(8,128)(2,1)}, bf16[64,1792]{1,0:T(8,128)(2,1)S(1)}, u32[]{:S(2)}) copy-start(bf16[64,1792]{1,0:T(8,128)(2,1)S(1)} %collective-permute-done.27.refs_7_) | copy-start | bytes 688132
  (18 other events, 24.4 us)
